TPU v7x, 512 devices: a whole 4x4x16 slice. The times are simulated.
512 devices in a mesh: region: 8 (over z_hi, x), blk: 64 (over z_lo, y, core).
Axes of the slice: x: 4, y: 4, z: 16 (z_hi: 2, z_lo: 8; z = z_hi * 8 + z_lo), core: 2. Of those that a mesh axis runs over, the one named last changes fastest.
Arguments:
- archive: bfloat16 [65536, 6, 1024], P(('region', 'blk')), may hold values from -6 to 6
- unit_of: int32 [65536], P(('region', 'blk')), may hold values from 0 to 4095, as said below
- row_counts: int32 [512], P(('region', 'blk')), may hold values from 0 to 128, as said below
Outputs:
- cycle_stack: bfloat16 [1024, 4, 2, 9, 2048], P(('region', 'blk'))
- region_stack: bfloat16 [1024, 2, 9, 2048], P(('region', 'blk'))
Inputs may be any that keep to these rules, and one draw needn't show every extreme that they name: `unit_of`: the first row_counts slots of each archive shard are live; over the live slots of a region's 64 shards every unit 0 .. 4095 appears exactly once. A shard holds at most 2 live units of one owner block (unit // 64), and some shard holds exactly 2 of some owner. Slots past the count hold arbitrary unit numbers. `row_counts`: the counts of one region's shards sum to 4096; in every region some shard has 128 live slots and some has none.
All inputs are finite; a program needn't handle non-finite values.
Results may differ from a plain program's by a relative error of at most 0.0068.
Values may be sent and summed in bfloat16 or wider, within the bound.
No kernel may reach another device: no remote copies, remote signals or barrier semaphores. Data moves between devices by JAX's collectives and lax.ppermute only.
A program may use at most 64 MiB of HBM per device.

v0:
```python
import math

import jax
import jax.numpy as jnp
from jax import lax
from jax.sharding import PartitionSpec as P

SB = 2
SEGS = 32
F = 1024
LAGS = 2048
HALF = 24
STEPS = 4
UNITS = 64
CAP = 128


epsilon = 1e-05


def shifted(shard, axis, by):
    size = lax.axis_size(axis)
    return lax.ppermute(shard, axis, [(i, (i + by) % size) for i in range(size)])


def make_table():
    bin_index = jnp.arange(F, dtype=jnp.int32)
    lag_index = jnp.arange(LAGS, dtype=jnp.int32) - LAGS // 2
    phase = bin_index[:, None] * lag_index[None, :] % (2 * F)
    angle = phase.astype(jnp.float32) * (math.pi / F)
    return jnp.concatenate([jnp.cos(angle), -jnp.sin(angle)], axis=0).astype(jnp.bfloat16)


def whiten(placed):
    spectra = placed.astype(jnp.float32).reshape(UNITS, 3, 2, F)
    magnitude = jnp.mean(
        jnp.sqrt(spectra[:, :, 0] * spectra[:, :, 0] + spectra[:, :, 1] * spectra[:, :, 1]), axis=1
    )
    padded = jnp.pad(magnitude, ((0, 0), (HALF, HALF)))
    window_sum = padded[:, 0:F]
    for offset in range(1, 2 * HALF + 1):
        window_sum = window_sum + padded[:, offset : offset + F]
    bin_index = jnp.arange(F, dtype=jnp.int32)
    bin_count = (
        jnp.minimum(bin_index + HALF, F - 1) - jnp.maximum(bin_index - HALF, 0) + 1
    ).astype(jnp.float32)
    level_mean = window_sum / bin_count + epsilon
    return (spectra / level_mean[:, None, None, :]).reshape(UNITS, 6, F).astype(jnp.bfloat16)


def cross_lags(mine_block, other_block, lag_table):
    mine_parts = mine_block.reshape(SB, SEGS, 3, 2, F)
    other_parts = other_block.reshape(SB, SEGS, 3, 2, F)
    mine_real = mine_parts[:, None, :, :, None, 0, :].astype(jnp.float32)
    mine_imag = mine_parts[:, None, :, :, None, 1, :].astype(jnp.float32)
    other_real = other_parts[None, :, :, None, :, 0, :].astype(jnp.float32)
    other_imag = other_parts[None, :, :, None, :, 1, :].astype(jnp.float32)
    real_part = jnp.sum(mine_real * other_real + mine_imag * other_imag, axis=2)
    imag_part = jnp.sum(mine_imag * other_real - mine_real * other_imag, axis=2)
    stacked = (
        jnp.concatenate([real_part, imag_part], axis=-1)
        .astype(jnp.bfloat16)
        .reshape(SB * SB * 9, 2 * F)
    )
    series = jnp.dot(stacked, lag_table, preferred_element_type=jnp.float32) * (
        1.0 / math.sqrt(F * SEGS)
    )
    return series.astype(jnp.bfloat16).reshape(SB, SB, 9, LAGS)


def body(archive, unit_of, row_counts):
    blocks = lax.axis_size("blk")
    per_pair = 2 * UNITS // blocks
    slot_index = jnp.arange(CAP, dtype=jnp.int32)
    live_slot = slot_index < row_counts[0]
    owners = unit_of // UNITS
    local_unit = unit_of % UNITS
    earlier = slot_index[:, None] < slot_index[None, :]
    same_owner = (
        (owners[:, None] == owners[None, :]) & live_slot[:, None] & live_slot[None, :] & earlier
    )
    slot_rank = jnp.sum(same_owner.astype(jnp.int32), axis=0)
    target = jnp.where(live_slot, owners * per_pair + slot_rank, -1)
    positions = jnp.arange(blocks * per_pair, dtype=jnp.int32)
    chosen = target[None, :] == positions[:, None]
    filled = jnp.any(chosen, axis=1)
    source = jnp.sum(chosen.astype(jnp.int32) * slot_index[None, :], axis=1)
    send_rows = jnp.where(
        filled[:, None, None], jnp.take(archive, source, axis=0), jnp.zeros((), jnp.bfloat16)
    )
    send_ids = jnp.where(filled, jnp.take(local_unit, source, axis=0), -1).astype(jnp.bfloat16)
    got_rows, got_ids = (
        lax.all_to_all(
            send_rows.reshape(blocks, per_pair, 6, F),
            "blk",
            split_axis=0,
            concat_axis=0,
            tiled=True,
        ),
        lax.all_to_all(
            send_ids.reshape(blocks, per_pair), "blk", split_axis=0, concat_axis=0, tiled=True
        ),
    )
    got_rows = got_rows.reshape(blocks * per_pair, 6, F)
    got_units = got_ids.reshape(-1).astype(jnp.int32)
    unit_index = jnp.arange(UNITS, dtype=jnp.int32)
    matches = got_units[None, :] == unit_index[:, None]
    where_from = jnp.sum(matches.astype(jnp.int32) * positions[None, :], axis=1)
    whitened = whiten(jnp.take(got_rows, where_from, axis=0))
    lag_table = make_table()
    previous = shifted(whitened, "region", 1)
    region_stack = cross_lags(whitened, previous, lag_table)
    results = []
    current = whitened
    for offset in range(STEPS):
        current = shifted(current, "blk", 1)
        results.append(cross_lags(whitened, current, lag_table))
    cycle_stack = jnp.stack(results, axis=1)
    return (cycle_stack, region_stack)


def solution(mesh):
    placed = (P(("region", "blk"), None, None), P(("region", "blk")), P(("region", "blk")))
    return jax.shard_map(
        body,
        mesh=mesh,
        in_specs=placed,
        out_specs=(
            P(("region", "blk"), None, None, None, None),
            P(("region", "blk"), None, None, None),
        ),
        check_vma=False,
    )
```

profile of v0, /device:TPU:6, one launch (start us, length us, event | category | flops | bytes accessed | tf_op | source)
XLA Modules:
  0.0 302.3 jit_solution(5612043078394445156)
XLA Ops:
  5.2 16.2 %all-to-all-start = ((bf16[64,1,2]{2,1,0:T(2,128)(2,1)}), bf16[64,1,2]{2,1,0:T(2,128)(2,1)S(1)}, u32[]{:S(2)}, u32[]{:S(2)}) async-start(bf16[64,1,2]{2,1,0:T(2,128)(2,1)} %copy.118), calls=%async_computation | async-start | bytes 65536 | tf_op jit(solution)/shard_map/all_to_all | solution.py:100
  21.6 5.2 %gather_fusion.1 = bf16[128,6,1024]{2,0,1:T(8,128)(2,1)S(1)} fusion(bf16[128,6,1024]{2,0,1:T(8,128)(2,1)S(1)} %copy-done, s32[1024]{0:T(1024)S(1)} %pad_clamp_fusion.1), kind=kCustom, calls=%fused_computation.1 | custom fusion | bytes 3146240 | tf_op jit(solution)/shard_map/jit(_take)/gather | solution.py:89
  26.8 2.0 gather.23
  28.9 4.4 %broadcast_select_fusion.1 = bf16[64,2,6,1024]{3,1,2,0:T(2,128)(2,1)} fusion(pred[64,2]{1,0:T(8,128)(4,1)S(1)} %broadcast_in_dim.73, pred[64,2]{1,0:T(8,128)(4,1)S(1)} %compare_and_fusion, bf16[64,2,6,1024]{3,1,0,2:T(2,128)(2,1)} %gather.23), kind=kLoop, calls=%fused_computation.26 | loop fusion | flops 1572864 | bytes 3145984 | tf_op jit(solution)/shard_map/jit(_where)/select_n | solution.py:88
  33.7 12.8 %all-to-all-start.1 = ((bf16[64,2,6,1024]{3,1,2,0:T(2,128)(2,1)}), bf16[64,2,6,1024]{3,1,2,0:T(2,128)(2,1)S(1)}, u32[]{:S(2)}, u32[]{:S(2)}) async-start(bf16[64,2,6,1024]{3,1,2,0:T(2,128)(2,1)} %broadcast_select_fusion.1), calls=%async_computation.1 | async-start | bytes 3145728 | tf_op jit(solution)/shard_map/all_to_all | solution.py:93
  46.6 35.0 %cosine_convert_fusion = (bf16[1024,2048]{1,0:T(8,128)(2,1)}, bf16[1024,2048]{1,0:T(8,128)(2,1)}) fusion(s32[2048]{0:T(1024)S(1)} %iota_add_fusion), kind=kLoop, calls=%fused_computation.11 | loop fusion | flops 35651584 | bytes 8396800 | tf_op jit(solution)/shard_map/convert.29
  82.1 38.2 %all-to-all-done.1 = bf16[64,2,6,1024]{3,1,2,0:T(2,128)(2,1)S(1)} async-done(((bf16[64,2,6,1024]{3,1,2,0:T(2,128)(2,1)}), bf16[64,2,6,1024]{3,1,2,0:T(2,128)(2,1)S(1)}, u32[]{:S(2)}, u32[]{:S(2)}) %all-to-all-start.1) | async-done | bytes 1572896 | tf_op jit(solution)/shard_map/all_to_all | solution.py:93
  120.2 1.9 copy.120
  122.2 2.2 gather_fusion.2
  125.3 3.3 %divide_add_fusion = f32[64,1024]{1,0:T(8,128)S(1)} fusion(f32[64,1024]{1,0:T(8,128)S(1)} %broadcast_multiply_fusion, f32[1024]{0:T(1024)S(1)} %fusion.64), kind=kLoop, calls=%fused_computation.70 | loop fusion | flops 3276800 | bytes 528384 | tf_op jit(solution)/shard_map/add | solution.py:47
  129.2 1.9 collective-permute-start
  131.1 8.1 %collective-permute-start.4 = (bf16[64,6,1024]{2,0,1:T(8,128)(2,1)S(1)}, bf16[64,6,1024]{2,0,1:T(8,128)(2,1)S(1)}, u32[]{:S(2)}, u32[]{:S(2)}) collective-permute-start(bf16[64,6,1024]{2,0,1:T(8,128)(2,1)S(1)} %divide_convert_fusion), channel_id=1, source_target_pairs={{0,64},{64,128},{128,192},{192,256},{256,320},{320,384},{384,448},... | collective-permute-start | bytes 2359304 | tf_op jit(solution)/shard_map/ppermute | solution.py:23
  139.7 20.5 %collective-permute-done = bf16[64,6,1024]{2,0,1:T(8,128)(2,1)S(1)} collective-permute-done((bf16[64,6,1024]{2,0,1:T(8,128)(2,1)S(1)}, bf16[64,6,1024]{2,0,1:T(8,128)(2,1)S(1)}, u32[]{:S(2)}, u32[]{:S(2)}) %collective-permute-start) | collective-permute-done | bytes 786464 | tf_op jit(solution)/shard_map/ppermute | solution.py:23
  162.6 21.8 %collective-permute-done.1 = bf16[64,6,1024]{2,0,1:T(8,128)(2,1)S(1)} collective-permute-done((bf16[64,6,1024]{2,0,1:T(8,128)(2,1)S(1)}, bf16[64,6,1024]{2,0,1:T(8,128)(2,1)S(1)}, u32[]{:S(2)}, u32[]{:S(2)}) %collective-permute-start.1) | collective-permute-done | bytes 786464 | tf_op jit(solution)/shard_map/ppermute | solution.py:23
  186.3 5.4 %collective-permute-done.4 = bf16[64,6,1024]{2,0,1:T(8,128)(2,1)S(1)} collective-permute-done((bf16[64,6,1024]{2,0,1:T(8,128)(2,1)S(1)}, bf16[64,6,1024]{2,0,1:T(8,128)(2,1)S(1)}, u32[]{:S(2)}, u32[]{:S(2)}) %collective-permute-start.4) | collective-permute-done | bytes 786464 | tf_op jit(solution)/shard_map/ppermute | solution.py:23
  192.1 47.4 %collective-permute-done.2 = bf16[64,6,1024]{2,0,1:T(8,128)(2,1)S(1)} collective-permute-done((bf16[64,6,1024]{2,0,1:T(8,128)(2,1)S(1)}, bf16[64,6,1024]{2,0,1:T(8,128)(2,1)S(1)}, u32[]{:S(2)}, u32[]{:S(2)}) %collective-permute-start.2) | collective-permute-done | bytes 786464 | tf_op jit(solution)/shard_map/ppermute | solution.py:23
  239.6 2.1 collective-permute-start.3
  242.1 19.5 %collective-permute-done.3 = bf16[64,6,1024]{2,0,1:T(8,128)(2,1)S(1)} collective-permute-done((bf16[64,6,1024]{2,0,1:T(8,128)(2,1)S(1)}, bf16[64,6,1024]{2,0,1:T(8,128)(2,1)S(1)}, u32[]{:S(2)}, u32[]{:S(2)}) %collective-permute-start.3) | collective-permute-done | bytes 786464 | tf_op jit(solution)/shard_map/ppermute | solution.py:23
  261.9 11.7 %add_reduce_fusion = (bf16[2,2,3,3,1024]{4,3,2,1,0:T(4,128)(2,1)S(1)}, bf16[2,2,3,3,1024]{4,3,2,1,0:T(4,128)(2,1)S(1)}, bf16[2,2,3,3,1024]{4,3,2,1,0:T(4,128)(2,...) fusion(f32[2,32,3,1024]{3,1,2,0:T(8,128)S(1)} %get-tuple-elemen, ...), kind=kLoop, calls=%fused_computation.16 | loop fusion | flops 46817280 | bytes 10174464 | tf_op jit(solution)/shard_map/reduce_sum | solution.py:58
  273.8 5.0 %fusion.10 = bf16[36,2048]{1,0:T(8,128)(2,1)S(1)} fusion(bf16[36,1024]{1,0:T(8,128)(2,1)S(1)} %concatenate.63, bf16[36,1024]{1,0:T(8,128)(2,1)S(1)} %concatenate.62, bf16[1024,2048]{1,0:T(8,128)(2,1)} %get-tuple-element.45, bf16[1024,2048]{1,0:T(8,128)(2,1)} %get-tuple-element.44), kind=kOutput, calls=%fused_computation.36 | convolution fusion | flops 319209472 | bytes 8683520 | tf_op jit(solution)/shard_map/dot_general | solution.py:65
  279.8 5.0 %fusion.6 = bf16[36,2048]{1,0:T(8,128)(2,1)S(1)} fusion(bf16[36,1024]{1,0:T(8,128)(2,1)S(1)} %concatenate.50, bf16[36,1024]{1,0:T(8,128)(2,1)S(1)} %concatenate.49, bf16[1024,2048]{1,0:T(8,128)(2,1)} %get-tuple-element.45, bf16[1024,2048]{1,0:T(8,128)(2,1)} %get-tuple-element.44), kind=kOutput, calls=%fused_computation.32 | convolution fusion | flops 319209472 | bytes 8683520 | tf_op jit(solution)/shard_map/dot_general | solution.py:65
  285.1 5.0 %fusion.7 = bf16[36,2048]{1,0:T(8,128)(2,1)S(1)} fusion(bf16[36,1024]{1,0:T(8,128)(2,1)S(1)} %concatenate.54, bf16[36,1024]{1,0:T(8,128)(2,1)S(1)} %concatenate.53, bf16[1024,2048]{1,0:T(8,128)(2,1)} %get-tuple-element.45, bf16[1024,2048]{1,0:T(8,128)(2,1)} %get-tuple-element.44), kind=kOutput, calls=%fused_computation.33 | convolution fusion | flops 319209472 | bytes 8683520 | tf_op jit(solution)/shard_map/dot_general | solution.py:65
  290.3 5.0 %fusion.8 = bf16[36,2048]{1,0:T(8,128)(2,1)S(1)} fusion(bf16[36,1024]{1,0:T(8,128)(2,1)S(1)} %concatenate.57, bf16[36,1024]{1,0:T(8,128)(2,1)S(1)} %concatenate.56, bf16[1024,2048]{1,0:T(8,128)(2,1)} %get-tuple-element.45, bf16[1024,2048]{1,0:T(8,128)(2,1)} %get-tuple-element.44), kind=kOutput, calls=%fused_computation.34 | convolution fusion | flops 319209472 | bytes 8683520 | tf_op jit(solution)/shard_map/dot_general | solution.py:65
  295.5 5.0 %fusion.9 = bf16[36,2048]{1,0:T(8,128)(2,1)S(1)} fusion(bf16[36,1024]{1,0:T(8,128)(2,1)S(1)} %concatenate.60, bf16[36,1024]{1,0:T(8,128)(2,1)S(1)} %concatenate.59, bf16[1024,2048]{1,0:T(8,128)(2,1)} %get-tuple-element.45, bf16[1024,2048]{1,0:T(8,128)(2,1)} %get-tuple-element.44), kind=kOutput, calls=%fused_computation.35 | convolution fusion | flops 319209472 | bytes 8683520 | tf_op jit(solution)/shard_map/dot_general | solution.py:65
  (71 shorter events, 15.7 us)
Async XLA Ops:
  0.6 21.0 %copy-start = (bf16[128,6,1024]{2,0,1:T(8,128)(2,1)S(1)}, bf16[128,6,1024]{2,0,1:T(8,128)(2,1)}, u32[]{:S(2)}) copy-start(bf16[128,6,1024]{2,0,1:T(8,128)(2,1)} %param.3) | copy-start | bytes 4718596
  5.2 28.6 %all-to-all-start = ((bf16[64,1,2]{2,1,0:T(2,128)(2,1)}), bf16[64,1,2]{2,1,0:T(2,128)(2,1)S(1)}, u32[]{:S(2)}, u32[]{:S(2)}) async-start(bf16[64,1,2]{2,1,0:T(2,128)(2,1)} %copy.118), calls=%async_computation | async-start | bytes 65536 | tf_op jit(solution)/shard_map/all_to_all | solution.py:100
  33.7 86.5 %all-to-all-start.1 = ((bf16[64,2,6,1024]{3,1,2,0:T(2,128)(2,1)}), bf16[64,2,6,1024]{3,1,2,0:T(2,128)(2,1)S(1)}, u32[]{:S(2)}, u32[]{:S(2)}) async-start(bf16[64,2,6,1024]{3,1,2,0:T(2,128)(2,1)} %broadcast_select_fusion.1), calls=%async_computation.1 | async-start | bytes 3145728 | tf_op jit(solution)/shard_map/all_to_all | solution.py:93
  129.2 31.1 %collective-permute-start = (bf16[64,6,1024]{2,0,1:T(8,128)(2,1)S(1)}, bf16[64,6,1024]{2,0,1:T(8,128)(2,1)S(1)}, u32[]{:S(2)}, u32[]{:S(2)}) collective-permute-start(bf16[64,6,1024]{2,0,1:T(8,128)(2,1)S(1)} %divide_convert_fusion), channel_id=1, source_target_pairs={{0,1},{1,2},{2,3},{3,4},{4,5},{5,6},{6,7},{7,8},{8,9},{9,10},{10,1... | collective-permute-start | bytes 2359304 | tf_op jit(solution)/shard_map/ppermute | solution.py:23
  131.1 60.6 %collective-permute-start.4 = (bf16[64,6,1024]{2,0,1:T(8,128)(2,1)S(1)}, bf16[64,6,1024]{2,0,1:T(8,128)(2,1)S(1)}, u32[]{:S(2)}, u32[]{:S(2)}) collective-permute-start(bf16[64,6,1024]{2,0,1:T(8,128)(2,1)S(1)} %divide_convert_fusion), channel_id=1, source_target_pairs={{0,64},{64,128},{128,192},{192,256},{256,320},{320,384},{384,448},... | collective-permute-start | bytes 2359304 | tf_op jit(solution)/shard_map/ppermute | solution.py:23
  160.2 24.1 %collective-permute-start.1 = (bf16[64,6,1024]{2,0,1:T(8,128)(2,1)S(1)}, bf16[64,6,1024]{2,0,1:T(8,128)(2,1)S(1)}, u32[]{:S(2)}, u32[]{:S(2)}) collective-permute-start(bf16[64,6,1024]{2,0,1:T(8,128)(2,1)S(1)} %collective-permute-done), channel_id=1, source_target_pairs={{0,1},{1,2},{2,3},{3,4},{4,5},{5,6},{6,7},{7,8},{8,9},{9,10},{10,1... | collective-permute-start | bytes 2359304 | tf_op jit(solution)/shard_map/ppermute | solution.py:23
  184.4 55.2 %collective-permute-start.2 = (bf16[64,6,1024]{2,0,1:T(8,128)(2,1)S(1)}, bf16[64,6,1024]{2,0,1:T(8,128)(2,1)S(1)}, u32[]{:S(2)}, u32[]{:S(2)}) collective-permute-start(bf16[64,6,1024]{2,0,1:T(8,128)(2,1)S(1)} %collective-permute-done.1), channel_id=1, source_target_pairs={{0,1},{1,2},{2,3},{3,4},{4,5},{5,6},{6,7},{7,8},{8,9},{9,10},{10,1... | collective-permute-start | bytes 2359304 | tf_op jit(solution)/shard_map/ppermute | solution.py:23
  239.6 22.0 %collective-permute-start.3 = (bf16[64,6,1024]{2,0,1:T(8,128)(2,1)S(1)}, bf16[64,6,1024]{2,0,1:T(8,128)(2,1)S(1)}, u32[]{:S(2)}, u32[]{:S(2)}) collective-permute-start(bf16[64,6,1024]{2,0,1:T(8,128)(2,1)S(1)} %collective-permute-done.2), channel_id=1, source_target_pairs={{0,1},{1,2},{2,3},{3,4},{4,5},{5,6},{6,7},{7,8},{8,9},{9,10},{10,1... | collective-permute-start | bytes 2359304 | tf_op jit(solution)/shard_map/ppermute | solution.py:23
where the time goes:
time: 303 us; the launch traced here: 302 us
  waiting for transfers between devices  153 us (50%)
  other arithmetic  58.3 us (19%)
  starting transfers between devices  45 us (15%)
  matrix products  25.1 us (8%)
  local copies, waits for them, and re-layouts  18.8 us (6%)
    ppermute x5, waiting for transfers between devices, shifted(): lax.ppermute(shard, axis, [(i, (i + by) % size) for i in range(size)])  115 us
    all_to_all x1, waiting for transfers between devices, body(): lax.all_to_all(send_rows.reshape(blocks, per_pair, 6, F), 'blk', split_ax...  38.2 us
    another operation x1, other arithmetic  35 us
    dot_general x5, matrix products, cross_lags(): jnp.dot(stacked, lag_table, preferred_element_type=jnp.float32)  25.1 us
    all_to_all x1, starting transfers between devices, body(): lax.all_to_all(send_ids.reshape(blocks, per_pair), 'blk', split_axis=0, c...  16.2 us
    ppermute x5, starting transfers between devices, shifted(): lax.ppermute(shard, axis, [(i, (i + by) % size) for i in range(size)])  16 us
    all_to_all x1, starting transfers between devices, body(): lax.all_to_all(send_rows.reshape(blocks, per_pair, 6, F), 'blk', split_ax...  12.8 us
    reduce_sum x1, other arithmetic, cross_lags(): real_part = jnp.sum(mine_real * other_real + mine_imag * other_imag, axis=2)  11.7 us
  transfers between devices with their start and end apart: 7, of which 7 were waited for; matrix products, arithmetic and copies ran while one was open for 16% of the time, Pallas kernels for 0%

commit v1 on v0

v1 whole, which is shorter than its diff:
```python
import functools
import math

import jax
import jax.numpy as jnp
from jax import lax
from jax.experimental import pallas as pl
from jax.experimental.pallas import tpu as pltpu
from jax.sharding import PartitionSpec as P

SB = 2
SEGS = 32
F = 1024
LAGS = 2048
HALF = 24
STEPS = 4
UNITS = 64
CAP = 128
LANES = 128
FH = F // LANES
TILE = 2 * FH
epsilon = 1e-05

CHUNKS = ((0, 1, 2),)
GROUP = 32
VMEM = pl.BlockSpec(memory_space=pltpu.VMEM)
SMEM = pl.BlockSpec(memory_space=pltpu.SMEM)


def pairs_of(chunk):
    before = [c for part in CHUNKS[:chunk] for c in part]
    now = before + list(CHUNKS[chunk])
    return [(c, d) for c in now for d in now if not (c in before and d in before)]


def place_of(component):
    for chunk, part in enumerate(CHUNKS):
        if component in part:
            return chunk, part.index(component)


def whiten_kernel(source_ref, band_ref, inverse_ref, archive_ref, *rest):
    outs, (level_ref,) = rest[:-1], rest[-1:]
    base = pl.program_id(0) * GROUP
    rows = GROUP * FH

    def slab_of(position):
        return archive_ref[source_ref[base + position]].astype(jnp.float32)

    def magnitude(position, carry):
        slab = slab_of(position)
        total = None
        for c in range(3):
            real = slab[c * TILE : c * TILE + FH]
            imag = slab[c * TILE + FH : (c + 1) * TILE]
            size = jnp.sqrt(real * real + imag * imag)
            total = size if total is None else total + size
        level_ref[pl.ds(pl.multiple_of(FH + position * FH, FH), FH), :] = total * (1.0 / 3.0)
        return carry

    lax.fori_loop(0, GROUP, magnitude, 0, unroll=4)
    here = level_ref[FH : FH + rows, :]
    before = level_ref[FH - 1 : FH - 1 + rows, :]
    after = level_ref[FH + 1 : FH + 1 + rows, :]
    lane = lax.broadcasted_iota(jnp.int32, (rows, LANES), 1)
    row = lax.broadcasted_iota(jnp.int32, (rows, LANES), 0) % FH
    edge = jnp.where(
        lane >= LANES // 2,
        jnp.where(row == 0, 0.0, before),
        jnp.where(row == FH - 1, 0.0, after),
    )
    spread = jnp.concatenate([here, edge], axis=1)
    high = spread.astype(jnp.bfloat16)
    low = (spread - high.astype(jnp.float32)).astype(jnp.bfloat16)
    band = band_ref[...]
    window = jnp.dot(high, band, preferred_element_type=jnp.float32) + jnp.dot(
        low, band, preferred_element_type=jnp.float32
    )
    level = window.reshape(GROUP, FH, LANES) * inverse_ref[...][None] + epsilon
    level_ref[FH : FH + rows, :] = (1.0 / level).reshape(rows, LANES)

    def divide(position, carry):
        slab = slab_of(position)
        gain = level_ref[pl.ds(pl.multiple_of(FH + position * FH, FH), FH), :]
        for out, part in zip(outs, CHUNKS):
            pieces = []
            for c in part:
                for half in range(2):
                    start = c * TILE + half * FH
                    pieces.append(slab[start : start + FH] * gain)
            out[position] = jnp.concatenate(pieces, axis=0).astype(jnp.bfloat16)
        return carry

    lax.fori_loop(0, GROUP, divide, 0, unroll=4)


def whiten(source, archive):
    low = jnp.arange(LANES, dtype=jnp.int32)
    gap = jnp.abs(low[:, None] - low[None, :])
    band = jnp.concatenate([gap <= HALF, gap >= LANES - HALF], axis=0).astype(jnp.bfloat16)
    bin_index = jnp.arange(F, dtype=jnp.int32)
    bin_count = (
        jnp.minimum(bin_index + HALF, F - 1) - jnp.maximum(bin_index - HALF, 0) + 1
    ).astype(jnp.float32)
    inverse = (1.0 / bin_count).reshape(FH, LANES)
    sizes = [len(part) * TILE for part in CHUNKS]
    return pl.pallas_call(
        whiten_kernel,
        grid=(CAP // GROUP,),
        in_specs=[SMEM, VMEM, VMEM, VMEM],
        out_specs=[pl.BlockSpec((GROUP, size, LANES), lambda g: (g, 0, 0)) for size in sizes],
        out_shape=[jax.ShapeDtypeStruct((CAP, size, LANES), jnp.bfloat16) for size in sizes],
        scratch_shapes=[pltpu.VMEM((GROUP * FH + 2 * FH, LANES), jnp.float32)],
        compiler_params=pltpu.CompilerParams(vmem_limit_bytes=16 * 1024 * 1024),
        cost_estimate=pl.CostEstimate(flops=200_000_000, bytes_accessed=4_000_000, transcendentals=0),
        name="whiten",
    )(source, band, inverse, archive)


def sort_kernel(source_ref, got_ref, out_ref):
    def move(unit, carry):
        out_ref[unit] = got_ref[source_ref[unit]]
        return carry

    lax.fori_loop(0, UNITS, move, 0, unroll=8)


def sort_units(source, got):
    return pl.pallas_call(
        sort_kernel,
        in_specs=[SMEM, VMEM],
        out_specs=VMEM,
        out_shape=jax.ShapeDtypeStruct((UNITS,) + got.shape[1:], jnp.bfloat16),
        compiler_params=pltpu.CompilerParams(vmem_limit_bytes=16 * 1024 * 1024),
        cost_estimate=pl.CostEstimate(flops=0, bytes_accessed=3_000_000, transcendentals=0),
        name="sort_units",
    )(source, got)


def products(mine, other, chunk, store):
    pairs = pairs_of(chunk)

    def load(refs, unit, component):
        which, at = place_of(component)
        tile = refs[which][unit, at * TILE : (at + 1) * TILE, :].astype(jnp.float32)
        return tile[:FH], tile[FH:]

    firsts = sorted({c for c, _ in pairs})
    seconds = sorted({d for _, d in pairs})
    for i in range(SB):
        for j in range(SB):

            def step(m, sums):
                left = {c: load(mine, i * SEGS + m, c) for c in firsts}
                right = {d: load(other, j * SEGS + m, d) for d in seconds}
                new = []
                for n, (c, d) in enumerate(pairs):
                    real, imag = sums[n]
                    (ar, ai), (br, bi) = left[c], right[d]
                    new.append((real + ar * br + ai * bi, imag + ai * br - ar * bi))
                return tuple(new)

            zero = jnp.zeros((FH, LANES), jnp.float32)
            sums = lax.fori_loop(
                0, SEGS, step, tuple((zero, zero) for _ in pairs), unroll=2
            )
            for n, (real, imag) in enumerate(sums):
                store(i, j, n, jnp.concatenate([real, imag], axis=0).astype(jnp.bfloat16))


def cross_kernel(chunk, plan, flag_ref, *refs):
    depth = chunk + 1
    blocks = [refs[n : n + depth] for n in range(0, len(refs) - len(plan), depth)]
    outs = refs[len(refs) - len(plan) :]
    for out, (left, when_zero, when_one) in zip(outs, plan):

        def store(i, j, n, tile, out=out):
            out[i * SB + j, n] = tile

        if when_zero == when_one:
            products(blocks[left], blocks[when_zero], chunk, store)
        else:
            for value, right in ((0, when_zero), (1, when_one)):

                @pl.when(flag_ref[0] == value)
                def _(right=right, left=left, store=store):
                    products(blocks[left], blocks[right], chunk, store)


def cross(chunk, plan, flag, *blocks):
    count = len(pairs_of(chunk))
    shape = (SB * SB, count, TILE, LANES)
    flat = [part for block in blocks for part in block[: chunk + 1]]
    return pl.pallas_call(
        functools.partial(cross_kernel, chunk, plan),
        in_specs=[SMEM] + [VMEM] * len(flat),
        out_specs=[VMEM] * len(plan),
        out_shape=[jax.ShapeDtypeStruct(shape, jnp.bfloat16)] * len(plan),
        compiler_params=pltpu.CompilerParams(vmem_limit_bytes=24 * 1024 * 1024),
        cost_estimate=pl.CostEstimate(
            flops=len(plan) * 40_000_000, bytes_accessed=len(plan) * 1_500_000, transcendentals=0
        ),
        name="cross",
    )(flag.reshape(1), *flat)


COLUMNS = 256
CYCLE_ROWS = SB * STEPS * 9 * SB
ALL_ROWS = CYCLE_ROWS + SB * 9 * SB


def series_kernel(table_ref, *refs):
    chunks = len(CHUNKS)
    sources = refs[: (STEPS + 1) * chunks]
    cycle_ref, region_ref, wide_ref, rows_ref = refs[(STEPS + 1) * chunks :]

    @pl.when(pl.program_id(0) == 0)
    def _():
        for k in range(STEPS + 1):
            for chunk in range(chunks):
                source = sources[k * chunks + chunk]
                for i in range(SB):
                    for j in range(SB):
                        for n, (c, d) in enumerate(pairs_of(chunk)):
                            if k < STEPS:
                                row = ((i * STEPS + k) * 9 + 3 * c + d) * SB + j
                            else:
                                row = CYCLE_ROWS + (i * 9 + 3 * c + d) * SB + j
                            wide_ref[row * TILE : (row + 1) * TILE, :] = source[
                                i * SB + j, n
                            ].astype(jnp.float32)
        for piece in range(TILE):
            rows_ref[:, piece * LANES : (piece + 1) * LANES] = wide_ref[
                pl.ds(piece, ALL_ROWS, stride=TILE), :
            ].astype(jnp.bfloat16)

    series = jnp.dot(rows_ref[...], table_ref[...], preferred_element_type=jnp.float32)
    series = (series * (1.0 / math.sqrt(F * SEGS))).astype(jnp.bfloat16)
    for i in range(SB):
        for k in range(STEPS):
            for n in range(9):
                row = ((i * STEPS + k) * 9 + n) * SB
                cycle_ref[i, k, n] = series[row : row + SB]
        for n in range(9):
            row = CYCLE_ROWS + (i * 9 + n) * SB
            region_ref[i, n] = series[row : row + SB]


def lag_series(table, sources):
    return pl.pallas_call(
        series_kernel,
        grid=(LAGS // COLUMNS,),
        in_specs=[pl.BlockSpec((2 * F, COLUMNS), lambda n: (0, n))] + [VMEM] * len(sources),
        out_specs=[
            pl.BlockSpec((SB, STEPS, 9, SB, COLUMNS), lambda n: (0, 0, 0, 0, n)),
            pl.BlockSpec((SB, 9, SB, COLUMNS), lambda n: (0, 0, 0, n)),
        ],
        out_shape=[
            jax.ShapeDtypeStruct((SB, STEPS, 9, SB, LAGS), jnp.bfloat16),
            jax.ShapeDtypeStruct((SB, 9, SB, LAGS), jnp.bfloat16),
        ],
        scratch_shapes=[
            pltpu.VMEM((ALL_ROWS * TILE, LANES), jnp.float32),
            pltpu.VMEM((ALL_ROWS, 2 * F), jnp.bfloat16),
        ],
        compiler_params=pltpu.CompilerParams(vmem_limit_bytes=32 * 1024 * 1024),
        cost_estimate=pl.CostEstimate(
            flops=2 * ALL_ROWS * 2 * F * LAGS, bytes_accessed=12_000_000, transcendentals=0
        ),
        name="lag_series",
    )(table, *sources)


def table_kernel(fine_ref, coarse_ref, out_ref):
    step = pl.program_id(0)
    for high in range(FH):
        cos_high = coarse_ref[0, high : high + 1, :]
        sin_high = coarse_ref[1, high : high + 1, :]
        cos_low, sin_low = fine_ref[0], fine_ref[1]

        @pl.when(step == 0)
        def _(high=high):
            out_ref[high * LANES : (high + 1) * LANES, :] = (
                cos_low * cos_high - sin_low * sin_high
            ).astype(jnp.bfloat16)

        @pl.when(step == 1)
        def _(high=high):
            out_ref[high * LANES : (high + 1) * LANES, :] = (
                -(sin_low * cos_high + cos_low * sin_high)
            ).astype(jnp.bfloat16)


def make_table():
    lag_index = jnp.arange(LAGS, dtype=jnp.int32) - LAGS // 2

    def angles(bins):
        phase = bins[:, None] * lag_index[None, :] % (2 * F)
        angle = phase.astype(jnp.float32) * (math.pi / F)
        return jnp.stack([jnp.cos(angle), jnp.sin(angle)])

    fine = angles(jnp.arange(LANES, dtype=jnp.int32))
    coarse = angles(LANES * jnp.arange(FH, dtype=jnp.int32))
    width = 512
    return pl.pallas_call(
        table_kernel,
        grid=(2, LAGS // width),
        in_specs=[
            pl.BlockSpec((2, LANES, width), lambda s, n: (0, 0, n)),
            pl.BlockSpec((2, FH, width), lambda s, n: (0, 0, n)),
        ],
        out_specs=pl.BlockSpec((F, width), lambda s, n: (s, n)),
        out_shape=jax.ShapeDtypeStruct((2 * F, LAGS), jnp.bfloat16),
        compiler_params=pltpu.CompilerParams(vmem_limit_bytes=16 * 1024 * 1024),
        cost_estimate=pl.CostEstimate(flops=16_000_000, bytes_accessed=12_000_000, transcendentals=0),
        name="lag_table",
    )(fine, coarse)


def shifted(block, axis, by):
    size = lax.axis_size(axis)
    return lax.ppermute(block, axis, [(i, (i + by) % size) for i in range(size)])


def swapped(block):
    return lax.ppermute(block, "blk", [(i, i ^ 1) for i in range(lax.axis_size("blk"))])


def from_previous_region(block, planes, crossing):
    regions = lax.axis_size("region")
    groups = [list(range(n, n + planes)) for n in range(0, regions, planes)]
    near = lax.ppermute(
        block, "region", [(i, i + 1) for i in range(regions) if (i + 1) % planes]
    )
    rows = block.shape[0] // planes
    parts = lax.all_to_all(
        block, "region", split_axis=0, concat_axis=0, tiled=True, axis_index_groups=groups
    )
    part = lax.ppermute(
        parts[(planes - 1) * rows :],
        "region",
        [(i, (i + planes) % regions) for i in range(regions)],
    )
    far = lax.all_gather(part, "region", axis=0, tiled=True, axis_index_groups=groups)
    return near, far


def body(archive, unit_of, row_counts):
    blocks = lax.axis_size("blk")
    slot = jnp.arange(CAP, dtype=jnp.int32)
    ids = jnp.where(slot < row_counts[0], unit_of, -1)
    ids_all = lax.all_gather(ids, "blk")

    owners = jnp.arange(blocks, dtype=jnp.int32)
    sent = (ids >> 6)[None, :] == owners[:, None]
    first = jnp.min(jnp.where(sent, slot, CAP - 1), axis=1)
    last = jnp.max(jnp.where(sent, slot, 0), axis=1)
    source = jnp.stack([first, last], axis=1).reshape(2 * blocks)
    send = whiten(source, archive.reshape(CAP, 3 * TILE, LANES))

    got = []
    for part in send:
        rows = part.shape[1]
        moved = lax.all_to_all(
            part.reshape(blocks, 2 * rows, LANES), "blk", split_axis=0, concat_axis=0, tiled=True
        )
        got.append(moved.reshape(2 * blocks, rows, LANES))

    table = make_table()
    index = lax.axis_index("blk")
    mine = (ids_all >> 6) == index
    key = slot[None, :] * UNITS + (ids_all & (UNITS - 1))
    none = CAP * UNITS
    low = jnp.min(jnp.where(mine, key, none), axis=1)
    high = jnp.max(jnp.where(mine, key, -1), axis=1)
    units = jnp.arange(UNITS, dtype=jnp.int32)[:, None]
    in_first = (low < none)[None, :] & ((low & (UNITS - 1))[None, :] == units)
    in_second = (high > low)[None, :] & ((high & (UNITS - 1))[None, :] == units)
    place = jnp.sum(
        jnp.where(in_first, 2 * owners[None, :], 0)
        + jnp.where(in_second, 2 * owners[None, :] + 1, 0),
        axis=1,
    )
    place = jnp.clip(place, 0, 2 * blocks - 1)

    core = index & 1
    planes = 4
    edge = (lax.axis_index("region") % planes == 0).astype(jnp.int32)
    own, twin, two, four, near, far = [], [], [], [], [], []
    cycle = [[], [], [], []]
    region = []
    for chunk in range(len(CHUNKS)):
        block = sort_units(place, got[chunk])
        own.append(block)
        closer, further = from_previous_region(block, planes, edge)
        two.append(shifted(block, "blk", 2))
        twin.append(swapped(block))
        four.append(shifted(block, "blk", 4))
        near.append(closer)
        far.append(further)
        by_two, for_one = cross(
            chunk, ((0, 2, 2), (1, 0, 2)), core, own, twin, two
        )
        by_four, for_three = cross(
            chunk, ((0, 3, 3), (1, 2, 3)), core, own, twin, two, four
        )
        by_one, by_three = swapped(for_one), swapped(for_three)
        for k, result in enumerate((by_one, by_two, by_three, by_four)):
            cycle[k].append(result)
        region.extend(cross(chunk, ((0, 1, 2),), edge, own, near, far))

    sources = [result for k in range(STEPS) for result in cycle[k]] + region
    cycle_series, region_series = lag_series(table, sources)
    return jnp.swapaxes(cycle_series, 2, 3), jnp.swapaxes(region_series, 1, 2)


def solution(mesh):
    placed = (P(("region", "blk"), None, None), P(("region", "blk")), P(("region", "blk")))
    return jax.shard_map(
        body,
        mesh=mesh,
        in_specs=placed,
        out_specs=(
            P(("region", "blk"), None, None, None, None),
            P(("region", "blk"), None, None, None),
        ),
        check_vma=False,
    )
```

time: 303 us -> 278 us (0.917)
  the two profiles are of different devices: /device:TPU:6 before, /device:TPU:2 now
where the time goes in v1:
time: 278 us; the launch traced here: 277 us
  blocking collectives  154 us (55%)
  starting transfers between devices  44.7 us (16%)
  waiting for transfers between devices  34.2 us (12%)
  Pallas kernels  30.2 us (11%)
  other arithmetic  8.18 us (3%)
  local copies, waits for them, and re-layouts  4.11 us (1%)
    all_gather x1, blocking collectives, body(): ids_all = lax.all_gather(ids, 'blk')  140 us
    ppermute x2, waiting for transfers between devices, shifted(): lax.ppermute(block, axis, [(i, (i + by) % size) for i in range(size)])  34.2 us
    all_to_all x1, starting transfers between devices, body(): lax.all_to_all(part.reshape(blocks, 2 * rows, LANES), 'blk', split_axis=0...  16.2 us
    all_gather x1, blocking collectives, from_previous_region(): lax.all_gather(part, 'region', axis=0, tiled=True, axis_index_groups=groups)  14.1 us
    pallas_call x3, Pallas kernels, cross(): pl.pallas_call(functools.partial(cross_kernel, chunk, plan), in_specs=[SM...  13.2 us
    ppermute x1, starting transfers between devices, from_previous_region(): lax.ppermute(parts[(planes - 1) * rows:], 'region', [(i, (i + planes) % r...  8.22 us
    ppermute x3, starting transfers between devices, swapped(): lax.ppermute(block, 'blk', [(i, i ^ 1) for i in range(lax.axis_size('blk'...  6.25 us
    ppermute x2, starting transfers between devices, shifted(): lax.ppermute(block, axis, [(i, (i + by) % size) for i in range(size)])  5.9 us
  transfers between devices with their start and end apart: 9, of which 2 were waited for; matrix products, arithmetic and copies ran while one was open for 3% of the time, Pallas kernels for 7%

profile of v1, /device:TPU:2, one launch (start us, length us, event | category | flops | bytes accessed | tf_op | source)
XLA Modules:
  0.0 276.9 jit_solution(1515015383163065379)
XLA Ops:
  2.4 1.9 copy.19
  4.3 1.0 copy.20.archive_ref
  5.3 3.9 %whiten.1 = bf16[128,48,128]{2,1,0:T(8,128)(2,1)} custom-call(s32[128]{0:T(128)S(1)} %reshape.292.source_ref, bf16[256,128]{1,0:T(8,128)(2,1)S(1)} %add_convert_fusion.band_ref, f32[8,128]{1,0:T(8,128)S(1)} %convert_divide_fusion.inverse_ref, bf16[128,48,128]{2,1,0:T(8,128)(2,1)S(1)} %copy.20.archive_ref), custom_call_target="tpu_custom_call" | custom-call | flops 200000000 | bytes 4000000 | tf_op jit(solution)/shard_map/whiten/pallas_call | solution.py:107
  9.2 16.2 %all-to-all-start = ((bf16[64,96,128]{2,1,0:T(8,128)(2,1)}), bf16[64,96,128]{2,1,0:T(8,128)(2,1)S(1)}, u32[]{:S(2)}, u32[]{:S(2)}) async-start(bf16[64,96,128]{2,1,0:T(8,128)(2,1)} %bitcast.9), calls=%async_computation | async-start | bytes 3145728 | tf_op jit(solution)/shard_map/all_to_all | solution.py:364
  25.4 139.8 %all-gather.1 = s32[64,1,128]{2,1,0:T(1,128)S(1)} all-gather(s32[1,1,128]{2,1,0:T(1,128)S(1)} %get-tuple-element.23), channel_id=2, replica_groups=mesh['region'=8,'blk'=64] {'blk'}, dimensions={0}, use_global_device_ids=true | all-gather | bytes 33280 | tf_op jit(solution)/shard_map/all_gather | solution.py:352
  165.5 5.0 %fusion.7 = (f32[1,128,2048]{2,1,0:T(8,128)}, f32[1,128,2048]{2,1,0:T(8,128)}) fusion(s32[2048]{0:T(1024)S(1)} %iota_add_fusion), kind=kLoop, calls=%fused_computation.11 | loop fusion | flops 3670016 | bytes 2105344 | tf_op jit(solution)/shard_map/cos | solution.py:300
  170.5 1.5 sort_units.1.refs_0_
  172.1 4.8 %all-to-all-start.1 = ((bf16[64,48,128]{2,1,0:T(8,128)(2,1)}), bf16[64,48,128]{2,1,0:T(8,128)(2,1)}, u32[]{:S(2)}, u32[]{:S(2)}) async-start(bf16[64,48,128]{2,1,0:T(8,128)(2,1)} %sort_units.1.refs_0_), calls=%async_computation.1 | async-start | bytes 1572864 | tf_op jit(solution)/shard_map/all_to_all | solution.py:336
  176.9 1.9 collective-permute-start.3
  178.8 4.0 %collective-permute-start.1 = (bf16[64,48,128]{2,1,0:T(8,128)(2,1)}, bf16[64,48,128]{2,1,0:T(8,128)(2,1)S(1)}, u32[]{:S(2)}, u32[]{:S(2)}) collective-permute-start(bf16[64,48,128]{2,1,0:T(8,128)(2,1)} %sort_units.1.refs_0_), channel_id=1, source_target_pairs={{0,2},{1,3},{2,4},{3,5},{4,6},{5,7},{6,8},{7,9},{8,10},{9,11},{10,... | collective-permute-start | bytes 2359304 | tf_op jit(solution)/shard_map/ppermute | solution.py:322
  182.8 1.9 collective-permute-start
  185.1 3.4 %collective-permute-start.5 = (bf16[64,48,128]{2,1,0:T(8,128)(2,1)}, bf16[64,48,128]{2,1,0:T(8,128)(2,1)}, u32[]{:S(2)}, u32[]{:S(2)}) collective-permute-start(bf16[64,48,128]{2,1,0:T(8,128)(2,1)} %sort_units.1.refs_0_), channel_id=1, source_target_pairs={{0,64},{64,128},{128,192},{256,320},{320,384},{384,448},{1,65},{65... | collective-permute-start | bytes 2359304 | tf_op jit(solution)/shard_map/ppermute | solution.py:332
  188.5 1.7 pad_maximum_fusion.fine_ref
  191.1 8.2 %collective-permute-start.6 = (bf16[16,48,128]{2,1,0:T(8,128)(2,1)S(1)}, bf16[16,48,128]{2,1,0:T(8,128)(2,1)S(1)}, u32[]{:S(2)}, u32[]{:S(2)}) collective-permute-start(bf16[16,48,128]{2,1,0:T(8,128)(2,1)S(1)} %slice.4), channel_id=1, source_target_pairs={{0,256},{64,320},{128,384},{192,448},{256,0},{320,64},{384,128},{4... | collective-permute-start | bytes 589832 | tf_op jit(solution)/shard_map/ppermute | solution.py:339
  199.4 5.7 %lag_table.1.table_ref = bf16[2048,2048]{1,0:T(8,128)(2,1)S(1)} custom-call(f32[2,128,2048]{2,1,0:T(8,128)S(1)} %pad_maximum_fusion.fine_ref, f32[2,8,2048]{2,1,0:T(8,128)S(1)} %pad_maximum_fusion.1.coarse_ref), custom_call_target="tpu_custom_call" | custom-call | flops 16000000 | bytes 12000000 | tf_op jit(solution)/shard_map/lag_table/pallas_call | solution.py:305
  205.1 10.3 %collective-permute-done.3.refs_3_ = bf16[64,48,128]{2,1,0:T(8,128)(2,1)} collective-permute-done((bf16[64,48,128]{2,1,0:T(8,128)(2,1)}, bf16[64,48,128]{2,1,0:T(8,128)(2,1)}, u32[]{:S(2)}, u32[]{:S(2)}) %collective-permute-start.3) | collective-permute-done | bytes 786464 | tf_op jit(solution)/shard_map/ppermute | solution.py:322
  215.4 23.9 %collective-permute-done.1.refs_2_ = bf16[64,48,128]{2,1,0:T(8,128)(2,1)S(1)} collective-permute-done((bf16[64,48,128]{2,1,0:T(8,128)(2,1)}, bf16[64,48,128]{2,1,0:T(8,128)(2,1)S(1)}, u32[]{:S(2)}, u32[]{:S(2)}) %collective-permute-start.1) | collective-permute-done | bytes 786464 | tf_op jit(solution)/shard_map/ppermute | solution.py:322
  239.3 5.1 %cross.4 = (bf16[4,9,16,128]{3,2,1,0:T(8,128)(2,1)S(1)}, bf16[4,9,16,128]{3,2,1,0:T(8,128)(2,1)S(1)}) custom-call(s32[1]{0:T(128)} %bitcast.flag_ref, bf16[64,48,128]{2,1,0:T(8,128)(2,1)} %sort_units.1.refs_0_, bf16[64,48,128]{2,1,0:T(8,128)(2,1)} %collective-permute-done.refs_1_, bf16[64,48,128]{2,1,0:T(8,128)(2,1)S(1)} %collective-permute-done.1.refs_2_, ...), custom_call_target="tpu_custom_call" | custom-call | flops 80000000 | bytes 3000000 | tf_op jit(solution)/shard_map/cross/pallas_call | solution.py:194
  244.4 1.9 collective-permute-start.4
  246.4 4.9 %cross.3 = (bf16[4,9,16,128]{3,2,1,0:T(8,128)(2,1)S(1)}, bf16[4,9,16,128]{3,2,1,0:T(8,128)(2,1)S(1)}) custom-call(s32[1]{0:T(128)} %bitcast.flag_ref, bf16[64,48,128]{2,1,0:T(8,128)(2,1)} %sort_units.1.refs_0_, bf16[64,48,128]{2,1,0:T(8,128)(2,1)} %collective-permute-done.refs_1_, bf16[64,48,128]{2,1,0:T(8,128)(2,1)S(1)} %collective-permute-done.1.refs_2_), custom_call_target="tpu_custom_call" | custom-call | flops 80000000 | bytes 3000000 | tf_op jit(solution)/shard_map/cross/pallas_call | solution.py:194
  251.3 2.4 collective-permute-start.2
  253.7 14.1 %all_gather.11.refs_2_ = bf16[64,48,128]{2,1,0:T(8,128)(2,1)S(1)} all-gather(bf16[16,48,128]{2,1,0:T(8,128)(2,1)S(1)} %collective-permute-done.6), channel_id=1, replica_groups={{0,64,128,192},{256,320,384,448},{1,65,129,193},{257,321,385,449},{2,66..., dimensions={0}, use_global_device_ids=true | all-gather | bytes 983040 | tf_op jit(solution)/shard_map/all_gather | solution.py:344
  267.8 3.1 %cross.5.refs_4_ = bf16[4,9,16,128]{3,2,1,0:T(8,128)(2,1)S(1)} custom-call(s32[1]{0:T(128)} %bitcast.11.flag_ref, bf16[64,48,128]{2,1,0:T(8,128)(2,1)} %sort_units.1.refs_0_, bf16[64,48,128]{2,1,0:T(8,128)(2,1)} %collective-permute-done.5.refs_1_, bf16[64,48,128]{2,1,0:T(8,128)(2,1)S(1)} %all_gather.11.refs_2_), custom_call_target="tpu_custom_call" | custom-call | flops 40000000 | bytes 1500000 | tf_op jit(solution)/shard_map/cross/pallas_call | solution.py:194
  271.0 5.9 %lag_series.1 = (bf16[2,4,9,2,2048]{4,3,2,1,0:T(2,128)(2,1)}, bf16[2,9,2,2048]{3,2,1,0:T(2,128)(2,1)}) custom-call(bf16[2048,2048]{1,0:T(8,128)(2,1)S(1)} %lag_table.1.table_ref, bf16[4,9,16,128]{3,2,1,0:T(8,128)(2,1)S(1)} %collective-permute-done.2.refs_0_, bf16[4,9,16,128]{3,2,1,0:T(8,128)(2,1)S(1)} %get-tuple-element.9.refs_1_, ...), custom_call_target="tpu_custom_call" | custom-call | flops 1509949440 | bytes 12000000 | tf_op jit(solution)/shard_map/lag_series/pallas_call | solution.py:250
  (27 shorter events, 2.7 us)
Async XLA Ops:
  9.2 161.3 %all-to-all-start = ((bf16[64,96,128]{2,1,0:T(8,128)(2,1)}), bf16[64,96,128]{2,1,0:T(8,128)(2,1)S(1)}, u32[]{:S(2)}, u32[]{:S(2)}) async-start(bf16[64,96,128]{2,1,0:T(8,128)(2,1)} %bitcast.9), calls=%async_computation | async-start | bytes 3145728 | tf_op jit(solution)/shard_map/all_to_all | solution.py:364
  172.1 18.1 %all-to-all-start.1 = ((bf16[64,48,128]{2,1,0:T(8,128)(2,1)}), bf16[64,48,128]{2,1,0:T(8,128)(2,1)}, u32[]{:S(2)}, u32[]{:S(2)}) async-start(bf16[64,48,128]{2,1,0:T(8,128)(2,1)} %sort_units.1.refs_0_), calls=%async_computation.1 | async-start | bytes 1572864 | tf_op jit(solution)/shard_map/all_to_all | solution.py:336
  176.9 38.5 %collective-permute-start.3 = (bf16[64,48,128]{2,1,0:T(8,128)(2,1)}, bf16[64,48,128]{2,1,0:T(8,128)(2,1)}, u32[]{:S(2)}, u32[]{:S(2)}) collective-permute-start(bf16[64,48,128]{2,1,0:T(8,128)(2,1)} %sort_units.1.refs_0_), channel_id=1, source_target_pairs={{0,4},{1,5},{2,6},{3,7},{4,8},{5,9},{6,10},{7,11},{8,12},{9,13},{1... | collective-permute-start | bytes 2359304 | tf_op jit(solution)/shard_map/ppermute | solution.py:322
  178.8 60.5 %collective-permute-start.1 = (bf16[64,48,128]{2,1,0:T(8,128)(2,1)}, bf16[64,48,128]{2,1,0:T(8,128)(2,1)S(1)}, u32[]{:S(2)}, u32[]{:S(2)}) collective-permute-start(bf16[64,48,128]{2,1,0:T(8,128)(2,1)} %sort_units.1.refs_0_), channel_id=1, source_target_pairs={{0,2},{1,3},{2,4},{3,5},{4,6},{5,7},{6,8},{7,9},{8,10},{9,11},{10,... | collective-permute-start | bytes 2359304 | tf_op jit(solution)/shard_map/ppermute | solution.py:322
  182.8 56.5 %collective-permute-start = (bf16[64,48,128]{2,1,0:T(8,128)(2,1)}, bf16[64,48,128]{2,1,0:T(8,128)(2,1)}, u32[]{:S(2)}, u32[]{:S(2)}) collective-permute-start(bf16[64,48,128]{2,1,0:T(8,128)(2,1)} %sort_units.1.refs_0_), channel_id=1, source_target_pairs={{0,1},{1,0},{2,3},{3,2},{4,5},{5,4},{6,7},{7,6},{8,9},{9,8},{10,11... | collective-permute-start | bytes 2359304 | tf_op jit(solution)/shard_map/ppermute | solution.py:326
  185.1 82.7 %collective-permute-start.5 = (bf16[64,48,128]{2,1,0:T(8,128)(2,1)}, bf16[64,48,128]{2,1,0:T(8,128)(2,1)}, u32[]{:S(2)}, u32[]{:S(2)}) collective-permute-start(bf16[64,48,128]{2,1,0:T(8,128)(2,1)} %sort_units.1.refs_0_), channel_id=1, source_target_pairs={{0,64},{64,128},{128,192},{256,320},{320,384},{384,448},{1,65},{65... | collective-permute-start | bytes 2359304 | tf_op jit(solution)/shard_map/ppermute | solution.py:332
  191.1 62.6 %collective-permute-start.6 = (bf16[16,48,128]{2,1,0:T(8,128)(2,1)S(1)}, bf16[16,48,128]{2,1,0:T(8,128)(2,1)S(1)}, u32[]{:S(2)}, u32[]{:S(2)}) collective-permute-start(bf16[16,48,128]{2,1,0:T(8,128)(2,1)S(1)} %slice.4), channel_id=1, source_target_pairs={{0,256},{64,320},{128,384},{192,448},{256,0},{320,64},{384,128},{4... | collective-permute-start | bytes 589832 | tf_op jit(solution)/shard_map/ppermute | solution.py:339
  244.4 26.5 %collective-permute-start.4 = (bf16[4,9,16,128]{3,2,1,0:T(8,128)(2,1)S(1)}, bf16[4,9,16,128]{3,2,1,0:T(8,128)(2,1)S(1)}, u32[]{:S(2)}, u32[]{:S(2)}) collective-permute-start(bf16[4,9,16,128]{3,2,1,0:T(8,128)(2,1)S(1)} %get-tuple-element.10), channel_id=1, source_target_pairs={{0,1},{1,0},{2,3},{3,2},{4,5},{5,4},{6,7},{7,6},{8,9},{9,8},{10,11... | collective-permute-start | bytes 442376 | tf_op jit(solution)/shard_map/ppermute | solution.py:326
  251.3 19.7 %collective-permute-start.2 = (bf16[4,9,16,128]{3,2,1,0:T(8,128)(2,1)S(1)}, bf16[4,9,16,128]{3,2,1,0:T(8,128)(2,1)S(1)}, u32[]{:S(2)}, u32[]{:S(2)}) collective-permute-start(bf16[4,9,16,128]{3,2,1,0:T(8,128)(2,1)S(1)} %get-tuple-element.8), channel_id=1, source_target_pairs={{0,1},{1,0},{2,3},{3,2},{4,5},{5,4},{6,7},{7,6},{8,9},{9,8},{10,11... | collective-permute-start | bytes 442376 | tf_op jit(solution)/shard_map/ppermute | solution.py:326

commit v2 on v1

--- a/solution.py
+++ b/solution.py
@@ -23,6 +23,8 @@
 
 CHUNKS = ((0, 1, 2),)
 GROUP = 32
+MARK = 8
+PIECE = 16
 VMEM = pl.BlockSpec(memory_space=pltpu.VMEM)
 SMEM = pl.BlockSpec(memory_space=pltpu.SMEM)
 
@@ -39,7 +41,7 @@
             return chunk, part.index(component)
 
 
-def whiten_kernel(source_ref, band_ref, inverse_ref, archive_ref, *rest):
+def whiten_kernel(source_ref, band_ref, inverse_ref, archive_ref, mark_ref, *rest):
     outs, (level_ref,) = rest[:-1], rest[-1:]
     base = pl.program_id(0) * GROUP
     rows = GROUP * FH
@@ -88,13 +90,18 @@
                 for half in range(2):
                     start = c * TILE + half * FH
                     pieces.append(slab[start : start + FH] * gain)
-            out[position] = jnp.concatenate(pieces, axis=0).astype(jnp.bfloat16)
+            size = len(part) * TILE
+            start = pl.multiple_of((position % 2) * size, TILE)
+            out[position // 2, pl.ds(start, size), :] = jnp.concatenate(pieces, axis=0).astype(
+                jnp.bfloat16
+            )
         return carry
 
     lax.fori_loop(0, GROUP, divide, 0, unroll=4)
-
-
-def whiten(source, archive):
+    outs[0][:, 2 * len(CHUNKS[0]) * TILE :, :] = mark_ref[...]
+
+
+def whiten(source, archive, marks):
     low = jnp.arange(LANES, dtype=jnp.int32)
     gap = jnp.abs(low[:, None] - low[None, :])
     band = jnp.concatenate([gap <= HALF, gap >= LANES - HALF], axis=0).astype(jnp.bfloat16)
@@ -103,79 +110,100 @@
         jnp.minimum(bin_index + HALF, F - 1) - jnp.maximum(bin_index - HALF, 0) + 1
     ).astype(jnp.float32)
     inverse = (1.0 / bin_count).reshape(FH, LANES)
-    sizes = [len(part) * TILE for part in CHUNKS]
+    sizes = [2 * len(part) * TILE for part in CHUNKS]
+    sizes[0] += MARK
     return pl.pallas_call(
         whiten_kernel,
         grid=(CAP // GROUP,),
-        in_specs=[SMEM, VMEM, VMEM, VMEM],
-        out_specs=[pl.BlockSpec((GROUP, size, LANES), lambda g: (g, 0, 0)) for size in sizes],
-        out_shape=[jax.ShapeDtypeStruct((CAP, size, LANES), jnp.bfloat16) for size in sizes],
+        in_specs=[SMEM, VMEM, VMEM, VMEM]
+        + [pl.BlockSpec((GROUP // 2, MARK, LANES), lambda g: (g, 0, 0))],
+        out_specs=[
+            pl.BlockSpec((GROUP // 2, size, LANES), lambda g: (g, 0, 0)) for size in sizes
+        ],
+        out_shape=[
+            jax.ShapeDtypeStruct((marks.shape[0], size, LANES), jnp.bfloat16) for size in sizes
+        ],
         scratch_shapes=[pltpu.VMEM((GROUP * FH + 2 * FH, LANES), jnp.float32)],
         compiler_params=pltpu.CompilerParams(vmem_limit_bytes=16 * 1024 * 1024),
         cost_estimate=pl.CostEstimate(flops=200_000_000, bytes_accessed=4_000_000, transcendentals=0),
         name="whiten",
-    )(source, band, inverse, archive)
-
-
-def sort_kernel(source_ref, got_ref, out_ref):
+    )(source, band, inverse, archive, marks)
+
+
+def sort_kernel(source_ref, got_ref, *rest):
+    out_ref = rest[-1]
+    rows = out_ref.shape[1]
+
     def move(unit, carry):
-        out_ref[unit] = got_ref[source_ref[unit]]
+        place = source_ref[unit]
+        start = pl.multiple_of((place & 1) * rows, TILE)
+        out_ref[unit] = got_ref[place >> 1, pl.ds(start, rows), :]
         return carry
 
     lax.fori_loop(0, UNITS, move, 0, unroll=8)
 
 
-def sort_units(source, got):
+def sort_units(source, got, rows, *after):
     return pl.pallas_call(
         sort_kernel,
-        in_specs=[SMEM, VMEM],
+        in_specs=[SMEM, VMEM] + [pl.BlockSpec(memory_space=pl.ANY)] * len(after),
         out_specs=VMEM,
-        out_shape=jax.ShapeDtypeStruct((UNITS,) + got.shape[1:], jnp.bfloat16),
+        out_shape=jax.ShapeDtypeStruct((UNITS, rows, LANES), jnp.bfloat16),
         compiler_params=pltpu.CompilerParams(vmem_limit_bytes=16 * 1024 * 1024),
         cost_estimate=pl.CostEstimate(flops=0, bytes_accessed=3_000_000, transcendentals=0),
         name="sort_units",
-    )(source, got)
-
-
-def products(mine, other, chunk, store):
+    )(source, got, *after)
+
+
+def products(left_block, right_block, chunk, store):
     pairs = pairs_of(chunk)
 
-    def load(refs, unit, component):
+    def load(block, base, m, component):
         which, at = place_of(component)
-        tile = refs[which][unit, at * TILE : (at + 1) * TILE, :].astype(jnp.float32)
+        pieces = block[which]
+        if len(pieces) > 1:
+            ref, unit = pieces[base // PIECE], m
+        else:
+            ref, unit = pieces[0], base + m
+        tile = ref[unit, at * TILE : (at + 1) * TILE, :].astype(jnp.float32)
         return tile[:FH], tile[FH:]
 
     firsts = sorted({c for c, _ in pairs})
     seconds = sorted({d for _, d in pairs})
     for i in range(SB):
         for j in range(SB):
-
-            def step(m, sums):
-                left = {c: load(mine, i * SEGS + m, c) for c in firsts}
-                right = {d: load(other, j * SEGS + m, d) for d in seconds}
-                new = []
-                for n, (c, d) in enumerate(pairs):
-                    real, imag = sums[n]
-                    (ar, ai), (br, bi) = left[c], right[d]
-                    new.append((real + ar * br + ai * bi, imag + ai * br - ar * bi))
-                return tuple(new)
-
             zero = jnp.zeros((FH, LANES), jnp.float32)
-            sums = lax.fori_loop(
-                0, SEGS, step, tuple((zero, zero) for _ in pairs), unroll=2
-            )
+            sums = tuple((zero, zero) for _ in pairs)
+            for start in range(0, SEGS, PIECE):
+
+                def step(m, sums, start=start):
+                    left = {c: load(left_block, i * SEGS + start, m, c) for c in firsts}
+                    right = {d: load(right_block, j * SEGS + start, m, d) for d in seconds}
+                    new = []
+                    for n, (c, d) in enumerate(pairs):
+                        real, imag = sums[n]
+                        (ar, ai), (br, bi) = left[c], right[d]
+                        new.append((real + ar * br + ai * bi, imag + ai * br - ar * bi))
+                    return tuple(new)
+
+                sums = lax.fori_loop(0, PIECE, step, sums, unroll=2)
             for n, (real, imag) in enumerate(sums):
                 store(i, j, n, jnp.concatenate([real, imag], axis=0).astype(jnp.bfloat16))
 
 
-def cross_kernel(chunk, plan, flag_ref, *refs):
-    depth = chunk + 1
-    blocks = [refs[n : n + depth] for n in range(0, len(refs) - len(plan), depth)]
-    outs = refs[len(refs) - len(plan) :]
-    for out, (left, when_zero, when_one) in zip(outs, plan):
-
-        def store(i, j, n, tile, out=out):
-            out[i * SB + j, n] = tile
+def cross_kernel(chunk, plan, counts, flag_ref, *refs):
+    blocks, at = [], 0
+    for count in counts:
+        block = []
+        for _ in range(chunk + 1):
+            block.append(refs[at : at + count])
+            at += count
+        blocks.append(block)
+    out = refs[at]
+    for slot, (left, when_zero, when_one) in enumerate(plan):
+
+        def store(i, j, n, tile, slot=slot):
+            out[(slot * SB + i) * SB + j, n] = tile
 
         if when_zero == when_one:
             products(blocks[left], blocks[when_zero], chunk, store)
@@ -189,13 +217,13 @@
 
 def cross(chunk, plan, flag, *blocks):
     count = len(pairs_of(chunk))
-    shape = (SB * SB, count, TILE, LANES)
-    flat = [part for block in blocks for part in block[: chunk + 1]]
+    shape = (len(plan) * SB * SB, count, TILE, LANES)
+    flat = [piece for block in blocks for part in block[: chunk + 1] for piece in part]
     return pl.pallas_call(
-        functools.partial(cross_kernel, chunk, plan),
+        functools.partial(cross_kernel, chunk, plan, tuple(len(block[0]) for block in blocks)),
         in_specs=[SMEM] + [VMEM] * len(flat),
-        out_specs=[VMEM] * len(plan),
-        out_shape=[jax.ShapeDtypeStruct(shape, jnp.bfloat16)] * len(plan),
+        out_specs=VMEM,
+        out_shape=jax.ShapeDtypeStruct(shape, jnp.bfloat16),
         compiler_params=pltpu.CompilerParams(vmem_limit_bytes=24 * 1024 * 1024),
         cost_estimate=pl.CostEstimate(
             flops=len(plan) * 40_000_000, bytes_accessed=len(plan) * 1_500_000, transcendentals=0
@@ -211,14 +239,15 @@
 
 def series_kernel(table_ref, *refs):
     chunks = len(CHUNKS)
-    sources = refs[: (STEPS + 1) * chunks]
-    cycle_ref, region_ref, wide_ref, rows_ref = refs[(STEPS + 1) * chunks :]
+    sources = refs[: 3 * chunks]
+    cycle_ref, region_ref, wide_ref, rows_ref = refs[3 * chunks :]
 
     @pl.when(pl.program_id(0) == 0)
     def _():
         for k in range(STEPS + 1):
             for chunk in range(chunks):
-                source = sources[k * chunks + chunk]
+                source = sources[(k // 2) * chunks + chunk]
+                first = (k % 2) * SB * SB
                 for i in range(SB):
                     for j in range(SB):
                         for n, (c, d) in enumerate(pairs_of(chunk)):
@@ -227,7 +256,7 @@
                             else:
                                 row = CYCLE_ROWS + (i * 9 + 3 * c + d) * SB + j
                             wide_ref[row * TILE : (row + 1) * TILE, :] = source[
-                                i * SB + j, n
+                                first + i * SB + j, n
                             ].astype(jnp.float32)
         for piece in range(TILE):
             rows_ref[:, piece * LANES : (piece + 1) * LANES] = wide_ref[
@@ -310,7 +339,7 @@
             pl.BlockSpec((2, FH, width), lambda s, n: (0, 0, n)),
         ],
         out_specs=pl.BlockSpec((F, width), lambda s, n: (s, n)),
-        out_shape=jax.ShapeDtypeStruct((2 * F, LAGS), jnp.bfloat16),
+        out_shape=pltpu.HBM((2 * F, LAGS), jnp.bfloat16),
         compiler_params=pltpu.CompilerParams(vmem_limit_bytes=16 * 1024 * 1024),
         cost_estimate=pl.CostEstimate(flops=16_000_000, bytes_accessed=12_000_000, transcendentals=0),
         name="lag_table",
@@ -322,26 +351,26 @@
     return lax.ppermute(block, axis, [(i, (i + by) % size) for i in range(size)])
 
 
-def swapped(block):
-    return lax.ppermute(block, "blk", [(i, i ^ 1) for i in range(lax.axis_size("blk"))])
-
-
-def from_previous_region(block, planes, crossing):
+def spread(block, planes):
     regions = lax.axis_size("region")
     groups = [list(range(n, n + planes)) for n in range(0, regions, planes)]
+    parts = lax.all_to_all(
+        block, "region", split_axis=0, concat_axis=0, tiled=True, axis_index_groups=groups
+    )
+    return parts[(planes - 1) * PIECE :]
+
+
+def from_previous_region(block, piece, planes):
+    regions = lax.axis_size("region")
     near = lax.ppermute(
         block, "region", [(i, i + 1) for i in range(regions) if (i + 1) % planes]
     )
-    rows = block.shape[0] // planes
-    parts = lax.all_to_all(
-        block, "region", split_axis=0, concat_axis=0, tiled=True, axis_index_groups=groups
-    )
-    part = lax.ppermute(
-        parts[(planes - 1) * rows :],
-        "region",
-        [(i, (i + planes) % regions) for i in range(regions)],
-    )
-    far = lax.all_gather(part, "region", axis=0, tiled=True, axis_index_groups=groups)
+    piece = lax.ppermute(piece, "region", [(i, (i + planes) % regions) for i in range(regions)])
+    far = [piece]
+    for plane in range(1, planes):
+        far.append(
+            lax.ppermute(piece, "region", [(n + plane, n) for n in range(0, regions, planes)])
+        )
     return near, far
 
 
@@ -349,68 +378,58 @@
     blocks = lax.axis_size("blk")
     slot = jnp.arange(CAP, dtype=jnp.int32)
     ids = jnp.where(slot < row_counts[0], unit_of, -1)
-    ids_all = lax.all_gather(ids, "blk")
-
     owners = jnp.arange(blocks, dtype=jnp.int32)
     sent = (ids >> 6)[None, :] == owners[:, None]
-    first = jnp.min(jnp.where(sent, slot, CAP - 1), axis=1)
-    last = jnp.max(jnp.where(sent, slot, 0), axis=1)
-    source = jnp.stack([first, last], axis=1).reshape(2 * blocks)
-    send = whiten(source, archive.reshape(CAP, 3 * TILE, LANES))
-
-    got = []
-    for part in send:
-        rows = part.shape[1]
-        moved = lax.all_to_all(
-            part.reshape(blocks, 2 * rows, LANES), "blk", split_axis=0, concat_axis=0, tiled=True
-        )
-        got.append(moved.reshape(2 * blocks, rows, LANES))
+    key = slot * UNITS + (ids & (UNITS - 1))
+    none = CAP * UNITS
+    first = jnp.min(jnp.where(sent, key, none), axis=1)
+    last = jnp.max(jnp.where(sent, key, -1), axis=1)
+    source = jnp.clip(jnp.stack([first, last], axis=1) >> 6, 0, CAP - 1).reshape(2 * blocks)
+    first_id = jnp.where(first < none, first & (UNITS - 1), -1).astype(jnp.bfloat16)
+    last_id = jnp.where(last > first, last & (UNITS - 1), -1).astype(jnp.bfloat16)
+    lane = jnp.arange(LANES, dtype=jnp.int32)
+    marks = jnp.broadcast_to(
+        jnp.where(lane[None, :] < LANES // 2, first_id[:, None], last_id[:, None])[:, None, :],
+        (blocks, MARK, LANES),
+    )
+    send = whiten(source, archive.reshape(CAP, 3 * TILE, LANES), marks)
+    got = [
+        lax.all_to_all(part, "blk", split_axis=0, concat_axis=0, tiled=True) for part in send
+    ]
 
     table = make_table()
-    index = lax.axis_index("blk")
-    mine = (ids_all >> 6) == index
-    key = slot[None, :] * UNITS + (ids_all & (UNITS - 1))
-    none = CAP * UNITS
-    low = jnp.min(jnp.where(mine, key, none), axis=1)
-    high = jnp.max(jnp.where(mine, key, -1), axis=1)
+    got[0], table = lax.optimization_barrier((got[0], table))
+    found = got[0][:, 2 * len(CHUNKS[0]) * TILE, :].astype(jnp.int32)
     units = jnp.arange(UNITS, dtype=jnp.int32)[:, None]
-    in_first = (low < none)[None, :] & ((low & (UNITS - 1))[None, :] == units)
-    in_second = (high > low)[None, :] & ((high & (UNITS - 1))[None, :] == units)
     place = jnp.sum(
-        jnp.where(in_first, 2 * owners[None, :], 0)
-        + jnp.where(in_second, 2 * owners[None, :] + 1, 0),
+        jnp.where(found[:, 0][None, :] == units, 2 * owners[None, :], 0)
+        + jnp.where(found[:, LANES - 1][None, :] == units, 2 * owners[None, :] + 1, 0),
         axis=1,
     )
     place = jnp.clip(place, 0, 2 * blocks - 1)
 
-    core = index & 1
     planes = 4
     edge = (lax.axis_index("region") % planes == 0).astype(jnp.int32)
-    own, twin, two, four, near, far = [], [], [], [], [], []
-    cycle = [[], [], [], []]
-    region = []
-    for chunk in range(len(CHUNKS)):
-        block = sort_units(place, got[chunk])
-        own.append(block)
-        closer, further = from_previous_region(block, planes, edge)
-        two.append(shifted(block, "blk", 2))
-        twin.append(swapped(block))
-        four.append(shifted(block, "blk", 4))
-        near.append(closer)
+    own, one, two, ahead, near, far = [], [], [], [], [], []
+    lower, upper, across = [], [], []
+    for chunk, part in enumerate(CHUNKS):
+        rows = len(part) * TILE
+        early = sort_units(place, got[chunk], rows)
+        piece = spread(early, planes)
+        closer, further = from_previous_region(early, piece, planes)
+        block = sort_units(place, got[chunk], rows, piece)
+        own.append([block])
+        one.append([shifted(block, "blk", 1)])
+        two.append([shifted(block, "blk", 2)])
+        ahead.append([shifted(block, "blk", -2)])
+        near.append([closer])
         far.append(further)
-        by_two, for_one = cross(
-            chunk, ((0, 2, 2), (1, 0, 2)), core, own, twin, two
-        )
-        by_four, for_three = cross(
-            chunk, ((0, 3, 3), (1, 2, 3)), core, own, twin, two, four
-        )
-        by_one, by_three = swapped(for_one), swapped(for_three)
-        for k, result in enumerate((by_one, by_two, by_three, by_four)):
-            cycle[k].append(result)
-        region.extend(cross(chunk, ((0, 1, 2),), edge, own, near, far))
-
-    sources = [result for k in range(STEPS) for result in cycle[k]] + region
-    cycle_series, region_series = lag_series(table, sources)
+        lower.append(cross(chunk, ((0, 1, 1), (0, 2, 2)), edge, own, one, two))
+        later = cross(chunk, ((0, 1, 1), (0, 2, 2)), edge, ahead, one, two)
+        upper.append(shifted(later, "blk", 2))
+        across.append(cross(chunk, ((0, 1, 2),), edge, own, near, far))
+
+    cycle_series, region_series = lag_series(table, lower + upper + across)
     return jnp.swapaxes(cycle_series, 2, 3), jnp.swapaxes(region_series, 1, 2)
 
 

time: 278 us -> 214 us (0.77)
  the two profiles are of different devices: /device:TPU:2 before, /device:TPU:57 now
where the time goes in v2:
time: 214 us; the launch traced here: 213 us
  waiting for transfers between devices  106 us (50%)
  starting transfers between devices  49.2 us (23%)
  Pallas kernels  30.3 us (14%)
  blocking collectives  14.2 us (7%)
  local copies, waits for them, and re-layouts  6.75 us (3%)
  other arithmetic  5.74 us (3%)
    all_to_all x1, waiting for transfers between devices, body(): lax.all_to_all(part, 'blk', split_axis=0, concat_axis=0, tiled=True)  65.4 us
    ppermute x4, waiting for transfers between devices, shifted(): lax.ppermute(block, axis, [(i, (i + by) % size) for i in range(size)])  22.1 us
    ppermute x4, starting transfers between devices, shifted(): lax.ppermute(block, axis, [(i, (i + by) % size) for i in range(size)])  18.5 us
    all_to_all x1, starting transfers between devices, body(): lax.all_to_all(part, 'blk', split_axis=0, concat_axis=0, tiled=True)  15.8 us
    all_to_all x1, blocking collectives, spread(): lax.all_to_all(block, 'region', split_axis=0, concat_axis=0, tiled=True,...  14.2 us
    ppermute x3, waiting for transfers between devices, from_previous_region(): lax.ppermute(piece, 'region', [(n + plane, n) for n in range(0, regions,...  12 us
    pallas_call x3, Pallas kernels, cross(): pl.pallas_call(functools.partial(cross_kernel, chunk, plan, tuple((len(bl...  11.1 us
    ppermute x1, starting transfers between devices, from_previous_region(): lax.ppermute(piece, 'region', [(i, (i + planes) % regions) for i in range...  7.93 us
  transfers between devices with their start and end apart: 10, of which 6 were waited for; matrix products, arithmetic and copies ran while one was open for 2% of the time, Pallas kernels for 9%

profile of v2, /device:TPU:57, one launch (start us, length us, event | category | flops | bytes accessed | tf_op | source)
XLA Modules:
  0.0 213.3 jit_solution(6692323405574972956)
XLA Ops:
  2.4 1.9 copy.11
  5.5 4.5 %whiten.1 = bf16[64,104,128]{2,1,0:T(8,128)(2,1)} custom-call(s32[128]{0:T(128)S(1)} %min.27.source_ref, bf16[256,128]{1,0:T(8,128)(2,1)S(1)} %add_convert_fusion.band_ref, f32[8,128]{1,0:T(8,128)S(1)} %convert_divide_fusion.inverse_ref, bf16[128,48,128]{2,1,0:T(8,128)(2,1)S(1)} %copy.12.archive_ref, bf16[64,8,128]{2,1,0:T(8,128)(2,1)S(1)} %broadcast_in_dim.91.mark_ref), custom_call_target="tpu_custom_call" | custom-call | flops 200000000 | bytes 4000000 | tf_op jit(solution)/shard_map/whiten/pallas_call | solution.py:115
  9.9 15.8 %all-to-all-start = ((bf16[64,104,128]{2,1,0:T(8,128)(2,1)}), bf16[64,104,128]{2,1,0:T(8,128)(2,1)S(1)}, u32[]{:S(2)}, u32[]{:S(2)}) async-start(bf16[64,104,128]{2,1,0:T(8,128)(2,1)} %whiten.1), calls=%async_computation | async-start | bytes 3407872 | tf_op jit(solution)/shard_map/all_to_all | solution.py:397
  26.1 4.1 %fusion.7 = (f32[1,128,2048]{2,1,0:T(8,128)S(1)}, f32[1,128,2048]{2,1,0:T(8,128)S(1)}) fusion(s32[2048]{0:T(1024)S(1)} %iota_add_fusion), kind=kLoop, calls=%fused_computation.11 | loop fusion | flops 3670016 | bytes 2105344 | tf_op jit(solution)/shard_map/cos | solution.py:329
  30.4 7.3 %lag_table.1.table_ref = bf16[2048,2048]{1,0:T(8,128)(2,1)} custom-call(f32[2,128,2048]{2,1,0:T(8,128)S(1)} %pad_maximum_fusion.fine_ref, f32[2,8,2048]{2,1,0:T(8,128)S(1)} %pad_maximum_fusion.1.coarse_ref), custom_call_target="tpu_custom_call" | custom-call | flops 16000000 | bytes 12000000 | tf_op jit(solution)/shard_map/lag_table/pallas_call | solution.py:334
  37.7 65.4 %all-to-all-done.got_ref = bf16[64,104,128]{2,1,0:T(8,128)(2,1)S(1)} async-done(((bf16[64,104,128]{2,1,0:T(8,128)(2,1)}), bf16[64,104,128]{2,1,0:T(8,128)(2,1)S(1)}, u32[]{:S(2)}, u32[]{:S(2)}) %all-to-all-start) | async-done | bytes 1703968 | tf_op jit(solution)/shard_map/all_to_all | solution.py:397
  104.3 14.2 %all_to_all.10 = bf16[64,48,128]{2,1,0:T(8,128)(2,1)S(1)} all-to-all(bf16[64,48,128]{2,1,0:T(8,128)(2,1)S(1)} %sort_units.2), channel_id=1, replica_groups={{0,64,128,192},{256,320,384,448},{1,65,129,193},{257,321,385,449},{2,66..., dimensions={0} | all-to-all | bytes 1572864 | tf_op jit(solution)/shard_map/all_to_all | solution.py:357
  119.3 6.4 %collective-permute-start = (bf16[64,48,128]{2,1,0:T(8,128)(2,1)S(1)}, bf16[64,48,128]{2,1,0:T(8,128)(2,1)S(1)}, u32[]{:S(2)}, u32[]{:S(2)}) collective-permute-start(bf16[64,48,128]{2,1,0:T(8,128)(2,1)S(1)} %sort_units.3.refs_0_), channel_id=1, source_target_pairs={{0,1},{1,2},{2,3},{3,4},{4,5},{5,6},{6,7},{7,8},{8,9},{9,10},{10,1... | collective-permute-start | bytes 2359304 | tf_op jit(solution)/shard_map/ppermute | solution.py:351
  125.7 3.1 %collective-permute-start.1 = (bf16[64,48,128]{2,1,0:T(8,128)(2,1)S(1)}, bf16[64,48,128]{2,1,0:T(8,128)(2,1)S(1)}, u32[]{:S(2)}, u32[]{:S(2)}) collective-permute-start(bf16[64,48,128]{2,1,0:T(8,128)(2,1)S(1)} %sort_units.3.refs_0_), channel_id=1, source_target_pairs={{0,2},{1,3},{2,4},{3,5},{4,6},{5,7},{6,8},{7,9},{8,10},{9,11},{10,... | collective-permute-start | bytes 2359304 | tf_op jit(solution)/shard_map/ppermute | solution.py:351
  128.8 2.2 %collective-permute-start.2 = (bf16[64,48,128]{2,1,0:T(8,128)(2,1)S(1)}, bf16[64,48,128]{2,1,0:T(8,128)(2,1)}, u32[]{:S(2)}, u32[]{:S(2)}) collective-permute-start(bf16[64,48,128]{2,1,0:T(8,128)(2,1)S(1)} %sort_units.3.refs_0_), channel_id=1, source_target_pairs={{0,62},{1,63},{2,0},{3,1},{4,2},{5,3},{6,4},{7,5},{8,6},{9,7},{10,... | collective-permute-start | bytes 2359304 | tf_op jit(solution)/shard_map/ppermute | solution.py:351
  131.0 3.1 %collective-permute-start.4 = (bf16[64,48,128]{2,1,0:T(8,128)(2,1)S(1)}, bf16[64,48,128]{2,1,0:T(8,128)(2,1)}, u32[]{:S(2)}, u32[]{:S(2)}) collective-permute-start(bf16[64,48,128]{2,1,0:T(8,128)(2,1)S(1)} %sort_units.2), channel_id=1, source_target_pairs={{0,64},{64,128},{128,192},{256,320},{320,384},{384,448},{1,65},{65... | collective-permute-start | bytes 2359304 | tf_op jit(solution)/shard_map/ppermute | solution.py:365
  134.1 7.9 %collective-permute-start.5 = (bf16[16,48,128]{2,1,0:T(8,128)(2,1)S(1)}, bf16[16,48,128]{2,1,0:T(8,128)(2,1)}, u32[]{:S(2)}, u32[]{:S(2)}) collective-permute-start(bf16[16,48,128]{2,1,0:T(8,128)(2,1)S(1)} %slice.18.rest_0_), channel_id=1, source_target_pairs={{0,256},{64,320},{128,384},{192,448},{256,0},{320,64},{384,128},{4... | collective-permute-start | bytes 589832 | tf_op jit(solution)/shard_map/ppermute | solution.py:368
  142.0 22.1 %collective-permute-done.1.refs_2_ = bf16[64,48,128]{2,1,0:T(8,128)(2,1)S(1)} collective-permute-done((bf16[64,48,128]{2,1,0:T(8,128)(2,1)S(1)}, bf16[64,48,128]{2,1,0:T(8,128)(2,1)S(1)}, u32[]{:S(2)}, u32[]{:S(2)}) %collective-permute-start.1) | collective-permute-done | bytes 786464 | tf_op jit(solution)/shard_map/ppermute | solution.py:351
  164.1 4.7 %cross.4 = bf16[8,9,16,128]{3,2,1,0:T(8,128)(2,1)S(1)} custom-call(s32[1]{0:T(128)} %bitcast.4.flag_ref, bf16[64,48,128]{2,1,0:T(8,128)(2,1)} %collective-permute-done.2.refs_0_, bf16[64,48,128]{2,1,0:T(8,128)(2,1)S(1)} %collective-permute-done.refs_1_, bf16[64,48,128]{2,1,0:T(8,128)(2,1)S(1)} %collective-permute-done.1.refs_2_), custom_call_target="tpu_custom_call" | custom-call | flops 80000000 | bytes 3000000 | tf_op jit(solution)/shard_map/cross/pallas_call | solution.py:222
  168.8 6.8 %collective-permute-start.3 = (bf16[8,9,16,128]{3,2,1,0:T(8,128)(2,1)S(1)}, bf16[8,9,16,128]{3,2,1,0:T(8,128)(2,1)S(1)}, u32[]{:S(2)}, u32[]{:S(2)}) collective-permute-start(bf16[8,9,16,128]{3,2,1,0:T(8,128)(2,1)S(1)} %cross.4), channel_id=1, source_target_pairs={{0,2},{1,3},{2,4},{3,5},{4,6},{5,7},{6,8},{7,9},{8,10},{9,11},{10,... | collective-permute-start | bytes 884744 | tf_op jit(solution)/shard_map/ppermute | solution.py:351
  175.6 6.0 %collective-permute-done.5.refs_2_ = bf16[16,48,128]{2,1,0:T(8,128)(2,1)} collective-permute-done((bf16[16,48,128]{2,1,0:T(8,128)(2,1)S(1)}, bf16[16,48,128]{2,1,0:T(8,128)(2,1)}, u32[]{:S(2)}, u32[]{:S(2)}) %collective-permute-start.5) | collective-permute-done | bytes 196640 | tf_op jit(solution)/shard_map/ppermute | solution.py:368
  182.9 1.3 collective-permute-start.7
  185.5 4.2 %collective-permute-done.6.refs_3_ = bf16[16,48,128]{2,1,0:T(8,128)(2,1)S(1)} collective-permute-done((bf16[16,48,128]{2,1,0:T(8,128)(2,1)}, bf16[16,48,128]{2,1,0:T(8,128)(2,1)S(1)}, u32[]{:S(2)}, u32[]{:S(2)}) %collective-permute-start.6) | collective-permute-done | bytes 196640 | tf_op jit(solution)/shard_map/ppermute | solution.py:372
  189.7 2.8 %collective-permute-done.7.refs_4_ = bf16[16,48,128]{2,1,0:T(8,128)(2,1)S(1)} collective-permute-done((bf16[16,48,128]{2,1,0:T(8,128)(2,1)}, bf16[16,48,128]{2,1,0:T(8,128)(2,1)S(1)}, u32[]{:S(2)}, u32[]{:S(2)}) %collective-permute-start.7) | collective-permute-done | bytes 196640 | tf_op jit(solution)/shard_map/ppermute | solution.py:372
  192.6 5.0 %collective-permute-done.8.refs_5_ = bf16[16,48,128]{2,1,0:T(8,128)(2,1)S(1)} collective-permute-done((bf16[16,48,128]{2,1,0:T(8,128)(2,1)}, bf16[16,48,128]{2,1,0:T(8,128)(2,1)S(1)}, u32[]{:S(2)}, u32[]{:S(2)}) %collective-permute-start.8) | collective-permute-done | bytes 196640 | tf_op jit(solution)/shard_map/ppermute | solution.py:372
  197.5 2.9 %cross.5.refs_2_ = bf16[4,9,16,128]{3,2,1,0:T(8,128)(2,1)S(1)} custom-call(s32[1]{0:T(128)} %bitcast.4.flag_ref, bf16[64,48,128]{2,1,0:T(8,128)(2,1)S(1)} %sort_units.3.refs_0_, bf16[64,48,128]{2,1,0:T(8,128)(2,1)} %collective-permute-done.4.refs_1_, bf16[16,48,128]{2,1,0:T(8,128)(2,1)} %collective-permute-done.5.refs_2_, ...), custom_call_target="tpu_custom_call" | custom-call | flops 40000000 | bytes 1500000 | tf_op jit(solution)/shard_map/cross/pallas_call | solution.py:222
  200.5 3.5 %cross.3.refs_0_ = bf16[8,9,16,128]{3,2,1,0:T(8,128)(2,1)S(1)} custom-call(s32[1]{0:T(128)} %bitcast.4.flag_ref, bf16[64,48,128]{2,1,0:T(8,128)(2,1)S(1)} %sort_units.3.refs_0_, bf16[64,48,128]{2,1,0:T(8,128)(2,1)S(1)} %collective-permute-done.refs_1_, bf16[64,48,128]{2,1,0:T(8,128)(2,1)S(1)} %collective-permute-done.1.refs_2_), custom_call_target="tpu_custom_call" | custom-call | flops 80000000 | bytes 3000000 | tf_op jit(solution)/shard_map/cross/pallas_call | solution.py:222
  204.0 3.4 %copy-done = bf16[2048,2048]{1,0:T(8,128)(2,1)S(1)} copy-done((bf16[2048,2048]{1,0:T(8,128)(2,1)S(1)}, bf16[2048,2048]{1,0:T(8,128)(2,1)}, u32[]{:S(2)}) %copy-start) | copy-done | bytes 8388632
  207.4 5.9 %lag_series.1 = (bf16[2,4,9,2,2048]{4,3,2,1,0:T(2,128)(2,1)}, bf16[2,9,2,2048]{3,2,1,0:T(2,128)(2,1)}) custom-call(bf16[2048,2048]{1,0:T(8,128)(2,1)S(1)} %copy-done, bf16[8,9,16,128]{3,2,1,0:T(8,128)(2,1)S(1)} %cross.3.refs_0_, bf16[8,9,16,128]{3,2,1,0:T(8,128)(2,1)S(1)} %collective-permute-done.3.refs_1_, bf16[4,9,16,128]{3,2,1,0:T(8,128)(2,1)S(1)} %cross.5.refs_2_), custom_call_target="tpu_custom_call" | custom-call | flops 1509949440 | bytes 12000000 | tf_op jit(solution)/shard_map/lag_series/pallas_call | solution.py:279
  (33 shorter events, 7.2 us)
Async XLA Ops:
  9.9 93.2 %all-to-all-start = ((bf16[64,104,128]{2,1,0:T(8,128)(2,1)}), bf16[64,104,128]{2,1,0:T(8,128)(2,1)S(1)}, u32[]{:S(2)}, u32[]{:S(2)}) async-start(bf16[64,104,128]{2,1,0:T(8,128)(2,1)} %whiten.1), calls=%async_computation | async-start | bytes 3407872 | tf_op jit(solution)/shard_map/all_to_all | solution.py:397
  119.3 22.8 %collective-permute-start = (bf16[64,48,128]{2,1,0:T(8,128)(2,1)S(1)}, bf16[64,48,128]{2,1,0:T(8,128)(2,1)S(1)}, u32[]{:S(2)}, u32[]{:S(2)}) collective-permute-start(bf16[64,48,128]{2,1,0:T(8,128)(2,1)S(1)} %sort_units.3.refs_0_), channel_id=1, source_target_pairs={{0,1},{1,2},{2,3},{3,4},{4,5},{5,6},{6,7},{7,8},{8,9},{9,10},{10,1... | collective-permute-start | bytes 2359304 | tf_op jit(solution)/shard_map/ppermute | solution.py:351
  125.7 38.4 %collective-permute-start.1 = (bf16[64,48,128]{2,1,0:T(8,128)(2,1)S(1)}, bf16[64,48,128]{2,1,0:T(8,128)(2,1)S(1)}, u32[]{:S(2)}, u32[]{:S(2)}) collective-permute-start(bf16[64,48,128]{2,1,0:T(8,128)(2,1)S(1)} %sort_units.3.refs_0_), channel_id=1, source_target_pairs={{0,2},{1,3},{2,4},{3,5},{4,6},{5,7},{6,8},{7,9},{8,10},{9,11},{10,... | collective-permute-start | bytes 2359304 | tf_op jit(solution)/shard_map/ppermute | solution.py:351
  128.8 35.3 %collective-permute-start.2 = (bf16[64,48,128]{2,1,0:T(8,128)(2,1)S(1)}, bf16[64,48,128]{2,1,0:T(8,128)(2,1)}, u32[]{:S(2)}, u32[]{:S(2)}) collective-permute-start(bf16[64,48,128]{2,1,0:T(8,128)(2,1)S(1)} %sort_units.3.refs_0_), channel_id=1, source_target_pairs={{0,62},{1,63},{2,0},{3,1},{4,2},{5,3},{6,4},{7,5},{8,6},{9,7},{10,... | collective-permute-start | bytes 2359304 | tf_op jit(solution)/shard_map/ppermute | solution.py:351
  131.0 54.5 %collective-permute-start.4 = (bf16[64,48,128]{2,1,0:T(8,128)(2,1)S(1)}, bf16[64,48,128]{2,1,0:T(8,128)(2,1)}, u32[]{:S(2)}, u32[]{:S(2)}) collective-permute-start(bf16[64,48,128]{2,1,0:T(8,128)(2,1)S(1)} %sort_units.2), channel_id=1, source_target_pairs={{0,64},{64,128},{128,192},{256,320},{320,384},{384,448},{1,65},{65... | collective-permute-start | bytes 2359304 | tf_op jit(solution)/shard_map/ppermute | solution.py:365
  134.1 47.5 %collective-permute-start.5 = (bf16[16,48,128]{2,1,0:T(8,128)(2,1)S(1)}, bf16[16,48,128]{2,1,0:T(8,128)(2,1)}, u32[]{:S(2)}, u32[]{:S(2)}) collective-permute-start(bf16[16,48,128]{2,1,0:T(8,128)(2,1)S(1)} %slice.18.rest_0_), channel_id=1, source_target_pairs={{0,256},{64,320},{128,384},{192,448},{256,0},{320,64},{384,128},{4... | collective-permute-start | bytes 589832 | tf_op jit(solution)/shard_map/ppermute | solution.py:368
  168.8 35.2 %collective-permute-start.3 = (bf16[8,9,16,128]{3,2,1,0:T(8,128)(2,1)S(1)}, bf16[8,9,16,128]{3,2,1,0:T(8,128)(2,1)S(1)}, u32[]{:S(2)}, u32[]{:S(2)}) collective-permute-start(bf16[8,9,16,128]{3,2,1,0:T(8,128)(2,1)S(1)} %cross.4), channel_id=1, source_target_pairs={{0,2},{1,3},{2,4},{3,5},{4,6},{5,7},{6,8},{7,9},{8,10},{9,11},{10,... | collective-permute-start | bytes 884744 | tf_op jit(solution)/shard_map/ppermute | solution.py:351
  181.6 8.1 %collective-permute-start.6 = (bf16[16,48,128]{2,1,0:T(8,128)(2,1)}, bf16[16,48,128]{2,1,0:T(8,128)(2,1)S(1)}, u32[]{:S(2)}, u32[]{:S(2)}) collective-permute-start(bf16[16,48,128]{2,1,0:T(8,128)(2,1)} %collective-permute-done.5.refs_2_), channel_id=1, source_target_pairs={{64,0},{320,256},{65,1},{321,257},{66,2},{322,258},{67,3},{323,259... | collective-permute-start | bytes 589832 | tf_op jit(solution)/shard_map/ppermute | solution.py:372
  182.9 9.7 %collective-permute-start.7 = (bf16[16,48,128]{2,1,0:T(8,128)(2,1)}, bf16[16,48,128]{2,1,0:T(8,128)(2,1)S(1)}, u32[]{:S(2)}, u32[]{:S(2)}) collective-permute-start(bf16[16,48,128]{2,1,0:T(8,128)(2,1)} %collective-permute-done.5.refs_2_), channel_id=1, source_target_pairs={{128,0},{384,256},{129,1},{385,257},{130,2},{386,258},{131,3},{387... | collective-permute-start | bytes 589832 | tf_op jit(solution)/shard_map/ppermute | solution.py:372
  184.2 13.4 %collective-permute-start.8 = (bf16[16,48,128]{2,1,0:T(8,128)(2,1)}, bf16[16,48,128]{2,1,0:T(8,128)(2,1)S(1)}, u32[]{:S(2)}, u32[]{:S(2)}) collective-permute-start(bf16[16,48,128]{2,1,0:T(8,128)(2,1)} %collective-permute-done.5.refs_2_), channel_id=1, source_target_pairs={{192,0},{448,256},{193,1},{449,257},{194,2},{450,258},{195,3},{451... | collective-permute-start | bytes 589832 | tf_op jit(solution)/shard_map/ppermute | solution.py:372
  204.0 3.4 %copy-start = (bf16[2048,2048]{1,0:T(8,128)(2,1)S(1)}, bf16[2048,2048]{1,0:T(8,128)(2,1)}, u32[]{:S(2)}) copy-start(bf16[2048,2048]{1,0:T(8,128)(2,1)} %lag_table.1.table_ref) | copy-start | bytes 25165828

commit v3 on v2

--- a/solution.py
+++ b/solution.py
@@ -130,8 +130,7 @@
     )(source, band, inverse, archive, marks)
 
 
-def sort_kernel(source_ref, got_ref, *rest):
-    out_ref = rest[-1]
+def sort_kernel(source_ref, got_ref, out_ref):
     rows = out_ref.shape[1]
 
     def move(unit, carry):
@@ -143,16 +142,46 @@
     lax.fori_loop(0, UNITS, move, 0, unroll=8)
 
 
-def sort_units(source, got, rows, *after):
+def sort_units(source, got, rows):
     return pl.pallas_call(
         sort_kernel,
-        in_specs=[SMEM, VMEM] + [pl.BlockSpec(memory_space=pl.ANY)] * len(after),
+        in_specs=[SMEM, VMEM],
         out_specs=VMEM,
         out_shape=jax.ShapeDtypeStruct((UNITS, rows, LANES), jnp.bfloat16),
         compiler_params=pltpu.CompilerParams(vmem_limit_bytes=16 * 1024 * 1024),
         cost_estimate=pl.CostEstimate(flops=0, bytes_accessed=3_000_000, transcendentals=0),
         name="sort_units",
-    )(source, got, *after)
+    )(source, got)
+
+
+def choose_kernel(plane_ref, block_ref, *refs):
+    pieces, (piece_ref, out_ref) = refs[:-2], refs[-2:]
+    last = len(pieces)
+    out_ref[...] = block_ref[...]
+    for plane, ref in enumerate(pieces):
+
+        @pl.when(plane_ref[0] == plane)
+        def _(ref=ref):
+            piece_ref[...] = ref[...]
+
+    @pl.when(plane_ref[0] == last)
+    def _():
+        piece_ref[...] = block_ref[last * PIECE :]
+
+
+def choose(plane, block, pieces):
+    return pl.pallas_call(
+        choose_kernel,
+        in_specs=[SMEM] + [VMEM] * (1 + len(pieces)),
+        out_specs=[VMEM, VMEM],
+        out_shape=[
+            jax.ShapeDtypeStruct(pieces[0].shape, jnp.bfloat16),
+            jax.ShapeDtypeStruct(block.shape, jnp.bfloat16),
+        ],
+        compiler_params=pltpu.CompilerParams(vmem_limit_bytes=16 * 1024 * 1024),
+        cost_estimate=pl.CostEstimate(flops=0, bytes_accessed=2_000_000, transcendentals=0),
+        name="choose_piece",
+    )(plane.reshape(1), block, *pieces)
 
 
 def products(left_block, right_block, chunk, store):
@@ -199,11 +228,11 @@
             block.append(refs[at : at + count])
             at += count
         blocks.append(block)
-    out = refs[at]
-    for slot, (left, when_zero, when_one) in enumerate(plan):
-
-        def store(i, j, n, tile, slot=slot):
-            out[(slot * SB + i) * SB + j, n] = tile
+    outs = refs[len(refs) - len(plan) :]
+    for out, (left, when_zero, when_one) in zip(outs, plan):
+
+        def store(i, j, n, tile, out=out):
+            out[i * SB + j, n] = tile
 
         if when_zero == when_one:
             products(blocks[left], blocks[when_zero], chunk, store)
@@ -215,21 +244,23 @@
                     products(blocks[left], blocks[right], chunk, store)
 
 
-def cross(chunk, plan, flag, *blocks):
+def cross(chunk, plan, flag, blocks, after=()):
     count = len(pairs_of(chunk))
-    shape = (len(plan) * SB * SB, count, TILE, LANES)
+    shape = (SB * SB, count, TILE, LANES)
     flat = [piece for block in blocks for part in block[: chunk + 1] for piece in part]
     return pl.pallas_call(
         functools.partial(cross_kernel, chunk, plan, tuple(len(block[0]) for block in blocks)),
-        in_specs=[SMEM] + [VMEM] * len(flat),
-        out_specs=VMEM,
-        out_shape=jax.ShapeDtypeStruct(shape, jnp.bfloat16),
+        in_specs=[SMEM]
+        + [VMEM] * len(flat)
+        + [pl.BlockSpec(memory_space=pl.ANY)] * len(after),
+        out_specs=[VMEM] * len(plan),
+        out_shape=[jax.ShapeDtypeStruct(shape, jnp.bfloat16)] * len(plan),
         compiler_params=pltpu.CompilerParams(vmem_limit_bytes=24 * 1024 * 1024),
         cost_estimate=pl.CostEstimate(
             flops=len(plan) * 40_000_000, bytes_accessed=len(plan) * 1_500_000, transcendentals=0
         ),
         name="cross",
-    )(flag.reshape(1), *flat)
+    )(flag.reshape(1), *flat, *after)
 
 
 COLUMNS = 256
@@ -239,15 +270,20 @@
 
 def series_kernel(table_ref, *refs):
     chunks = len(CHUNKS)
-    sources = refs[: 3 * chunks]
-    cycle_ref, region_ref, wide_ref, rows_ref = refs[3 * chunks :]
-
-    @pl.when(pl.program_id(0) == 0)
+    sources = refs[: (STEPS + 1) * chunks]
+    cycle_ref, region_ref, wide_ref, rows_ref, held_ref, sems = refs[(STEPS + 1) * chunks :]
+    step = pl.program_id(0)
+
+    def fetch(n):
+        return pltpu.make_async_copy(table_ref.at[n], held_ref.at[n], sems.at[n])
+
+    @pl.when(step == 0)
     def _():
+        for n in range(LAGS // COLUMNS):
+            fetch(n).start()
         for k in range(STEPS + 1):
             for chunk in range(chunks):
-                source = sources[(k // 2) * chunks + chunk]
-                first = (k % 2) * SB * SB
+                source = sources[k * chunks + chunk]
                 for i in range(SB):
                     for j in range(SB):
                         for n, (c, d) in enumerate(pairs_of(chunk)):
@@ -256,14 +292,15 @@
                             else:
                                 row = CYCLE_ROWS + (i * 9 + 3 * c + d) * SB + j
                             wide_ref[row * TILE : (row + 1) * TILE, :] = source[
-                                first + i * SB + j, n
+                                i * SB + j, n
                             ].astype(jnp.float32)
         for piece in range(TILE):
             rows_ref[:, piece * LANES : (piece + 1) * LANES] = wide_ref[
                 pl.ds(piece, ALL_ROWS, stride=TILE), :
             ].astype(jnp.bfloat16)
 
-    series = jnp.dot(rows_ref[...], table_ref[...], preferred_element_type=jnp.float32)
+    fetch(step).wait()
+    series = jnp.dot(rows_ref[...], held_ref[step], preferred_element_type=jnp.float32)
     series = (series * (1.0 / math.sqrt(F * SEGS))).astype(jnp.bfloat16)
     for i in range(SB):
         for k in range(STEPS):
@@ -279,7 +316,7 @@
     return pl.pallas_call(
         series_kernel,
         grid=(LAGS // COLUMNS,),
-        in_specs=[pl.BlockSpec((2 * F, COLUMNS), lambda n: (0, n))] + [VMEM] * len(sources),
+        in_specs=[pl.BlockSpec(memory_space=pl.ANY)] + [VMEM] * len(sources),
         out_specs=[
             pl.BlockSpec((SB, STEPS, 9, SB, COLUMNS), lambda n: (0, 0, 0, 0, n)),
             pl.BlockSpec((SB, 9, SB, COLUMNS), lambda n: (0, 0, 0, n)),
@@ -291,13 +328,15 @@
         scratch_shapes=[
             pltpu.VMEM((ALL_ROWS * TILE, LANES), jnp.float32),
             pltpu.VMEM((ALL_ROWS, 2 * F), jnp.bfloat16),
+            pltpu.VMEM((LAGS // COLUMNS, 2 * F, COLUMNS), jnp.bfloat16),
+            pltpu.SemaphoreType.DMA((LAGS // COLUMNS,)),
         ],
         compiler_params=pltpu.CompilerParams(vmem_limit_bytes=32 * 1024 * 1024),
         cost_estimate=pl.CostEstimate(
             flops=2 * ALL_ROWS * 2 * F * LAGS, bytes_accessed=12_000_000, transcendentals=0
         ),
         name="lag_series",
-    )(table, *sources)
+    )(pltpu.with_memory_space_constraint(table, pltpu.HBM), *sources)
 
 
 def table_kernel(fine_ref, coarse_ref, out_ref):
@@ -309,13 +348,13 @@
 
         @pl.when(step == 0)
         def _(high=high):
-            out_ref[high * LANES : (high + 1) * LANES, :] = (
+            out_ref[0, high * LANES : (high + 1) * LANES, :] = (
                 cos_low * cos_high - sin_low * sin_high
             ).astype(jnp.bfloat16)
 
         @pl.when(step == 1)
         def _(high=high):
-            out_ref[high * LANES : (high + 1) * LANES, :] = (
+            out_ref[0, high * LANES : (high + 1) * LANES, :] = (
                 -(sin_low * cos_high + cos_low * sin_high)
             ).astype(jnp.bfloat16)
 
@@ -330,16 +369,15 @@
 
     fine = angles(jnp.arange(LANES, dtype=jnp.int32))
     coarse = angles(LANES * jnp.arange(FH, dtype=jnp.int32))
-    width = 512
     return pl.pallas_call(
         table_kernel,
-        grid=(2, LAGS // width),
+        grid=(2, LAGS // COLUMNS),
         in_specs=[
-            pl.BlockSpec((2, LANES, width), lambda s, n: (0, 0, n)),
-            pl.BlockSpec((2, FH, width), lambda s, n: (0, 0, n)),
-        ],
-        out_specs=pl.BlockSpec((F, width), lambda s, n: (s, n)),
-        out_shape=pltpu.HBM((2 * F, LAGS), jnp.bfloat16),
+            pl.BlockSpec((2, LANES, COLUMNS), lambda s, n: (0, 0, n)),
+            pl.BlockSpec((2, FH, COLUMNS), lambda s, n: (0, 0, n)),
+        ],
+        out_specs=pl.BlockSpec((1, F, COLUMNS), lambda s, n: (n, s, 0)),
+        out_shape=pltpu.HBM((LAGS // COLUMNS, 2 * F, COLUMNS), jnp.bfloat16),
         compiler_params=pltpu.CompilerParams(vmem_limit_bytes=16 * 1024 * 1024),
         cost_estimate=pl.CostEstimate(flops=16_000_000, bytes_accessed=12_000_000, transcendentals=0),
         name="lag_table",
@@ -351,13 +389,20 @@
     return lax.ppermute(block, axis, [(i, (i + by) % size) for i in range(size)])
 
 
+def swapped(block):
+    return lax.ppermute(block, "blk", [(i, i ^ 1) for i in range(lax.axis_size("blk"))])
+
+
 def spread(block, planes):
-    regions = lax.axis_size("region")
-    groups = [list(range(n, n + planes)) for n in range(0, regions, planes)]
-    parts = lax.all_to_all(
-        block, "region", split_axis=0, concat_axis=0, tiled=True, axis_index_groups=groups
-    )
-    return parts[(planes - 1) * PIECE :]
+    starts = range(0, lax.axis_size("region"), planes)
+    return [
+        lax.ppermute(
+            block[plane * PIECE : (plane + 1) * PIECE],
+            "region",
+            [(n + planes - 1, n + plane) for n in starts],
+        )
+        for plane in range(planes - 1)
+    ]
 
 
 def from_previous_region(block, piece, planes):
@@ -409,27 +454,32 @@
     place = jnp.clip(place, 0, 2 * blocks - 1)
 
     planes = 4
-    edge = (lax.axis_index("region") % planes == 0).astype(jnp.int32)
-    own, one, two, ahead, near, far = [], [], [], [], [], []
-    lower, upper, across = [], [], []
+    plane = lax.axis_index("region") % planes
+    edge = (plane == 0).astype(jnp.int32)
+    core = lax.axis_index("blk") & 1
+    own, twin, two, four, near, far = [], [], [], [], [], []
+    results = [[] for _ in range(STEPS + 1)]
     for chunk, part in enumerate(CHUNKS):
-        rows = len(part) * TILE
-        early = sort_units(place, got[chunk], rows)
-        piece = spread(early, planes)
-        closer, further = from_previous_region(early, piece, planes)
-        block = sort_units(place, got[chunk], rows, piece)
+        early = sort_units(place, got[chunk], len(part) * TILE)
+        piece, block = choose(plane, early, spread(early, planes))
+        closer, further = from_previous_region(block, piece, planes)
         own.append([block])
-        one.append([shifted(block, "blk", 1)])
+        four.append([shifted(block, "blk", 4)])
         two.append([shifted(block, "blk", 2)])
-        ahead.append([shifted(block, "blk", -2)])
+        twin.append([swapped(block)])
         near.append([closer])
         far.append(further)
-        lower.append(cross(chunk, ((0, 1, 1), (0, 2, 2)), edge, own, one, two))
-        later = cross(chunk, ((0, 1, 1), (0, 2, 2)), edge, ahead, one, two)
-        upper.append(shifted(later, "blk", 2))
-        across.append(cross(chunk, ((0, 1, 2),), edge, own, near, far))
-
-    cycle_series, region_series = lag_series(table, lower + upper + across)
+        by_two, for_one = cross(chunk, ((0, 2, 2), (1, 0, 2)), core, (own, twin, two))
+        (for_three,) = cross(
+            chunk, ((0, 1, 2),), core, (twin, two, four), (for_one,)
+        )
+        (by_four,) = cross(chunk, ((0, 1, 1),), core, (own, four), (for_three,))
+        (by_region,) = cross(chunk, ((0, 1, 2),), edge, (own, near, far), (by_four,))
+        every = (swapped(for_one), by_two, swapped(for_three), by_four, by_region)
+        for k, result in enumerate(every):
+            results[k].append(result)
+
+    cycle_series, region_series = lag_series(table, [r for result in results for r in result])
     return jnp.swapaxes(cycle_series, 2, 3), jnp.swapaxes(region_series, 1, 2)
 
 

time: 214 us -> 225 us (1.051)
  the two profiles are of different devices: /device:TPU:57 before, /device:TPU:29 now
where the time goes in v3:
time: 225 us; the launch traced here: 224 us
  waiting for transfers between devices  134 us (60%)
  starting transfers between devices  47.1 us (21%)
  Pallas kernels  31.2 us (14%)
  other arithmetic  5.74 us (3%)
  local copies, waits for them, and re-layouts  4.07 us (2%)
    all_to_all x1, waiting for transfers between devices, body(): lax.all_to_all(part, 'blk', split_axis=0, concat_axis=0, tiled=True)  64.6 us
    ppermute x1, waiting for transfers between devices, from_previous_region(): lax.ppermute(piece, 'region', [(i, (i + planes) % regions) for i in range...  59.8 us
    all_to_all x1, starting transfers between devices, body(): lax.all_to_all(part, 'blk', split_axis=0, concat_axis=0, tiled=True)  16.3 us
    pallas_call x4, Pallas kernels, cross(): pl.pallas_call(functools.partial(cross_kernel, chunk, plan, tuple((len(bl...  10.9 us
    ppermute x3, waiting for transfers between devices, spread(): lax.ppermute(block[plane * PIECE:(plane + 1) * PIECE], 'region', [(n + pl...  9.9 us
    pallas_call x1, Pallas kernels, make_table(): pl.pallas_call(table_kernel, grid=(2, LAGS // COLUMNS), in_specs=[pl.Bloc...  9.34 us
    ppermute x3, starting transfers between devices, swapped(): lax.ppermute(block, 'blk', [(i, i ^ 1) for i in range(lax.axis_size('blk'...  8.7 us
    ppermute x1, starting transfers between devices, from_previous_region(): lax.ppermute(piece, 'region', [(i, (i + planes) % regions) for i in range...  7.94 us
  transfers between devices with their start and end apart: 14, of which 3 were waited for; matrix products, arithmetic and copies ran while one was open for 2% of the time, Pallas kernels for 9%

profile of v3, /device:TPU:29, one launch (start us, length us, event | category | flops | bytes accessed | tf_op | source)
XLA Modules:
  0.0 224.1 jit_solution(16049177064278442720)
XLA Ops:
  2.4 1.9 copy.11
  5.5 4.5 %whiten.1 = bf16[64,104,128]{2,1,0:T(8,128)(2,1)} custom-call(s32[128]{0:T(128)S(1)} %min.27.source_ref, bf16[256,128]{1,0:T(8,128)(2,1)S(1)} %add_convert_fusion.band_ref, f32[8,128]{1,0:T(8,128)S(1)} %convert_divide_fusion.inverse_ref, bf16[128,48,128]{2,1,0:T(8,128)(2,1)S(1)} %copy.12.archive_ref, bf16[64,8,128]{2,1,0:T(8,128)(2,1)S(1)} %broadcast_in_dim.91.mark_ref), custom_call_target="tpu_custom_call" | custom-call | flops 200000000 | bytes 4000000 | tf_op jit(solution)/shard_map/whiten/pallas_call | solution.py:115
  9.9 16.3 %all-to-all-start = ((bf16[64,104,128]{2,1,0:T(8,128)(2,1)}), bf16[64,104,128]{2,1,0:T(8,128)(2,1)S(1)}, u32[]{:S(2)}, u32[]{:S(2)}) async-start(bf16[64,104,128]{2,1,0:T(8,128)(2,1)} %whiten.1), calls=%async_computation | async-start | bytes 3407872 | tf_op jit(solution)/shard_map/all_to_all | solution.py:442
  26.6 4.1 %fusion.7 = (f32[1,128,2048]{2,1,0:T(8,128)S(1)}, f32[1,128,2048]{2,1,0:T(8,128)S(1)}) fusion(s32[2048]{0:T(1024)S(1)} %iota_add_fusion), kind=kLoop, calls=%fused_computation.11 | loop fusion | flops 3670016 | bytes 2105344 | tf_op jit(solution)/shard_map/cos | solution.py:368
  30.9 9.3 %lag_table.1.table_ref = bf16[8,2048,256]{2,1,0:T(8,128)(2,1)} custom-call(f32[2,128,2048]{2,1,0:T(8,128)S(1)} %pad_maximum_fusion.fine_ref, f32[2,8,2048]{2,1,0:T(8,128)S(1)} %pad_maximum_fusion.1.coarse_ref), custom_call_target="tpu_custom_call" | custom-call | flops 16000000 | bytes 12000000 | tf_op jit(solution)/shard_map/lag_table/pallas_call | solution.py:372
  40.2 64.6 %all-to-all-done.got_ref = bf16[64,104,128]{2,1,0:T(8,128)(2,1)S(1)} async-done(((bf16[64,104,128]{2,1,0:T(8,128)(2,1)}), bf16[64,104,128]{2,1,0:T(8,128)(2,1)S(1)}, u32[]{:S(2)}, u32[]{:S(2)}) %all-to-all-start) | async-done | bytes 1703968 | tf_op jit(solution)/shard_map/all_to_all | solution.py:442
  107.3 1.3 collective-permute-start.2
  108.6 9.9 %collective-permute-done.2.refs_2_ = bf16[16,48,128]{2,1,0:T(8,128)(2,1)S(1)} collective-permute-done((bf16[16,48,128]{2,1,0:T(8,128)(2,1)S(1)}, bf16[16,48,128]{2,1,0:T(8,128)(2,1)S(1)}, u32[]{:S(2)}, u32[]{:S(2)}) %collective-permute-start.2) | collective-permute-done | bytes 196640 | tf_op jit(solution)/shard_map/ppermute | solution.py:399
  118.6 4.0 %collective-permute-start.3 = (bf16[64,48,128]{2,1,0:T(8,128)(2,1)S(1)}, bf16[64,48,128]{2,1,0:T(8,128)(2,1)S(1)}, u32[]{:S(2)}, u32[]{:S(2)}) collective-permute-start(bf16[64,48,128]{2,1,0:T(8,128)(2,1)S(1)} %get-tuple-element.12.refs_0_), channel_id=1, source_target_pairs={{0,1},{1,0},{2,3},{3,2},{4,5},{5,4},{6,7},{7,6},{8,9},{9,8},{10,11... | collective-permute-start | bytes 2359304 | tf_op jit(solution)/shard_map/ppermute | solution.py:393
  122.6 1.9 collective-permute-start.4
  124.5 3.1 %collective-permute-start.6 = (bf16[64,48,128]{2,1,0:T(8,128)(2,1)S(1)}, bf16[64,48,128]{2,1,0:T(8,128)(2,1)S(1)}, u32[]{:S(2)}, u32[]{:S(2)}) collective-permute-start(bf16[64,48,128]{2,1,0:T(8,128)(2,1)S(1)} %get-tuple-element.12.refs_0_), channel_id=1, source_target_pairs={{0,4},{1,5},{2,6},{3,7},{4,8},{5,9},{6,10},{7,11},{8,12},{9,13},{1... | collective-permute-start | bytes 2359304 | tf_op jit(solution)/shard_map/ppermute | solution.py:389
  127.6 1.9 collective-permute-start.8
  129.6 7.9 %collective-permute-start.9 = (bf16[16,48,128]{2,1,0:T(8,128)(2,1)S(1)}, bf16[16,48,128]{2,1,0:T(8,128)(2,1)S(1)}, u32[]{:S(2)}, u32[]{:S(2)}) collective-permute-start(bf16[16,48,128]{2,1,0:T(8,128)(2,1)S(1)} %get-tuple-element.15), channel_id=1, source_target_pairs={{0,256},{64,320},{128,384},{192,448},{256,0},{320,64},{384,128},{4... | collective-permute-start | bytes 589832 | tf_op jit(solution)/shard_map/ppermute | solution.py:413
  137.5 59.8 %collective-permute-done.9.refs_2_ = bf16[16,48,128]{2,1,0:T(8,128)(2,1)S(1)} collective-permute-done((bf16[16,48,128]{2,1,0:T(8,128)(2,1)S(1)}, bf16[16,48,128]{2,1,0:T(8,128)(2,1)S(1)}, u32[]{:S(2)}, u32[]{:S(2)}) %collective-permute-start.9) | collective-permute-done | bytes 196640 | tf_op jit(solution)/shard_map/ppermute | solution.py:413
  197.3 1.3 collective-permute-start.10
  198.7 2.0 collective-permute-start.11
  200.6 1.3 collective-permute-start.12
  202.0 4.2 %cross.4 = (bf16[4,9,16,128]{3,2,1,0:T(8,128)(2,1)S(1)}, bf16[4,9,16,128]{3,2,1,0:T(8,128)(2,1)}) custom-call(s32[1]{0:T(128)} %bitcast.4.flag_ref, bf16[64,48,128]{2,1,0:T(8,128)(2,1)S(1)} %get-tuple-element.12.refs_0_, bf16[64,48,128]{2,1,0:T(8,128)(2,1)S(1)} %collective-permute-done.3.refs_1_.refs_0_, ...), custom_call_target="tpu_custom_call" | custom-call | flops 80000000 | bytes 3000000 | tf_op jit(solution)/shard_map/cross/pallas_call | solution.py:251
  206.8 1.8 cross.5.refs_2_
  208.6 2.8 %collective-permute-start.7 = (bf16[4,9,16,128]{3,2,1,0:T(8,128)(2,1)S(1)}, bf16[4,9,16,128]{3,2,1,0:T(8,128)(2,1)S(1)}, u32[]{:S(2)}, u32[]{:S(2)}) collective-permute-start(bf16[4,9,16,128]{3,2,1,0:T(8,128)(2,1)S(1)} %cross.5.refs_2_), channel_id=1, source_target_pairs={{0,1},{1,0},{2,3},{3,2},{4,5},{5,4},{6,7},{7,6},{8,9},{9,8},{10,11... | collective-permute-start | bytes 442376 | tf_op jit(solution)/shard_map/ppermute | solution.py:393
  211.4 1.9 collective-permute-start.5
  213.3 1.8 cross.6.refs_6_.refs_3_
  215.1 3.1 %cross.7.refs_4_ = bf16[4,9,16,128]{3,2,1,0:T(8,128)(2,1)S(1)} custom-call(s32[1]{0:T(128)} %bitcast.7.flag_ref, bf16[64,48,128]{2,1,0:T(8,128)(2,1)S(1)} %get-tuple-element.12.refs_0_, bf16[64,48,128]{2,1,0:T(8,128)(2,1)} %collective-permute-done.8.refs_1_, bf16[16,48,128]{2,1,0:T(8,128)(2,1)S(1)} %collective-permute-done.9.refs_2_, ...), custom_call_target="tpu_custom_call" | custom-call | flops 40000000 | bytes 1500000 | tf_op jit(solution)/shard_map/cross/pallas_call | solution.py:251
  218.3 5.8 %lag_series.1 = (bf16[2,4,9,2,2048]{4,3,2,1,0:T(2,128)(2,1)}, bf16[2,9,2,2048]{3,2,1,0:T(2,128)(2,1)}) custom-call(bf16[8,2048,256]{2,1,0:T(8,128)(2,1)} %lag_table.1.table_ref, bf16[4,9,16,128]{3,2,1,0:T(8,128)(2,1)S(1)} %collective-permute-done.5.refs_0_, bf16[4,9,16,128]{3,2,1,0:T(8,128)(2,1)S(1)} %copy-done.1, ...), custom_call_target="tpu_custom_call" | custom-call | flops 1509949440 | bytes 12000000 | tf_op jit(solution)/shard_map/lag_series/pallas_call | solution.py:316
  (43 shorter events, 6.0 us)
Async XLA Ops:
  9.9 94.8 %all-to-all-start = ((bf16[64,104,128]{2,1,0:T(8,128)(2,1)}), bf16[64,104,128]{2,1,0:T(8,128)(2,1)S(1)}, u32[]{:S(2)}, u32[]{:S(2)}) async-start(bf16[64,104,128]{2,1,0:T(8,128)(2,1)} %whiten.1), calls=%async_computation | async-start | bytes 3407872 | tf_op jit(solution)/shard_map/all_to_all | solution.py:442
  105.9 2.7 %collective-permute-start = (bf16[16,48,128]{2,1,0:T(8,128)(2,1)S(1)}, bf16[16,48,128]{2,1,0:T(8,128)(2,1)S(1)}, u32[]{:S(2)}, u32[]{:S(2)}) collective-permute-start(bf16[16,48,128]{2,1,0:T(8,128)(2,1)S(1)} %get-tuple-element.24), channel_id=1, source_target_pairs={{192,0},{448,256},{193,1},{449,257},{194,2},{450,258},{195,3},{451... | collective-permute-start | bytes 589832 | tf_op jit(solution)/shard_map/ppermute | solution.py:399
  106.6 2.0 collective-permute-start.1
  107.3 11.2 %collective-permute-start.2 = (bf16[16,48,128]{2,1,0:T(8,128)(2,1)S(1)}, bf16[16,48,128]{2,1,0:T(8,128)(2,1)S(1)}, u32[]{:S(2)}, u32[]{:S(2)}) collective-permute-start(bf16[16,48,128]{2,1,0:T(8,128)(2,1)S(1)} %get-tuple-element.22), channel_id=1, source_target_pairs={{192,128},{448,384},{193,129},{449,385},{194,130},{450,386},{195,1... | collective-permute-start | bytes 589832 | tf_op jit(solution)/shard_map/ppermute | solution.py:399
  118.6 80.0 %collective-permute-start.3 = (bf16[64,48,128]{2,1,0:T(8,128)(2,1)S(1)}, bf16[64,48,128]{2,1,0:T(8,128)(2,1)S(1)}, u32[]{:S(2)}, u32[]{:S(2)}) collective-permute-start(bf16[64,48,128]{2,1,0:T(8,128)(2,1)S(1)} %get-tuple-element.12.refs_0_), channel_id=1, source_target_pairs={{0,1},{1,0},{2,3},{3,2},{4,5},{5,4},{6,7},{7,6},{8,9},{9,8},{10,11... | collective-permute-start | bytes 2359304 | tf_op jit(solution)/shard_map/ppermute | solution.py:393
  122.6 78.0 %collective-permute-start.4 = (bf16[64,48,128]{2,1,0:T(8,128)(2,1)S(1)}, bf16[64,48,128]{2,1,0:T(8,128)(2,1)S(1)}, u32[]{:S(2)}, u32[]{:S(2)}) collective-permute-start(bf16[64,48,128]{2,1,0:T(8,128)(2,1)S(1)} %get-tuple-element.12.refs_0_), channel_id=1, source_target_pairs={{0,2},{1,3},{2,4},{3,5},{4,6},{5,7},{6,8},{7,9},{8,10},{9,11},{10,... | collective-permute-start | bytes 2359304 | tf_op jit(solution)/shard_map/ppermute | solution.py:389
  124.5 82.3 %collective-permute-start.6 = (bf16[64,48,128]{2,1,0:T(8,128)(2,1)S(1)}, bf16[64,48,128]{2,1,0:T(8,128)(2,1)S(1)}, u32[]{:S(2)}, u32[]{:S(2)}) collective-permute-start(bf16[64,48,128]{2,1,0:T(8,128)(2,1)S(1)} %get-tuple-element.12.refs_0_), channel_id=1, source_target_pairs={{0,4},{1,5},{2,6},{3,7},{4,8},{5,9},{6,10},{7,11},{8,12},{9,13},{1... | collective-permute-start | bytes 2359304 | tf_op jit(solution)/shard_map/ppermute | solution.py:389
  127.6 87.5 %collective-permute-start.8 = (bf16[64,48,128]{2,1,0:T(8,128)(2,1)S(1)}, bf16[64,48,128]{2,1,0:T(8,128)(2,1)}, u32[]{:S(2)}, u32[]{:S(2)}) collective-permute-start(bf16[64,48,128]{2,1,0:T(8,128)(2,1)S(1)} %get-tuple-element.12.refs_0_), channel_id=1, source_target_pairs={{0,64},{64,128},{128,192},{256,320},{320,384},{384,448},{1,65},{65... | collective-permute-start | bytes 2359304 | tf_op jit(solution)/shard_map/ppermute | solution.py:410
  129.6 67.8 %collective-permute-start.9 = (bf16[16,48,128]{2,1,0:T(8,128)(2,1)S(1)}, bf16[16,48,128]{2,1,0:T(8,128)(2,1)S(1)}, u32[]{:S(2)}, u32[]{:S(2)}) collective-permute-start(bf16[16,48,128]{2,1,0:T(8,128)(2,1)S(1)} %get-tuple-element.15), channel_id=1, source_target_pairs={{0,256},{64,320},{128,384},{192,448},{256,0},{320,64},{384,128},{4... | collective-permute-start | bytes 589832 | tf_op jit(solution)/shard_map/ppermute | solution.py:413
  197.3 14.1 %collective-permute-start.10 = (bf16[16,48,128]{2,1,0:T(8,128)(2,1)S(1)}, bf16[16,48,128]{2,1,0:T(8,128)(2,1)}, u32[]{:S(2)}, u32[]{:S(2)}) collective-permute-start(bf16[16,48,128]{2,1,0:T(8,128)(2,1)S(1)} %collective-permute-done.9.refs_2_), channel_id=1, source_target_pairs={{64,0},{320,256},{65,1},{321,257},{66,2},{322,258},{67,3},{323,259... | collective-permute-start | bytes 589832 | tf_op jit(solution)/shard_map/ppermute | solution.py:417
  198.7 16.5 %collective-permute-start.11 = (bf16[16,48,128]{2,1,0:T(8,128)(2,1)S(1)}, bf16[16,48,128]{2,1,0:T(8,128)(2,1)}, u32[]{:S(2)}, u32[]{:S(2)}) collective-permute-start(bf16[16,48,128]{2,1,0:T(8,128)(2,1)S(1)} %collective-permute-done.9.refs_2_), channel_id=1, source_target_pairs={{128,0},{384,256},{129,1},{385,257},{130,2},{386,258},{131,3},{387... | collective-permute-start | bytes 589832 | tf_op jit(solution)/shard_map/ppermute | solution.py:417
  200.6 14.5 %collective-permute-start.12 = (bf16[16,48,128]{2,1,0:T(8,128)(2,1)S(1)}, bf16[16,48,128]{2,1,0:T(8,128)(2,1)}, u32[]{:S(2)}, u32[]{:S(2)}) collective-permute-start(bf16[16,48,128]{2,1,0:T(8,128)(2,1)S(1)} %collective-permute-done.9.refs_2_), channel_id=1, source_target_pairs={{192,0},{448,256},{193,1},{449,257},{194,2},{450,258},{195,3},{451... | collective-permute-start | bytes 589832 | tf_op jit(solution)/shard_map/ppermute | solution.py:417
  206.2 0.7 copy-start
  208.6 9.7 %collective-permute-start.7 = (bf16[4,9,16,128]{3,2,1,0:T(8,128)(2,1)S(1)}, bf16[4,9,16,128]{3,2,1,0:T(8,128)(2,1)S(1)}, u32[]{:S(2)}, u32[]{:S(2)}) collective-permute-start(bf16[4,9,16,128]{3,2,1,0:T(8,128)(2,1)S(1)} %cross.5.refs_2_), channel_id=1, source_target_pairs={{0,1},{1,0},{2,3},{3,2},{4,5},{5,4},{6,7},{7,6},{8,9},{9,8},{10,11... | collective-permute-start | bytes 442376 | tf_op jit(solution)/shard_map/ppermute | solution.py:393
  211.4 6.9 %collective-permute-start.5 = (bf16[4,9,16,128]{3,2,1,0:T(8,128)(2,1)}, bf16[4,9,16,128]{3,2,1,0:T(8,128)(2,1)S(1)}, u32[]{:S(2)}, u32[]{:S(2)}) collective-permute-start(bf16[4,9,16,128]{3,2,1,0:T(8,128)(2,1)} %get-tuple-element.13.refs_3_), channel_id=1, source_target_pairs={{0,1},{1,0},{2,3},{3,2},{4,5},{5,4},{6,7},{7,6},{8,9},{9,8},{10,11... | collective-permute-start | bytes 442376 | tf_op jit(solution)/shard_map/ppermute | solution.py:393
  215.1 3.2 %copy-start.1 = (bf16[4,9,16,128]{3,2,1,0:T(8,128)(2,1)S(1)}, bf16[4,9,16,128]{3,2,1,0:T(8,128)(2,1)}, u32[]{:S(2)}) copy-start(bf16[4,9,16,128]{3,2,1,0:T(8,128)(2,1)} %copy-done) | copy-start | bytes 442372

commit v4 on v3

--- a/solution.py
+++ b/solution.py
@@ -182,6 +182,22 @@
         cost_estimate=pl.CostEstimate(flops=0, bytes_accessed=2_000_000, transcendentals=0),
         name="choose_piece",
     )(plane.reshape(1), block, *pieces)
+
+
+def relay_kernel(piece_ref, *refs):
+    refs[-1][...] = piece_ref[...]
+
+
+def relay(piece, *after):
+    return pl.pallas_call(
+        relay_kernel,
+        in_specs=[VMEM] + [pl.BlockSpec(memory_space=pl.ANY)] * len(after),
+        out_specs=VMEM,
+        out_shape=jax.ShapeDtypeStruct(piece.shape, jnp.bfloat16),
+        compiler_params=pltpu.CompilerParams(vmem_limit_bytes=8 * 1024 * 1024),
+        cost_estimate=pl.CostEstimate(flops=20_000_000_000, bytes_accessed=400_000, transcendentals=0),
+        name="relay_piece",
+    )(piece, *after)
 
 
 def products(left_block, right_block, chunk, store):
@@ -405,13 +421,14 @@
     ]
 
 
-def from_previous_region(block, piece, planes):
+def from_previous_region(block, piece, planes, *after):
     regions = lax.axis_size("region")
     near = lax.ppermute(
         block, "region", [(i, i + 1) for i in range(regions) if (i + 1) % planes]
     )
     piece = lax.ppermute(piece, "region", [(i, (i + planes) % regions) for i in range(regions)])
     far = [piece]
+    piece = relay(piece, near, *after)
     for plane in range(1, planes):
         far.append(
             lax.ppermute(piece, "region", [(n + plane, n) for n in range(0, regions, planes)])
@@ -462,19 +479,19 @@
     for chunk, part in enumerate(CHUNKS):
         early = sort_units(place, got[chunk], len(part) * TILE)
         piece, block = choose(plane, early, spread(early, planes))
-        closer, further = from_previous_region(block, piece, planes)
+        twin.append([swapped(block)])
+        closer, further = from_previous_region(block, piece, planes, twin[chunk][0])
         own.append([block])
         four.append([shifted(block, "blk", 4)])
         two.append([shifted(block, "blk", 2)])
-        twin.append([swapped(block)])
         near.append([closer])
         far.append(further)
-        by_two, for_one = cross(chunk, ((0, 2, 2), (1, 0, 2)), core, (own, twin, two))
-        (for_three,) = cross(
-            chunk, ((0, 1, 2),), core, (twin, two, four), (for_one,)
+        (by_region,) = cross(chunk, ((0, 1, 2),), edge, (own, near, far))
+        by_two, for_one = cross(
+            chunk, ((0, 2, 2), (1, 0, 2)), core, (own, twin, two), (by_region,)
         )
+        (for_three,) = cross(chunk, ((0, 1, 2),), core, (twin, two, four), (for_one,))
         (by_four,) = cross(chunk, ((0, 1, 1),), core, (own, four), (for_three,))
-        (by_region,) = cross(chunk, ((0, 1, 2),), edge, (own, near, far), (by_four,))
         every = (swapped(for_one), by_two, swapped(for_three), by_four, by_region)
         for k, result in enumerate(every):
             results[k].append(result)

time: 225 us -> 218 us (0.969)
  the two profiles are of different devices: /device:TPU:29 before, /device:TPU:11 now
where the time goes in v4:
time: 218 us; the launch traced here: 217 us
  waiting for transfers between devices  122 us (56%)
  starting transfers between devices  51.9 us (24%)
  Pallas kernels  31 us (14%)
  other arithmetic  5.74 us (3%)
  local copies, waits for them, and re-layouts  4.85 us (2%)
    all_to_all x1, waiting for transfers between devices, body(): lax.all_to_all(part, 'blk', split_axis=0, concat_axis=0, tiled=True)  64.7 us
    ppermute x2, waiting for transfers between devices, shifted(): lax.ppermute(block, axis, [(i, (i + by) % size) for i in range(size)])  37.9 us
    all_to_all x1, starting transfers between devices, body(): lax.all_to_all(part, 'blk', split_axis=0, concat_axis=0, tiled=True)  16.5 us
    ppermute x1, waiting for transfers between devices, from_previous_region(): lax.ppermute(piece, 'region', [(i, (i + planes) % regions) for i in range...  11.4 us
    ppermute x3, starting transfers between devices, swapped(): lax.ppermute(block, 'blk', [(i, i ^ 1) for i in range(lax.axis_size('blk'...  10.5 us
    pallas_call x4, Pallas kernels, cross(): pl.pallas_call(functools.partial(cross_kernel, chunk, plan, tuple((len(bl...  9.87 us
    pallas_call x1, Pallas kernels, make_table(): pl.pallas_call(table_kernel, grid=(2, LAGS // COLUMNS), in_specs=[pl.Bloc...  9.34 us
    ppermute x1, starting transfers between devices, from_previous_region(): lax.ppermute(piece, 'region', [(i, (i + planes) % regions) for i in range...  7.94 us
  transfers between devices with their start and end apart: 14, of which 5 were waited for; matrix products, arithmetic and copies ran while one was open for 2% of the time, Pallas kernels for 8%

profile of v4, /device:TPU:11, one launch (start us, length us, event | category | flops | bytes accessed | tf_op | source)
XLA Modules:
  0.0 217.2 jit_solution(17366817618559547647)
XLA Ops:
  2.4 1.9 copy.11
  5.5 4.5 %whiten.1 = bf16[64,104,128]{2,1,0:T(8,128)(2,1)} custom-call(s32[128]{0:T(128)S(1)} %min.27.source_ref, bf16[256,128]{1,0:T(8,128)(2,1)S(1)} %add_convert_fusion.band_ref, f32[8,128]{1,0:T(8,128)S(1)} %convert_divide_fusion.inverse_ref, bf16[128,48,128]{2,1,0:T(8,128)(2,1)S(1)} %copy.12.archive_ref, bf16[64,8,128]{2,1,0:T(8,128)(2,1)S(1)} %broadcast_in_dim.91.mark_ref), custom_call_target="tpu_custom_call" | custom-call | flops 200000000 | bytes 4000000 | tf_op jit(solution)/shard_map/whiten/pallas_call | solution.py:115
  9.9 16.5 %all-to-all-start = ((bf16[64,104,128]{2,1,0:T(8,128)(2,1)}), bf16[64,104,128]{2,1,0:T(8,128)(2,1)S(1)}, u32[]{:S(2)}, u32[]{:S(2)}) async-start(bf16[64,104,128]{2,1,0:T(8,128)(2,1)} %whiten.1), calls=%async_computation | async-start | bytes 3407872 | tf_op jit(solution)/shard_map/all_to_all | solution.py:459
  26.8 4.1 %fusion.7 = (f32[1,128,2048]{2,1,0:T(8,128)S(1)}, f32[1,128,2048]{2,1,0:T(8,128)S(1)}) fusion(s32[2048]{0:T(1024)S(1)} %iota_add_fusion), kind=kLoop, calls=%fused_computation.11 | loop fusion | flops 3670016 | bytes 2105344 | tf_op jit(solution)/shard_map/cos | solution.py:384
  31.1 9.3 %lag_table.1.table_ref = bf16[8,2048,256]{2,1,0:T(8,128)(2,1)} custom-call(f32[2,128,2048]{2,1,0:T(8,128)S(1)} %pad_maximum_fusion.fine_ref, f32[2,8,2048]{2,1,0:T(8,128)S(1)} %pad_maximum_fusion.1.coarse_ref), custom_call_target="tpu_custom_call" | custom-call | flops 16000000 | bytes 12000000 | tf_op jit(solution)/shard_map/lag_table/pallas_call | solution.py:388
  40.4 64.7 %all-to-all-done.got_ref = bf16[64,104,128]{2,1,0:T(8,128)(2,1)S(1)} async-done(((bf16[64,104,128]{2,1,0:T(8,128)(2,1)}), bf16[64,104,128]{2,1,0:T(8,128)(2,1)S(1)}, u32[]{:S(2)}, u32[]{:S(2)}) %all-to-all-start) | async-done | bytes 1703968 | tf_op jit(solution)/shard_map/all_to_all | solution.py:459
  109.0 6.8 %collective-permute-done.1.refs_1_ = bf16[16,48,128]{2,1,0:T(8,128)(2,1)S(1)} collective-permute-done((bf16[16,48,128]{2,1,0:T(8,128)(2,1)S(1)}, bf16[16,48,128]{2,1,0:T(8,128)(2,1)S(1)}, u32[]{:S(2)}, u32[]{:S(2)}) %collective-permute-start.1) | collective-permute-done | bytes 196640 | tf_op jit(solution)/shard_map/ppermute | solution.py:415
  115.8 5.4 %collective-permute-start.3 = (bf16[64,48,128]{2,1,0:T(8,128)(2,1)S(1)}, bf16[64,48,128]{2,1,0:T(8,128)(2,1)S(1)}, u32[]{:S(2)}, u32[]{:S(2)}) collective-permute-start(bf16[64,48,128]{2,1,0:T(8,128)(2,1)S(1)} %get-tuple-element.12.refs_0_), channel_id=1, source_target_pairs={{0,1},{1,0},{2,3},{3,2},{4,5},{5,4},{6,7},{7,6},{8,9},{9,8},{10,11... | collective-permute-start | bytes 2359304 | tf_op jit(solution)/shard_map/ppermute | solution.py:409
  121.2 4.9 %collective-permute-start.5 = (bf16[64,48,128]{2,1,0:T(8,128)(2,1)S(1)}, bf16[64,48,128]{2,1,0:T(8,128)(2,1)S(1)}, u32[]{:S(2)}, u32[]{:S(2)}) collective-permute-start(bf16[64,48,128]{2,1,0:T(8,128)(2,1)S(1)} %get-tuple-element.12.refs_0_), channel_id=1, source_target_pairs={{0,64},{64,128},{128,192},{256,320},{320,384},{384,448},{1,65},{65... | collective-permute-start | bytes 2359304 | tf_op jit(solution)/shard_map/ppermute | solution.py:426
  126.1 7.9 %collective-permute-start.6 = (bf16[16,48,128]{2,1,0:T(8,128)(2,1)S(1)}, bf16[16,48,128]{2,1,0:T(8,128)(2,1)S(1)}, u32[]{:S(2)}, u32[]{:S(2)}) collective-permute-start(bf16[16,48,128]{2,1,0:T(8,128)(2,1)S(1)} %get-tuple-element.13), channel_id=1, source_target_pairs={{0,256},{64,320},{128,384},{192,448},{256,0},{320,64},{384,128},{4... | collective-permute-start | bytes 589832 | tf_op jit(solution)/shard_map/ppermute | solution.py:429
  134.0 3.0 %collective-permute-start.4 = (bf16[64,48,128]{2,1,0:T(8,128)(2,1)S(1)}, bf16[64,48,128]{2,1,0:T(8,128)(2,1)S(1)}, u32[]{:S(2)}, u32[]{:S(2)}) collective-permute-start(bf16[64,48,128]{2,1,0:T(8,128)(2,1)S(1)} %get-tuple-element.12.refs_0_), channel_id=1, source_target_pairs={{0,2},{1,3},{2,4},{3,5},{4,6},{5,7},{6,8},{7,9},{8,10},{9,11},{10,... | collective-permute-start | bytes 2359304 | tf_op jit(solution)/shard_map/ppermute | solution.py:405
  137.0 2.5 %collective-permute-start.11 = (bf16[64,48,128]{2,1,0:T(8,128)(2,1)S(1)}, bf16[64,48,128]{2,1,0:T(8,128)(2,1)S(1)}, u32[]{:S(2)}, u32[]{:S(2)}) collective-permute-start(bf16[64,48,128]{2,1,0:T(8,128)(2,1)S(1)} %get-tuple-element.12.refs_0_), channel_id=1, source_target_pairs={{0,4},{1,5},{2,6},{3,7},{4,8},{5,9},{6,10},{7,11},{8,12},{9,13},{1... | collective-permute-start | bytes 2359304 | tf_op jit(solution)/shard_map/ppermute | solution.py:405
  139.5 11.4 %collective-permute-done.6.piece_ref.refs_2_ = bf16[16,48,128]{2,1,0:T(8,128)(2,1)S(1)} collective-permute-done((bf16[16,48,128]{2,1,0:T(8,128)(2,1)S(1)}, bf16[16,48,128]{2,1,0:T(8,128)(2,1)S(1)}, u32[]{:S(2)}, u32[]{:S(2)}) %collective-permute-start.6) | collective-permute-done | bytes 196640 | tf_op jit(solution)/shard_map/ppermute | solution.py:429
  152.0 1.4 collective-permute-start.7
  153.3 1.3 collective-permute-start.8
  156.0 1.4 collective-permute-done.7.refs_3_
  158.5 2.8 %cross.4.refs_3_.refs_4_ = bf16[4,9,16,128]{3,2,1,0:T(8,128)(2,1)S(1)} custom-call(s32[1]{0:T(128)} %bitcast.7.flag_ref, bf16[64,48,128]{2,1,0:T(8,128)(2,1)S(1)} %get-tuple-element.12.refs_0_, bf16[64,48,128]{2,1,0:T(8,128)(2,1)S(1)} %copy-done.1, bf16[16,48,128]{2,1,0:T(8,128)(2,1)S(1)} %collective-permute-done.6.piece_ref.refs_2_, ...), custom_call_target="tpu_custom_call" | custom-call | flops 40000000 | bytes 1500000 | tf_op jit(solution)/shard_map/cross/pallas_call | solution.py:267
  161.3 3.5 %cross.5 = (bf16[4,9,16,128]{3,2,1,0:T(8,128)(2,1)S(1)}, bf16[4,9,16,128]{3,2,1,0:T(8,128)(2,1)S(1)}) custom-call(s32[1]{0:T(128)} %bitcast.4.flag_ref, bf16[64,48,128]{2,1,0:T(8,128)(2,1)S(1)} %get-tuple-element.12.refs_0_, bf16[64,48,128]{2,1,0:T(8,128)(2,1)S(1)} %collective-permute-done.3.refs_1_.refs_0_, ...), custom_call_target="tpu_custom_call" | custom-call | flops 80000000 | bytes 3000000 | tf_op jit(solution)/shard_map/cross/pallas_call | solution.py:267
  164.9 37.9 %collective-permute-done.11.refs_2_.refs_1_ = bf16[64,48,128]{2,1,0:T(8,128)(2,1)S(1)} collective-permute-done((bf16[64,48,128]{2,1,0:T(8,128)(2,1)S(1)}, bf16[64,48,128]{2,1,0:T(8,128)(2,1)S(1)}, u32[]{:S(2)}, u32[]{:S(2)}) %collective-permute-start.11) | collective-permute-done | bytes 786464 | tf_op jit(solution)/shard_map/ppermute | solution.py:405
  202.8 1.8 cross.6.refs_2_
  204.5 3.2 %collective-permute-start.12 = (bf16[4,9,16,128]{3,2,1,0:T(8,128)(2,1)S(1)}, bf16[4,9,16,128]{3,2,1,0:T(8,128)(2,1)S(1)}, u32[]{:S(2)}, u32[]{:S(2)}) collective-permute-start(bf16[4,9,16,128]{3,2,1,0:T(8,128)(2,1)S(1)} %cross.6.refs_2_), channel_id=1, source_target_pairs={{0,1},{1,0},{2,3},{3,2},{4,5},{5,4},{6,7},{7,6},{8,9},{9,8},{10,11... | collective-permute-start | bytes 442376 | tf_op jit(solution)/shard_map/ppermute | solution.py:409
  207.7 1.9 collective-permute-start.10
  209.6 1.8 cross.7.refs_3_
  211.4 5.8 %lag_series.1 = (bf16[2,4,9,2,2048]{4,3,2,1,0:T(2,128)(2,1)}, bf16[2,9,2,2048]{3,2,1,0:T(2,128)(2,1)}) custom-call(bf16[8,2048,256]{2,1,0:T(8,128)(2,1)} %lag_table.1.table_ref, bf16[4,9,16,128]{3,2,1,0:T(8,128)(2,1)S(1)} %collective-permute-done.10.refs_0_, bf16[4,9,16,128]{3,2,1,0:T(8,128)(2,1)S(1)} %get-tuple-element.15.refs_1_, ...), custom_call_target="tpu_custom_call" | custom-call | flops 1509949440 | bytes 12000000 | tf_op jit(solution)/shard_map/lag_series/pallas_call | solution.py:332
  (44 shorter events, 10.2 us)
Async XLA Ops:
  9.9 95.2 %all-to-all-start = ((bf16[64,104,128]{2,1,0:T(8,128)(2,1)}), bf16[64,104,128]{2,1,0:T(8,128)(2,1)S(1)}, u32[]{:S(2)}, u32[]{:S(2)}) async-start(bf16[64,104,128]{2,1,0:T(8,128)(2,1)} %whiten.1), calls=%async_computation | async-start | bytes 3407872 | tf_op jit(solution)/shard_map/all_to_all | solution.py:459
  106.3 2.7 %collective-permute-start = (bf16[16,48,128]{2,1,0:T(8,128)(2,1)S(1)}, bf16[16,48,128]{2,1,0:T(8,128)(2,1)S(1)}, u32[]{:S(2)}, u32[]{:S(2)}) collective-permute-start(bf16[16,48,128]{2,1,0:T(8,128)(2,1)S(1)} %get-tuple-element.24), channel_id=1, source_target_pairs={{192,0},{448,256},{193,1},{449,257},{194,2},{450,258},{195,3},{451... | collective-permute-start | bytes 589832 | tf_op jit(solution)/shard_map/ppermute | solution.py:415
  107.0 8.8 %collective-permute-start.1 = (bf16[16,48,128]{2,1,0:T(8,128)(2,1)S(1)}, bf16[16,48,128]{2,1,0:T(8,128)(2,1)S(1)}, u32[]{:S(2)}, u32[]{:S(2)}) collective-permute-start(bf16[16,48,128]{2,1,0:T(8,128)(2,1)S(1)} %get-tuple-element.23), channel_id=1, source_target_pairs={{192,64},{448,320},{193,65},{449,321},{194,66},{450,322},{195,67},... | collective-permute-start | bytes 589832 | tf_op jit(solution)/shard_map/ppermute | solution.py:415
  108.3 7.5 %collective-permute-start.2 = (bf16[16,48,128]{2,1,0:T(8,128)(2,1)S(1)}, bf16[16,48,128]{2,1,0:T(8,128)(2,1)S(1)}, u32[]{:S(2)}, u32[]{:S(2)}) collective-permute-start(bf16[16,48,128]{2,1,0:T(8,128)(2,1)S(1)} %get-tuple-element.22), channel_id=1, source_target_pairs={{192,128},{448,384},{193,129},{449,385},{194,130},{450,386},{195,1... | collective-permute-start | bytes 589832 | tf_op jit(solution)/shard_map/ppermute | solution.py:415
  115.8 35.1 %collective-permute-start.3 = (bf16[64,48,128]{2,1,0:T(8,128)(2,1)S(1)}, bf16[64,48,128]{2,1,0:T(8,128)(2,1)S(1)}, u32[]{:S(2)}, u32[]{:S(2)}) collective-permute-start(bf16[64,48,128]{2,1,0:T(8,128)(2,1)S(1)} %get-tuple-element.12.refs_0_), channel_id=1, source_target_pairs={{0,1},{1,0},{2,3},{3,2},{4,5},{5,4},{6,7},{7,6},{8,9},{9,8},{10,11... | collective-permute-start | bytes 2359304 | tf_op jit(solution)/shard_map/ppermute | solution.py:409
  121.2 29.7 %collective-permute-start.5 = (bf16[64,48,128]{2,1,0:T(8,128)(2,1)S(1)}, bf16[64,48,128]{2,1,0:T(8,128)(2,1)S(1)}, u32[]{:S(2)}, u32[]{:S(2)}) collective-permute-start(bf16[64,48,128]{2,1,0:T(8,128)(2,1)S(1)} %get-tuple-element.12.refs_0_), channel_id=1, source_target_pairs={{0,64},{64,128},{128,192},{256,320},{320,384},{384,448},{1,65},{65... | collective-permute-start | bytes 2359304 | tf_op jit(solution)/shard_map/ppermute | solution.py:426
  126.1 24.8 %collective-permute-start.6 = (bf16[16,48,128]{2,1,0:T(8,128)(2,1)S(1)}, bf16[16,48,128]{2,1,0:T(8,128)(2,1)S(1)}, u32[]{:S(2)}, u32[]{:S(2)}) collective-permute-start(bf16[16,48,128]{2,1,0:T(8,128)(2,1)S(1)} %get-tuple-element.13), channel_id=1, source_target_pairs={{0,256},{64,320},{128,384},{192,448},{256,0},{320,64},{384,128},{4... | collective-permute-start | bytes 589832 | tf_op jit(solution)/shard_map/ppermute | solution.py:429
  134.0 27.3 %collective-permute-start.4 = (bf16[64,48,128]{2,1,0:T(8,128)(2,1)S(1)}, bf16[64,48,128]{2,1,0:T(8,128)(2,1)S(1)}, u32[]{:S(2)}, u32[]{:S(2)}) collective-permute-start(bf16[64,48,128]{2,1,0:T(8,128)(2,1)S(1)} %get-tuple-element.12.refs_0_), channel_id=1, source_target_pairs={{0,2},{1,3},{2,4},{3,5},{4,6},{5,7},{6,8},{7,9},{8,10},{9,11},{10,... | collective-permute-start | bytes 2359304 | tf_op jit(solution)/shard_map/ppermute | solution.py:405
  137.0 65.8 %collective-permute-start.11 = (bf16[64,48,128]{2,1,0:T(8,128)(2,1)S(1)}, bf16[64,48,128]{2,1,0:T(8,128)(2,1)S(1)}, u32[]{:S(2)}, u32[]{:S(2)}) collective-permute-start(bf16[64,48,128]{2,1,0:T(8,128)(2,1)S(1)} %get-tuple-element.12.refs_0_), channel_id=1, source_target_pairs={{0,4},{1,5},{2,6},{3,7},{4,8},{5,9},{6,10},{7,11},{8,12},{9,13},{1... | collective-permute-start | bytes 2359304 | tf_op jit(solution)/shard_map/ppermute | solution.py:405
  150.9 1.0 copy-start
  152.0 5.4 %collective-permute-start.7 = (bf16[16,48,128]{2,1,0:T(8,128)(2,1)}, bf16[16,48,128]{2,1,0:T(8,128)(2,1)S(1)}, u32[]{:S(2)}, u32[]{:S(2)}) collective-permute-start(bf16[16,48,128]{2,1,0:T(8,128)(2,1)} %relay_piece.1), channel_id=1, source_target_pairs={{64,0},{320,256},{65,1},{321,257},{66,2},{322,258},{67,3},{323,259... | collective-permute-start | bytes 589832 | tf_op jit(solution)/shard_map/ppermute | solution.py:434
  153.3 4.0 %collective-permute-start.8 = (bf16[16,48,128]{2,1,0:T(8,128)(2,1)}, bf16[16,48,128]{2,1,0:T(8,128)(2,1)}, u32[]{:S(2)}, u32[]{:S(2)}) collective-permute-start(bf16[16,48,128]{2,1,0:T(8,128)(2,1)} %relay_piece.1), channel_id=1, source_target_pairs={{128,0},{384,256},{129,1},{385,257},{130,2},{386,258},{131,3},{387... | collective-permute-start | bytes 589832 | tf_op jit(solution)/shard_map/ppermute | solution.py:434
  154.7 2.7 %collective-permute-start.9 = (bf16[16,48,128]{2,1,0:T(8,128)(2,1)}, bf16[16,48,128]{2,1,0:T(8,128)(2,1)}, u32[]{:S(2)}, u32[]{:S(2)}) collective-permute-start(bf16[16,48,128]{2,1,0:T(8,128)(2,1)} %relay_piece.1), channel_id=1, source_target_pairs={{192,0},{448,256},{193,1},{449,257},{194,2},{450,258},{195,3},{451... | collective-permute-start | bytes 589832 | tf_op jit(solution)/shard_map/ppermute | solution.py:434
  157.4 1.1 copy-start.1
  204.5 6.9 %collective-permute-start.12 = (bf16[4,9,16,128]{3,2,1,0:T(8,128)(2,1)S(1)}, bf16[4,9,16,128]{3,2,1,0:T(8,128)(2,1)S(1)}, u32[]{:S(2)}, u32[]{:S(2)}) collective-permute-start(bf16[4,9,16,128]{3,2,1,0:T(8,128)(2,1)S(1)} %cross.6.refs_2_), channel_id=1, source_target_pairs={{0,1},{1,0},{2,3},{3,2},{4,5},{5,4},{6,7},{7,6},{8,9},{9,8},{10,11... | collective-permute-start | bytes 442376 | tf_op jit(solution)/shard_map/ppermute | solution.py:409
  207.7 3.7 %collective-permute-start.10 = (bf16[4,9,16,128]{3,2,1,0:T(8,128)(2,1)S(1)}, bf16[4,9,16,128]{3,2,1,0:T(8,128)(2,1)S(1)}, u32[]{:S(2)}, u32[]{:S(2)}) collective-permute-start(bf16[4,9,16,128]{3,2,1,0:T(8,128)(2,1)S(1)} %get-tuple-element.14.refs_3_), channel_id=1, source_target_pairs={{0,1},{1,0},{2,3},{3,2},{4,5},{5,4},{6,7},{7,6},{8,9},{9,8},{10,11... | collective-permute-start | bytes 442376 | tf_op jit(solution)/shard_map/ppermute | solution.py:409

commit v5 on v4

--- a/solution.py
+++ b/solution.py
@@ -236,7 +236,7 @@
                 store(i, j, n, jnp.concatenate([real, imag], axis=0).astype(jnp.bfloat16))
 
 
-def cross_kernel(chunk, plan, counts, flag_ref, *refs):
+def cross_kernel(chunk, plan, counts, carried, flag_ref, *refs):
     blocks, at = [], 0
     for count in counts:
         block = []
@@ -244,33 +244,39 @@
             block.append(refs[at : at + count])
             at += count
         blocks.append(block)
-    outs = refs[len(refs) - len(plan) :]
-    for out, (left, when_zero, when_one) in zip(outs, plan):
-
-        def store(i, j, n, tile, out=out):
-            out[i * SB + j, n] = tile
+    out = refs[-1]
+    size = SB * SB
+    for slot in range(carried):
+        out[slot * size : (slot + 1) * size] = refs[at + slot][...]
+    for slot, (when_zero, when_one) in enumerate(plan, carried):
+
+        def store(i, j, n, tile, slot=slot):
+            out[slot * size + i * SB + j, n] = tile
 
         if when_zero == when_one:
-            products(blocks[left], blocks[when_zero], chunk, store)
+            products(blocks[when_zero[0]], blocks[when_zero[1]], chunk, store)
         else:
-            for value, right in ((0, when_zero), (1, when_one)):
+            for value, (left, right) in ((0, when_zero), (1, when_one)):
 
                 @pl.when(flag_ref[0] == value)
                 def _(right=right, left=left, store=store):
                     products(blocks[left], blocks[right], chunk, store)
 
 
-def cross(chunk, plan, flag, blocks, after=()):
+def cross(chunk, plan, flag, blocks, carried=(), after=()):
     count = len(pairs_of(chunk))
-    shape = (SB * SB, count, TILE, LANES)
+    shape = ((len(carried) + len(plan)) * SB * SB, count, TILE, LANES)
     flat = [piece for block in blocks for part in block[: chunk + 1] for piece in part]
-    return pl.pallas_call(
-        functools.partial(cross_kernel, chunk, plan, tuple(len(block[0]) for block in blocks)),
+    flat += carried
+    return pl.pallas_call(
+        functools.partial(
+            cross_kernel, chunk, plan, tuple(len(block[0]) for block in blocks), len(carried)
+        ),
         in_specs=[SMEM]
         + [VMEM] * len(flat)
         + [pl.BlockSpec(memory_space=pl.ANY)] * len(after),
-        out_specs=[VMEM] * len(plan),
-        out_shape=[jax.ShapeDtypeStruct(shape, jnp.bfloat16)] * len(plan),
+        out_specs=VMEM,
+        out_shape=jax.ShapeDtypeStruct(shape, jnp.bfloat16),
         compiler_params=pltpu.CompilerParams(vmem_limit_bytes=24 * 1024 * 1024),
         cost_estimate=pl.CostEstimate(
             flops=len(plan) * 40_000_000, bytes_accessed=len(plan) * 1_500_000, transcendentals=0
@@ -284,32 +290,43 @@
 ALL_ROWS = CYCLE_ROWS + SB * 9 * SB
 
 
-def series_kernel(table_ref, *refs):
-    chunks = len(CHUNKS)
-    sources = refs[: (STEPS + 1) * chunks]
-    cycle_ref, region_ref, wide_ref, rows_ref, held_ref, sems = refs[(STEPS + 1) * chunks :]
+def series_kernel(core_ref, table_ref, one_ref, two_ref, kept_ref, got_ref, across_ref, *refs):
+    cycle_ref, region_ref, wide_ref, rows_ref, held_ref, sems = refs
     step = pl.program_id(0)
+    size = SB * SB
 
     def fetch(n):
         return pltpu.make_async_copy(table_ref.at[n], held_ref.at[n], sems.at[n])
+
+    def place(k, source, first):
+        for i in range(SB):
+            for j in range(SB):
+                for n, (c, d) in enumerate(pairs_of(0)):
+                    if k < STEPS:
+                        row = ((i * STEPS + k) * 9 + 3 * c + d) * SB + j
+                    else:
+                        row = CYCLE_ROWS + (i * 9 + 3 * c + d) * SB + j
+                    wide_ref[row * TILE : (row + 1) * TILE, :] = source[
+                        first + i * SB + j, n
+                    ].astype(jnp.float32)
 
     @pl.when(step == 0)
     def _():
         for n in range(LAGS // COLUMNS):
             fetch(n).start()
-        for k in range(STEPS + 1):
-            for chunk in range(chunks):
-                source = sources[k * chunks + chunk]
-                for i in range(SB):
-                    for j in range(SB):
-                        for n, (c, d) in enumerate(pairs_of(chunk)):
-                            if k < STEPS:
-                                row = ((i * STEPS + k) * 9 + 3 * c + d) * SB + j
-                            else:
-                                row = CYCLE_ROWS + (i * 9 + 3 * c + d) * SB + j
-                            wide_ref[row * TILE : (row + 1) * TILE, :] = source[
-                                i * SB + j, n
-                            ].astype(jnp.float32)
+        place(0, one_ref, 0)
+        place(1, two_ref, 0)
+        place(3, got_ref, 0)
+        place(4, across_ref, 0)
+
+        @pl.when(core_ref[0] == 0)
+        def _():
+            place(2, got_ref, size)
+
+        @pl.when(core_ref[0] == 1)
+        def _():
+            place(2, kept_ref, size)
+
         for piece in range(TILE):
             rows_ref[:, piece * LANES : (piece + 1) * LANES] = wide_ref[
                 pl.ds(piece, ALL_ROWS, stride=TILE), :
@@ -328,11 +345,11 @@
             region_ref[i, n] = series[row : row + SB]
 
 
-def lag_series(table, sources):
+def lag_series(core, table, *sources):
     return pl.pallas_call(
         series_kernel,
         grid=(LAGS // COLUMNS,),
-        in_specs=[pl.BlockSpec(memory_space=pl.ANY)] + [VMEM] * len(sources),
+        in_specs=[SMEM, pl.BlockSpec(memory_space=pl.ANY)] + [VMEM] * len(sources),
         out_specs=[
             pl.BlockSpec((SB, STEPS, 9, SB, COLUMNS), lambda n: (0, 0, 0, 0, n)),
             pl.BlockSpec((SB, 9, SB, COLUMNS), lambda n: (0, 0, 0, n)),
@@ -352,7 +369,7 @@
             flops=2 * ALL_ROWS * 2 * F * LAGS, bytes_accessed=12_000_000, transcendentals=0
         ),
         name="lag_series",
-    )(pltpu.with_memory_space_constraint(table, pltpu.HBM), *sources)
+    )(core.reshape(1), pltpu.with_memory_space_constraint(table, pltpu.HBM), *sources)
 
 
 def table_kernel(fine_ref, coarse_ref, out_ref):
@@ -474,29 +491,25 @@
     plane = lax.axis_index("region") % planes
     edge = (plane == 0).astype(jnp.int32)
     core = lax.axis_index("blk") & 1
-    own, twin, two, four, near, far = [], [], [], [], [], []
-    results = [[] for _ in range(STEPS + 1)]
-    for chunk, part in enumerate(CHUNKS):
-        early = sort_units(place, got[chunk], len(part) * TILE)
-        piece, block = choose(plane, early, spread(early, planes))
-        twin.append([swapped(block)])
-        closer, further = from_previous_region(block, piece, planes, twin[chunk][0])
-        own.append([block])
-        four.append([shifted(block, "blk", 4)])
-        two.append([shifted(block, "blk", 2)])
-        near.append([closer])
-        far.append(further)
-        (by_region,) = cross(chunk, ((0, 1, 2),), edge, (own, near, far))
-        by_two, for_one = cross(
-            chunk, ((0, 2, 2), (1, 0, 2)), core, (own, twin, two), (by_region,)
-        )
-        (for_three,) = cross(chunk, ((0, 1, 2),), core, (twin, two, four), (for_one,))
-        (by_four,) = cross(chunk, ((0, 1, 1),), core, (own, four), (for_three,))
-        every = (swapped(for_one), by_two, swapped(for_three), by_four, by_region)
-        for k, result in enumerate(every):
-            results[k].append(result)
-
-    cycle_series, region_series = lag_series(table, [r for result in results for r in result])
+    early = sort_units(place, got[0], 3 * TILE)
+    piece, block = choose(plane, early, spread(early, planes))
+    twin = swapped(block)
+    near, far = from_previous_region(block, piece, planes, twin)
+    two = shifted(block, "blk", 2)
+    ahead = shifted(block, "blk", -2)
+    beside = swapped(two)
+    own, twin, two, ahead, beside, near, far = (
+        [block] for block in ([block], [twin], [two], [ahead], [beside], [near], far)
+    )
+    by_two = cross(0, (((0, 1), (0, 1)),), core, (own, two), (), ())
+    by_four = cross(0, (((0, 1), (0, 1)),), core, (ahead, two), (), (by_two,))
+    by_region = cross(0, (((0, 1), (0, 2)),), edge, (own, near, far), (), (by_four,))
+    sent = cross(0, (((1, 2), (0, 2)),), core, (own, ahead, beside), (by_four,), (by_region,))
+    got_two = shifted(sent, "blk", 2)
+    by_one = cross(0, (((0, 2), (0, 1)),), core, (own, twin, beside), (), (sent,))
+    cycle_series, region_series = lag_series(
+        core, table, by_one, by_two, sent, got_two, by_region
+    )
     return jnp.swapaxes(cycle_series, 2, 3), jnp.swapaxes(region_series, 1, 2)
 
 

time: 218 us -> 207 us (0.950)
  the two profiles are of different devices: /device:TPU:11 before, /device:TPU:64 now
where the time goes in v5:
time: 207 us
  waiting for transfers between devices  114 us (55%)
  starting transfers between devices  50.3 us (24%)
  Pallas kernels  31 us (15%)
  other arithmetic  5.74 us (3%)
  local copies, waits for them, and re-layouts  3.9 us (2%)
    all_to_all x1, waiting for transfers between devices, body(): lax.all_to_all(part, 'blk', split_axis=0, concat_axis=0, tiled=True)  65.3 us
    ppermute x1, waiting for transfers between devices, from_previous_region(): lax.ppermute(piece, 'region', [(i, (i + planes) % regions) for i in range...  28.4 us
    all_to_all x1, starting transfers between devices, body(): lax.all_to_all(part, 'blk', split_axis=0, concat_axis=0, tiled=True)  15.4 us
    ppermute x3, starting transfers between devices, shifted(): lax.ppermute(block, axis, [(i, (i + by) % size) for i in range(size)])  10.7 us
    pallas_call x5, Pallas kernels, cross(): pl.pallas_call(functools.partial(cross_kernel, chunk, plan, tuple((len(bl...  9.9 us
    pallas_call x1, Pallas kernels, make_table(): pl.pallas_call(table_kernel, grid=(2, LAGS // COLUMNS), in_specs=[pl.Bloc...  9.35 us
    ppermute x1, starting transfers between devices, from_previous_region(): lax.ppermute(piece, 'region', [(i, (i + planes) % regions) for i in range...  8.22 us
    ppermute x3, waiting for transfers between devices, shifted(): lax.ppermute(block, axis, [(i, (i + by) % size) for i in range(size)])  7.82 us
  transfers between devices with their start and end apart: 14, of which 6 were waited for; matrix products, arithmetic and copies ran while one was open for 2% of the time, Pallas kernels for 9%

profile of v5, /device:TPU:64, one launch (start us, length us, event | category | flops | bytes accessed | tf_op | source)
XLA Modules:
  0.0 206.6 jit_solution(11208503370857250736)
XLA Ops:
  2.4 1.9 copy.11
  5.5 4.5 %whiten.1 = bf16[64,104,128]{2,1,0:T(8,128)(2,1)} custom-call(s32[128]{0:T(128)S(1)} %min.27.source_ref, bf16[256,128]{1,0:T(8,128)(2,1)S(1)} %add_convert_fusion.band_ref, f32[8,128]{1,0:T(8,128)S(1)} %convert_divide_fusion.inverse_ref, bf16[128,48,128]{2,1,0:T(8,128)(2,1)S(1)} %copy.12.archive_ref, bf16[64,8,128]{2,1,0:T(8,128)(2,1)S(1)} %broadcast_in_dim.91.mark_ref), custom_call_target="tpu_custom_call" | custom-call | flops 200000000 | bytes 4000000 | tf_op jit(solution)/shard_map/whiten/pallas_call | solution.py:115
  9.9 15.4 %all-to-all-start = ((bf16[64,104,128]{2,1,0:T(8,128)(2,1)}), bf16[64,104,128]{2,1,0:T(8,128)(2,1)S(1)}, u32[]{:S(2)}, u32[]{:S(2)}) async-start(bf16[64,104,128]{2,1,0:T(8,128)(2,1)} %whiten.1), calls=%async_computation | async-start | bytes 3407872 | tf_op jit(solution)/shard_map/all_to_all | solution.py:476
  25.7 4.1 %fusion.7 = (f32[1,128,2048]{2,1,0:T(8,128)S(1)}, f32[1,128,2048]{2,1,0:T(8,128)S(1)}) fusion(s32[2048]{0:T(1024)S(1)} %iota_add_fusion), kind=kLoop, calls=%fused_computation.11 | loop fusion | flops 3670016 | bytes 2105344 | tf_op jit(solution)/shard_map/cos | solution.py:401
  30.0 9.3 %lag_table.1.table_ref = bf16[8,2048,256]{2,1,0:T(8,128)(2,1)} custom-call(f32[2,128,2048]{2,1,0:T(8,128)S(1)} %pad_maximum_fusion.fine_ref, f32[2,8,2048]{2,1,0:T(8,128)S(1)} %pad_maximum_fusion.1.coarse_ref), custom_call_target="tpu_custom_call" | custom-call | flops 16000000 | bytes 12000000 | tf_op jit(solution)/shard_map/lag_table/pallas_call | solution.py:405
  39.3 65.3 %all-to-all-done.got_ref = bf16[64,104,128]{2,1,0:T(8,128)(2,1)S(1)} async-done(((bf16[64,104,128]{2,1,0:T(8,128)(2,1)}), bf16[64,104,128]{2,1,0:T(8,128)(2,1)S(1)}, u32[]{:S(2)}, u32[]{:S(2)}) %all-to-all-start) | async-done | bytes 1703968 | tf_op jit(solution)/shard_map/all_to_all | solution.py:476
  108.4 6.1 %collective-permute-done.refs_0_ = bf16[16,48,128]{2,1,0:T(8,128)(2,1)S(1)} collective-permute-done((bf16[16,48,128]{2,1,0:T(8,128)(2,1)S(1)}, bf16[16,48,128]{2,1,0:T(8,128)(2,1)S(1)}, u32[]{:S(2)}, u32[]{:S(2)}) %collective-permute-start) | collective-permute-done | bytes 196640 | tf_op jit(solution)/shard_map/ppermute | solution.py:432
  114.6 3.4 %collective-permute-start.4 = (bf16[64,48,128]{2,1,0:T(8,128)(2,1)S(1)}, bf16[64,48,128]{2,1,0:T(8,128)(2,1)S(1)}, u32[]{:S(2)}, u32[]{:S(2)}) collective-permute-start(bf16[64,48,128]{2,1,0:T(8,128)(2,1)S(1)} %get-tuple-element.10.refs_0_), channel_id=1, source_target_pairs={{0,2},{1,3},{2,4},{3,5},{4,6},{5,7},{6,8},{7,9},{8,10},{9,11},{10,... | collective-permute-start | bytes 2359304 | tf_op jit(solution)/shard_map/ppermute | solution.py:422
  118.0 1.9 collective-permute-start.3
  119.9 5.7 %collective-permute-start.7 = (bf16[64,48,128]{2,1,0:T(8,128)(2,1)S(1)}, bf16[64,48,128]{2,1,0:T(8,128)(2,1)S(1)}, u32[]{:S(2)}, u32[]{:S(2)}) collective-permute-start(bf16[64,48,128]{2,1,0:T(8,128)(2,1)S(1)} %get-tuple-element.10.refs_0_), channel_id=1, source_target_pairs={{0,64},{64,128},{128,192},{256,320},{320,384},{384,448},{1,65},{65... | collective-permute-start | bytes 2359304 | tf_op jit(solution)/shard_map/ppermute | solution.py:443
  125.6 8.2 %collective-permute-start.8 = (bf16[16,48,128]{2,1,0:T(8,128)(2,1)S(1)}, bf16[16,48,128]{2,1,0:T(8,128)(2,1)S(1)}, u32[]{:S(2)}, u32[]{:S(2)}) collective-permute-start(bf16[16,48,128]{2,1,0:T(8,128)(2,1)S(1)} %get-tuple-element.11), channel_id=1, source_target_pairs={{0,256},{64,320},{128,384},{192,448},{256,0},{320,64},{384,128},{4... | collective-permute-start | bytes 589832 | tf_op jit(solution)/shard_map/ppermute | solution.py:446
  133.8 5.4 %collective-permute-start.6 = (bf16[64,48,128]{2,1,0:T(8,128)(2,1)S(1)}, bf16[64,48,128]{2,1,0:T(8,128)(2,1)S(1)}, u32[]{:S(2)}, u32[]{:S(2)}) collective-permute-start(bf16[64,48,128]{2,1,0:T(8,128)(2,1)S(1)} %get-tuple-element.10.refs_0_), channel_id=1, source_target_pairs={{0,62},{1,63},{2,0},{3,1},{4,2},{5,3},{6,4},{7,5},{8,6},{9,7},{10,... | collective-permute-start | bytes 2359304 | tf_op jit(solution)/shard_map/ppermute | solution.py:422
  139.3 1.9 collective-permute-start.5
  141.2 28.4 %collective-permute-done.8.piece_ref.refs_2_ = bf16[16,48,128]{2,1,0:T(8,128)(2,1)S(1)} collective-permute-done((bf16[16,48,128]{2,1,0:T(8,128)(2,1)S(1)}, bf16[16,48,128]{2,1,0:T(8,128)(2,1)S(1)}, u32[]{:S(2)}, u32[]{:S(2)}) %collective-permute-start.8) | collective-permute-done | bytes 196640 | tf_op jit(solution)/shard_map/ppermute | solution.py:446
  174.8 1.8 cross.5.refs_2_.two_ref
  176.6 1.8 cross.6.refs_6_.refs_3_
  178.4 4.6 %collective-permute-done.10.refs_4_ = bf16[16,48,128]{2,1,0:T(8,128)(2,1)S(1)} collective-permute-done((bf16[16,48,128]{2,1,0:T(8,128)(2,1)}, bf16[16,48,128]{2,1,0:T(8,128)(2,1)S(1)}, u32[]{:S(2)}, u32[]{:S(2)}) %collective-permute-start.10) | collective-permute-done | bytes 196640 | tf_op jit(solution)/shard_map/ppermute | solution.py:451
  183.0 1.7 collective-permute-done.11.refs_5_
  184.7 2.8 %cross.7.refs_4_.across_ref = bf16[4,9,16,128]{3,2,1,0:T(8,128)(2,1)S(1)} custom-call(s32[1]{0:T(128)} %bitcast.7.flag_ref, bf16[64,48,128]{2,1,0:T(8,128)(2,1)S(1)} %get-tuple-element.10.refs_0_, bf16[64,48,128]{2,1,0:T(8,128)(2,1)S(1)} %copy-done.3, bf16[16,48,128]{2,1,0:T(8,128)(2,1)S(1)} %collective-permute-done.8.piece_ref.refs_2_, ...), custom_call_target="tpu_custom_call" | custom-call | flops 40000000 | bytes 1500000 | tf_op jit(solution)/shard_map/cross/pallas_call | solution.py:271
  187.5 1.8 cross.8.refs_3_.kept_ref
  189.3 1.9 collective-permute-start.12
  191.3 1.8 cross.9.one_ref
  193.1 7.8 %collective-permute-done.12.got_ref = bf16[8,9,16,128]{3,2,1,0:T(8,128)(2,1)S(1)} collective-permute-done((bf16[8,9,16,128]{3,2,1,0:T(8,128)(2,1)S(1)}, bf16[8,9,16,128]{3,2,1,0:T(8,128)(2,1)S(1)}, u32[]{:S(2)}, u32[]{:S(2)}) %collective-permute-start.12) | collective-permute-done | bytes 294944 | tf_op jit(solution)/shard_map/ppermute | solution.py:422
  200.9 5.7 %lag_series.1 = (bf16[2,4,9,2,2048]{4,3,2,1,0:T(2,128)(2,1)}, bf16[2,9,2,2048]{3,2,1,0:T(2,128)(2,1)}) custom-call(s32[1]{0:T(128)} %bitcast.flag_ref.core_ref, bf16[8,2048,256]{2,1,0:T(8,128)(2,1)} %lag_table.1.table_ref, bf16[4,9,16,128]{3,2,1,0:T(8,128)(2,1)S(1)} %cross.9.one_ref, bf16[4,9,16,128]{3,2,1,0:T(8,128)(2,1)S(1)} %cross.5.refs_2_.two_ref, ...), custom_call_target="tpu_custom_call" | custom-call | flops 1509949440 | bytes 12000000 | tf_op jit(solution)/shard_map/lag_series/pallas_call | solution.py:349
  (49 shorter events, 11.8 us)
Async XLA Ops:
  9.9 94.7 %all-to-all-start = ((bf16[64,104,128]{2,1,0:T(8,128)(2,1)}), bf16[64,104,128]{2,1,0:T(8,128)(2,1)S(1)}, u32[]{:S(2)}, u32[]{:S(2)}) async-start(bf16[64,104,128]{2,1,0:T(8,128)(2,1)} %whiten.1), calls=%async_computation | async-start | bytes 3407872 | tf_op jit(solution)/shard_map/all_to_all | solution.py:476
  105.8 8.8 %collective-permute-start = (bf16[16,48,128]{2,1,0:T(8,128)(2,1)S(1)}, bf16[16,48,128]{2,1,0:T(8,128)(2,1)S(1)}, u32[]{:S(2)}, u32[]{:S(2)}) collective-permute-start(bf16[16,48,128]{2,1,0:T(8,128)(2,1)S(1)} %get-tuple-element.20), channel_id=1, source_target_pairs={{192,0},{448,256},{193,1},{449,257},{194,2},{450,258},{195,3},{451... | collective-permute-start | bytes 589832 | tf_op jit(solution)/shard_map/ppermute | solution.py:432
  107.1 7.5 %collective-permute-start.1 = (bf16[16,48,128]{2,1,0:T(8,128)(2,1)S(1)}, bf16[16,48,128]{2,1,0:T(8,128)(2,1)S(1)}, u32[]{:S(2)}, u32[]{:S(2)}) collective-permute-start(bf16[16,48,128]{2,1,0:T(8,128)(2,1)S(1)} %get-tuple-element.19), channel_id=1, source_target_pairs={{192,64},{448,320},{193,65},{449,321},{194,66},{450,322},{195,67},... | collective-permute-start | bytes 589832 | tf_op jit(solution)/shard_map/ppermute | solution.py:432
  107.7 6.8 %collective-permute-start.2 = (bf16[16,48,128]{2,1,0:T(8,128)(2,1)S(1)}, bf16[16,48,128]{2,1,0:T(8,128)(2,1)S(1)}, u32[]{:S(2)}, u32[]{:S(2)}) collective-permute-start(bf16[16,48,128]{2,1,0:T(8,128)(2,1)S(1)} %get-tuple-element.18), channel_id=1, source_target_pairs={{192,128},{448,384},{193,129},{449,385},{194,130},{450,386},{195,1... | collective-permute-start | bytes 589832 | tf_op jit(solution)/shard_map/ppermute | solution.py:432
  114.6 24.7 %collective-permute-start.4 = (bf16[64,48,128]{2,1,0:T(8,128)(2,1)S(1)}, bf16[64,48,128]{2,1,0:T(8,128)(2,1)S(1)}, u32[]{:S(2)}, u32[]{:S(2)}) collective-permute-start(bf16[64,48,128]{2,1,0:T(8,128)(2,1)S(1)} %get-tuple-element.10.refs_0_), channel_id=1, source_target_pairs={{0,2},{1,3},{2,4},{3,5},{4,6},{5,7},{6,8},{7,9},{8,10},{9,11},{10,... | collective-permute-start | bytes 2359304 | tf_op jit(solution)/shard_map/ppermute | solution.py:422
  118.0 51.7 %collective-permute-start.3 = (bf16[64,48,128]{2,1,0:T(8,128)(2,1)S(1)}, bf16[64,48,128]{2,1,0:T(8,128)(2,1)S(1)}, u32[]{:S(2)}, u32[]{:S(2)}) collective-permute-start(bf16[64,48,128]{2,1,0:T(8,128)(2,1)S(1)} %get-tuple-element.10.refs_0_), channel_id=1, source_target_pairs={{0,1},{1,0},{2,3},{3,2},{4,5},{5,4},{6,7},{7,6},{8,9},{9,8},{10,11... | collective-permute-start | bytes 2359304 | tf_op jit(solution)/shard_map/ppermute | solution.py:426
  119.9 49.7 %collective-permute-start.7 = (bf16[64,48,128]{2,1,0:T(8,128)(2,1)S(1)}, bf16[64,48,128]{2,1,0:T(8,128)(2,1)S(1)}, u32[]{:S(2)}, u32[]{:S(2)}) collective-permute-start(bf16[64,48,128]{2,1,0:T(8,128)(2,1)S(1)} %get-tuple-element.10.refs_0_), channel_id=1, source_target_pairs={{0,64},{64,128},{128,192},{256,320},{320,384},{384,448},{1,65},{65... | collective-permute-start | bytes 2359304 | tf_op jit(solution)/shard_map/ppermute | solution.py:443
  125.6 44.0 %collective-permute-start.8 = (bf16[16,48,128]{2,1,0:T(8,128)(2,1)S(1)}, bf16[16,48,128]{2,1,0:T(8,128)(2,1)S(1)}, u32[]{:S(2)}, u32[]{:S(2)}) collective-permute-start(bf16[16,48,128]{2,1,0:T(8,128)(2,1)S(1)} %get-tuple-element.11), channel_id=1, source_target_pairs={{0,256},{64,320},{128,384},{192,448},{256,0},{320,64},{384,128},{4... | collective-permute-start | bytes 589832 | tf_op jit(solution)/shard_map/ppermute | solution.py:446
  133.8 42.8 %collective-permute-start.6 = (bf16[64,48,128]{2,1,0:T(8,128)(2,1)S(1)}, bf16[64,48,128]{2,1,0:T(8,128)(2,1)S(1)}, u32[]{:S(2)}, u32[]{:S(2)}) collective-permute-start(bf16[64,48,128]{2,1,0:T(8,128)(2,1)S(1)} %get-tuple-element.10.refs_0_), channel_id=1, source_target_pairs={{0,62},{1,63},{2,0},{3,1},{4,2},{5,3},{6,4},{7,5},{8,6},{9,7},{10,... | collective-permute-start | bytes 2359304 | tf_op jit(solution)/shard_map/ppermute | solution.py:422
  139.3 48.2 %collective-permute-start.5 = (bf16[64,48,128]{2,1,0:T(8,128)(2,1)S(1)}, bf16[64,48,128]{2,1,0:T(8,128)(2,1)S(1)}, u32[]{:S(2)}, u32[]{:S(2)}) collective-permute-start(bf16[64,48,128]{2,1,0:T(8,128)(2,1)S(1)} %collective-permute-done.4.refs_1_), channel_id=1, source_target_pairs={{0,1},{1,0},{2,3},{3,2},{4,5},{5,4},{6,7},{7,6},{8,9},{9,8},{10,11... | collective-permute-start | bytes 2359304 | tf_op jit(solution)/shard_map/ppermute | solution.py:426
  169.7 1.0 copy-start
  169.7 1.3 copy-start.2
  170.9 12.1 %collective-permute-start.10 = (bf16[16,48,128]{2,1,0:T(8,128)(2,1)}, bf16[16,48,128]{2,1,0:T(8,128)(2,1)S(1)}, u32[]{:S(2)}, u32[]{:S(2)}) collective-permute-start(bf16[16,48,128]{2,1,0:T(8,128)(2,1)} %relay_piece.1), channel_id=1, source_target_pairs={{128,0},{384,256},{129,1},{385,257},{130,2},{386,258},{131,3},{387... | collective-permute-start | bytes 589832 | tf_op jit(solution)/shard_map/ppermute | solution.py:451
  172.2 12.5 %collective-permute-start.11 = (bf16[16,48,128]{2,1,0:T(8,128)(2,1)}, bf16[16,48,128]{2,1,0:T(8,128)(2,1)}, u32[]{:S(2)}, u32[]{:S(2)}) collective-permute-start(bf16[16,48,128]{2,1,0:T(8,128)(2,1)} %relay_piece.1), channel_id=1, source_target_pairs={{192,0},{448,256},{193,1},{449,257},{194,2},{450,258},{195,3},{451... | collective-permute-start | bytes 589832 | tf_op jit(solution)/shard_map/ppermute | solution.py:451
  173.5 11.2 %collective-permute-start.9 = (bf16[16,48,128]{2,1,0:T(8,128)(2,1)}, bf16[16,48,128]{2,1,0:T(8,128)(2,1)}, u32[]{:S(2)}, u32[]{:S(2)}) collective-permute-start(bf16[16,48,128]{2,1,0:T(8,128)(2,1)} %relay_piece.1), channel_id=1, source_target_pairs={{64,0},{320,256},{65,1},{321,257},{66,2},{322,258},{67,3},{323,259... | collective-permute-start | bytes 589832 | tf_op jit(solution)/shard_map/ppermute | solution.py:451
  174.8 9.9 %copy-start.3 = (bf16[64,48,128]{2,1,0:T(8,128)(2,1)S(1)}, bf16[64,48,128]{2,1,0:T(8,128)(2,1)}, u32[]{:S(2)}) copy-start(bf16[64,48,128]{2,1,0:T(8,128)(2,1)} %copy-done.2) | copy-start | bytes 2359300
  187.5 3.7 %copy-start.1 = (bf16[64,48,128]{2,1,0:T(8,128)(2,1)S(1)}, bf16[64,48,128]{2,1,0:T(8,128)(2,1)}, u32[]{:S(2)}) copy-start(bf16[64,48,128]{2,1,0:T(8,128)(2,1)} %copy-done) | copy-start | bytes 2359300
  189.3 11.5 %collective-permute-start.12 = (bf16[8,9,16,128]{3,2,1,0:T(8,128)(2,1)S(1)}, bf16[8,9,16,128]{3,2,1,0:T(8,128)(2,1)S(1)}, u32[]{:S(2)}, u32[]{:S(2)}) collective-permute-start(bf16[8,9,16,128]{3,2,1,0:T(8,128)(2,1)S(1)} %cross.8.refs_3_.kept_ref), channel_id=1, source_target_pairs={{0,2},{1,3},{2,4},{3,5},{4,6},{5,7},{6,8},{7,9},{8,10},{9,11},{10,... | collective-permute-start | bytes 884744 | tf_op jit(solution)/shard_map/ppermute | solution.py:422

commit v6 on v5

--- a/solution.py
+++ b/solution.py
@@ -43,62 +43,70 @@
 
 def whiten_kernel(source_ref, band_ref, inverse_ref, archive_ref, mark_ref, *rest):
     outs, (level_ref,) = rest[:-1], rest[-1:]
-    base = pl.program_id(0) * GROUP
     rows = GROUP * FH
-
-    def slab_of(position):
-        return archive_ref[source_ref[base + position]].astype(jnp.float32)
-
-    def magnitude(position, carry):
-        slab = slab_of(position)
-        total = None
-        for c in range(3):
-            real = slab[c * TILE : c * TILE + FH]
-            imag = slab[c * TILE + FH : (c + 1) * TILE]
-            size = jnp.sqrt(real * real + imag * imag)
-            total = size if total is None else total + size
-        level_ref[pl.ds(pl.multiple_of(FH + position * FH, FH), FH), :] = total * (1.0 / 3.0)
-        return carry
-
-    lax.fori_loop(0, GROUP, magnitude, 0, unroll=4)
-    here = level_ref[FH : FH + rows, :]
-    before = level_ref[FH - 1 : FH - 1 + rows, :]
-    after = level_ref[FH + 1 : FH + 1 + rows, :]
+    band = band_ref[...]
+    inverse = inverse_ref[...]
     lane = lax.broadcasted_iota(jnp.int32, (rows, LANES), 1)
     row = lax.broadcasted_iota(jnp.int32, (rows, LANES), 0) % FH
-    edge = jnp.where(
-        lane >= LANES // 2,
-        jnp.where(row == 0, 0.0, before),
-        jnp.where(row == FH - 1, 0.0, after),
-    )
-    spread = jnp.concatenate([here, edge], axis=1)
-    high = spread.astype(jnp.bfloat16)
-    low = (spread - high.astype(jnp.float32)).astype(jnp.bfloat16)
-    band = band_ref[...]
-    window = jnp.dot(high, band, preferred_element_type=jnp.float32) + jnp.dot(
-        low, band, preferred_element_type=jnp.float32
-    )
-    level = window.reshape(GROUP, FH, LANES) * inverse_ref[...][None] + epsilon
-    level_ref[FH : FH + rows, :] = (1.0 / level).reshape(rows, LANES)
-
-    def divide(position, carry):
-        slab = slab_of(position)
-        gain = level_ref[pl.ds(pl.multiple_of(FH + position * FH, FH), FH), :]
-        for out, part in zip(outs, CHUNKS):
-            pieces = []
-            for c in part:
-                for half in range(2):
-                    start = c * TILE + half * FH
-                    pieces.append(slab[start : start + FH] * gain)
-            size = len(part) * TILE
-            start = pl.multiple_of((position % 2) * size, TILE)
-            out[position // 2, pl.ds(start, size), :] = jnp.concatenate(pieces, axis=0).astype(
-                jnp.bfloat16
-            )
+    outs[0][:, 2 * len(CHUNKS[0]) * TILE :, :] = mark_ref[...]
+
+    def group(step, carry):
+        base = step * GROUP
+
+        def slab_of(position):
+            return archive_ref[source_ref[base + position]].astype(jnp.float32)
+
+        def magnitude(position, carry):
+            slab = slab_of(position)
+            total = None
+            for c in range(3):
+                real = slab[c * TILE : c * TILE + FH]
+                imag = slab[c * TILE + FH : (c + 1) * TILE]
+                size = jnp.sqrt(real * real + imag * imag)
+                total = size if total is None else total + size
+            start = pl.multiple_of(FH + position * FH, FH)
+            level_ref[pl.ds(start, FH), :] = total * (1.0 / 3.0)
+            return carry
+
+        lax.fori_loop(0, GROUP, magnitude, 0, unroll=8)
+        here = level_ref[FH : FH + rows, :]
+        before = level_ref[FH - 1 : FH - 1 + rows, :]
+        after = level_ref[FH + 1 : FH + 1 + rows, :]
+        edge = jnp.where(
+            lane >= LANES // 2,
+            jnp.where(row == 0, 0.0, before),
+            jnp.where(row == FH - 1, 0.0, after),
+        )
+        spread = jnp.concatenate([here, edge], axis=1)
+        high = spread.astype(jnp.bfloat16)
+        low = (spread - high.astype(jnp.float32)).astype(jnp.bfloat16)
+        window = jnp.dot(high, band, preferred_element_type=jnp.float32) + jnp.dot(
+            low, band, preferred_element_type=jnp.float32
+        )
+        level = window.reshape(GROUP, FH, LANES) * inverse[None] + epsilon
+        level_ref[FH : FH + rows, :] = (1.0 / level).reshape(rows, LANES)
+
+        def divide(pair, carry):
+            for slot in range(2):
+                position = 2 * pair + slot
+                slab = slab_of(position)
+                gain = level_ref[pl.ds(pl.multiple_of(FH + position * FH, FH), FH), :]
+                for out, part in zip(outs, CHUNKS):
+                    pieces = []
+                    for c in part:
+                        for half in range(2):
+                            start = c * TILE + half * FH
+                            pieces.append(slab[start : start + FH] * gain)
+                    size = len(part) * TILE
+                    out[base // 2 + pair, slot * size : (slot + 1) * size, :] = (
+                        jnp.concatenate(pieces, axis=0).astype(jnp.bfloat16)
+                    )
+            return carry
+
+        lax.fori_loop(0, GROUP // 2, divide, 0, unroll=4)
         return carry
 
-    lax.fori_loop(0, GROUP, divide, 0, unroll=4)
-    outs[0][:, 2 * len(CHUNKS[0]) * TILE :, :] = mark_ref[...]
+    lax.fori_loop(0, CAP // GROUP, group, 0)
 
 
 def whiten(source, archive, marks):
@@ -114,12 +122,8 @@
     sizes[0] += MARK
     return pl.pallas_call(
         whiten_kernel,
-        grid=(CAP // GROUP,),
-        in_specs=[SMEM, VMEM, VMEM, VMEM]
-        + [pl.BlockSpec((GROUP // 2, MARK, LANES), lambda g: (g, 0, 0))],
-        out_specs=[
-            pl.BlockSpec((GROUP // 2, size, LANES), lambda g: (g, 0, 0)) for size in sizes
-        ],
+        in_specs=[SMEM, VMEM, VMEM, VMEM, VMEM],
+        out_specs=[VMEM for _ in sizes],
         out_shape=[
             jax.ShapeDtypeStruct((marks.shape[0], size, LANES), jnp.bfloat16) for size in sizes
         ],
@@ -179,7 +183,7 @@
             jax.ShapeDtypeStruct(block.shape, jnp.bfloat16),
         ],
         compiler_params=pltpu.CompilerParams(vmem_limit_bytes=16 * 1024 * 1024),
-        cost_estimate=pl.CostEstimate(flops=0, bytes_accessed=2_000_000, transcendentals=0),
+        cost_estimate=pl.CostEstimate(flops=20_000_000_000, bytes_accessed=2_000_000, transcendentals=0),
         name="choose_piece",
     )(plane.reshape(1), block, *pieces)
 
@@ -493,9 +497,9 @@
     core = lax.axis_index("blk") & 1
     early = sort_units(place, got[0], 3 * TILE)
     piece, block = choose(plane, early, spread(early, planes))
-    twin = swapped(block)
-    near, far = from_previous_region(block, piece, planes, twin)
-    two = shifted(block, "blk", 2)
+    twin = swapped(early)
+    near, far = from_previous_region(early, piece, planes, twin)
+    two = shifted(early, "blk", 2)
     ahead = shifted(block, "blk", -2)
     beside = swapped(two)
     own, twin, two, ahead, beside, near, far = (

time: 207 us -> 205 us (level)
  starting transfers between devices: 50.3 us -> 47.2 us
    ppermute x3, waiting for transfers between devices: 7.82 us -> 30.5 us  [shifted(): lax.ppermute(block, axis, [(i, (i + by) % size) for i in range(size)])]
    ppermute x1, waiting for transfers between devices: 28.4 us -> 11.3 us  [from_previous_region(): lax.ppermute(piece, 'region', [(i, (i + planes) % regions) for i in range...]
    ppermute x3, waiting for transfers between devices: 6.11 us -> 0.73 us  [spread(): lax.ppermute(block[plane * PIECE:(plane + 1) * PIECE], 'region', [(n + pl...]
    ppermute x1, starting transfers between devices: 5.67 us -> 3.44 us  [from_previous_region(): lax.ppermute(block, 'region', [(i, i + 1) for i in range(regions) if (i +...]
    ppermute x3, waiting for transfers between devices: 6.32 us -> 4.1 us  [from_previous_region(): lax.ppermute(piece, 'region', [(n + plane, n) for n in range(0, regions,...]
  transfers between devices with their start and end apart: 14 -> 14, of which waited for: 6 -> 7; matrix products, arithmetic and copies ran while one was open for 2% -> 2% of each run, Pallas kernels for 9% -> 10%
where the time goes in v6:
time: 205 us; the launch traced here: 204 us
  waiting for transfers between devices  112 us (55%)
  starting transfers between devices  47.2 us (23%)
  Pallas kernels  32.6 us (16%)
  other arithmetic  5.74 us (3%)
  local copies, waits for them, and re-layouts  5.01 us (2%)
    all_to_all x1, waiting for transfers between devices, body(): lax.all_to_all(part, 'blk', split_axis=0, concat_axis=0, tiled=True)  65.3 us
    ppermute x3, waiting for transfers between devices, shifted(): lax.ppermute(block, axis, [(i, (i + by) % size) for i in range(size)])  30.5 us
    all_to_all x1, starting transfers between devices, body(): lax.all_to_all(part, 'blk', split_axis=0, concat_axis=0, tiled=True)  15.4 us
    ppermute x1, waiting for transfers between devices, from_previous_region(): lax.ppermute(piece, 'region', [(i, (i + planes) % regions) for i in range...  11.3 us
    pallas_call x5, Pallas kernels, cross(): pl.pallas_call(functools.partial(cross_kernel, chunk, plan, tuple((len(bl...  9.89 us
    ppermute x3, starting transfers between devices, shifted(): lax.ppermute(block, axis, [(i, (i + by) % size) for i in range(size)])  9.86 us
    pallas_call x1, Pallas kernels, make_table(): pl.pallas_call(table_kernel, grid=(2, LAGS // COLUMNS), in_specs=[pl.Bloc...  9.35 us
    ppermute x1, starting transfers between devices, from_previous_region(): lax.ppermute(piece, 'region', [(i, (i + planes) % regions) for i in range...  8.22 us
  transfers between devices with their start and end apart: 14, of which 7 were waited for; matrix products, arithmetic and copies ran while one was open for 2% of the time, Pallas kernels for 10%

profile of v6, /device:TPU:64, one launch (start us, length us, event | category | flops | bytes accessed | tf_op | source)
XLA Modules:
  0.0 204.2 jit_solution(6311549540105102100)
XLA Ops:
  2.4 1.9 copy.11
  5.5 4.0 %whiten.1 = bf16[64,104,128]{2,1,0:T(8,128)(2,1)} custom-call(s32[128]{0:T(128)S(1)} %min.27.source_ref, bf16[256,128]{1,0:T(8,128)(2,1)S(1)} %add_convert_fusion.band_ref, f32[8,128]{1,0:T(8,128)S(1)} %convert_divide_fusion.inverse_ref, bf16[128,48,128]{2,1,0:T(8,128)(2,1)S(1)} %copy.12.archive_ref, bf16[64,8,128]{2,1,0:T(8,128)(2,1)S(1)} %broadcast_in_dim.91.mark_ref), custom_call_target="tpu_custom_call" | custom-call | flops 200000000 | bytes 4000000 | tf_op jit(solution)/shard_map/whiten/pallas_call | solution.py:123
  9.5 15.4 %all-to-all-start = ((bf16[64,104,128]{2,1,0:T(8,128)(2,1)}), bf16[64,104,128]{2,1,0:T(8,128)(2,1)S(1)}, u32[]{:S(2)}, u32[]{:S(2)}) async-start(bf16[64,104,128]{2,1,0:T(8,128)(2,1)} %whiten.1), calls=%async_computation | async-start | bytes 3407872 | tf_op jit(solution)/shard_map/all_to_all | solution.py:480
  25.3 4.1 %fusion.7 = (f32[1,128,2048]{2,1,0:T(8,128)S(1)}, f32[1,128,2048]{2,1,0:T(8,128)S(1)}) fusion(s32[2048]{0:T(1024)S(1)} %iota_add_fusion), kind=kLoop, calls=%fused_computation.11 | loop fusion | flops 3670016 | bytes 2105344 | tf_op jit(solution)/shard_map/cos | solution.py:405
  29.6 9.3 %lag_table.1.table_ref = bf16[8,2048,256]{2,1,0:T(8,128)(2,1)} custom-call(f32[2,128,2048]{2,1,0:T(8,128)S(1)} %pad_maximum_fusion.fine_ref, f32[2,8,2048]{2,1,0:T(8,128)S(1)} %pad_maximum_fusion.1.coarse_ref), custom_call_target="tpu_custom_call" | custom-call | flops 16000000 | bytes 12000000 | tf_op jit(solution)/shard_map/lag_table/pallas_call | solution.py:409
  38.9 65.3 %all-to-all-done.got_ref = bf16[64,104,128]{2,1,0:T(8,128)(2,1)S(1)} async-done(((bf16[64,104,128]{2,1,0:T(8,128)(2,1)}), bf16[64,104,128]{2,1,0:T(8,128)(2,1)S(1)}, u32[]{:S(2)}, u32[]{:S(2)}) %all-to-all-start) | async-done | bytes 1703968 | tf_op jit(solution)/shard_map/all_to_all | solution.py:480
  110.0 1.9 collective-permute-start.3
  111.9 3.4 %collective-permute-start.7 = (bf16[64,48,128]{2,1,0:T(8,128)(2,1)}, bf16[64,48,128]{2,1,0:T(8,128)(2,1)S(1)}, u32[]{:S(2)}, u32[]{:S(2)}) collective-permute-start(bf16[64,48,128]{2,1,0:T(8,128)(2,1)} %sort_units.1.block_ref), channel_id=1, source_target_pairs={{0,64},{64,128},{128,192},{256,320},{320,384},{384,448},{1,65},{65... | collective-permute-start | bytes 2359304 | tf_op jit(solution)/shard_map/ppermute | solution.py:447
  116.1 3.3 %collective-permute-start.4 = (bf16[64,48,128]{2,1,0:T(8,128)(2,1)}, bf16[64,48,128]{2,1,0:T(8,128)(2,1)S(1)}, u32[]{:S(2)}, u32[]{:S(2)}) collective-permute-start(bf16[64,48,128]{2,1,0:T(8,128)(2,1)} %sort_units.1.block_ref), channel_id=1, source_target_pairs={{0,2},{1,3},{2,4},{3,5},{4,6},{5,7},{6,8},{7,9},{8,10},{9,11},{10,... | collective-permute-start | bytes 2359304 | tf_op jit(solution)/shard_map/ppermute | solution.py:426
  120.7 8.2 %collective-permute-start.8 = (bf16[16,48,128]{2,1,0:T(8,128)(2,1)S(1)}, bf16[16,48,128]{2,1,0:T(8,128)(2,1)S(1)}, u32[]{:S(2)}, u32[]{:S(2)}) collective-permute-start(bf16[16,48,128]{2,1,0:T(8,128)(2,1)S(1)} %get-tuple-element.11), channel_id=1, source_target_pairs={{0,256},{64,320},{128,384},{192,448},{256,0},{320,64},{384,128},{4... | collective-permute-start | bytes 589832 | tf_op jit(solution)/shard_map/ppermute | solution.py:450
  129.0 4.6 %collective-permute-start.6 = (bf16[64,48,128]{2,1,0:T(8,128)(2,1)S(1)}, bf16[64,48,128]{2,1,0:T(8,128)(2,1)S(1)}, u32[]{:S(2)}, u32[]{:S(2)}) collective-permute-start(bf16[64,48,128]{2,1,0:T(8,128)(2,1)S(1)} %get-tuple-element.10.refs_0_), channel_id=1, source_target_pairs={{0,62},{1,63},{2,0},{3,1},{4,2},{5,3},{6,4},{7,5},{8,6},{9,7},{10,... | collective-permute-start | bytes 2359304 | tf_op jit(solution)/shard_map/ppermute | solution.py:426
  133.6 19.4 %collective-permute-done.4.refs_1_ = bf16[64,48,128]{2,1,0:T(8,128)(2,1)S(1)} collective-permute-done((bf16[64,48,128]{2,1,0:T(8,128)(2,1)}, bf16[64,48,128]{2,1,0:T(8,128)(2,1)S(1)}, u32[]{:S(2)}, u32[]{:S(2)}) %collective-permute-start.4) | collective-permute-done | bytes 786464 | tf_op jit(solution)/shard_map/ppermute | solution.py:426
  153.0 1.9 collective-permute-start.5
  154.9 11.3 %collective-permute-done.8.piece_ref.refs_2_ = bf16[16,48,128]{2,1,0:T(8,128)(2,1)S(1)} collective-permute-done((bf16[16,48,128]{2,1,0:T(8,128)(2,1)S(1)}, bf16[16,48,128]{2,1,0:T(8,128)(2,1)S(1)}, u32[]{:S(2)}, u32[]{:S(2)}) %collective-permute-start.8) | collective-permute-done | bytes 196640 | tf_op jit(solution)/shard_map/ppermute | solution.py:450
  171.4 1.8 cross.5.refs_2_.two_ref
  173.2 1.8 cross.6.refs_6_.refs_3_
  175.0 1.9 collective-permute-done.10.refs_4_
  176.8 2.2 %collective-permute-done.11.refs_5_ = bf16[16,48,128]{2,1,0:T(8,128)(2,1)} collective-permute-done((bf16[16,48,128]{2,1,0:T(8,128)(2,1)}, bf16[16,48,128]{2,1,0:T(8,128)(2,1)}, u32[]{:S(2)}, u32[]{:S(2)}) %collective-permute-start.11) | collective-permute-done | bytes 196640 | tf_op jit(solution)/shard_map/ppermute | solution.py:455
  179.1 2.8 %cross.7.refs_4_.across_ref = bf16[4,9,16,128]{3,2,1,0:T(8,128)(2,1)S(1)} custom-call(s32[1]{0:T(128)} %bitcast.7.flag_ref, bf16[64,48,128]{2,1,0:T(8,128)(2,1)S(1)} %get-tuple-element.10.refs_0_, bf16[64,48,128]{2,1,0:T(8,128)(2,1)S(1)} %copy-done.3, bf16[16,48,128]{2,1,0:T(8,128)(2,1)S(1)} %collective-permute-done.8.piece_ref.refs_2_, ...), custom_call_target="tpu_custom_call" | custom-call | flops 40000000 | bytes 1500000 | tf_op jit(solution)/shard_map/cross/pallas_call | solution.py:275
  181.9 1.8 cross.8.refs_3_.kept_ref
  183.7 1.9 collective-permute-start.12
  185.6 1.8 cross.9.one_ref
  187.4 11.1 %collective-permute-done.12.got_ref = bf16[8,9,16,128]{3,2,1,0:T(8,128)(2,1)S(1)} collective-permute-done((bf16[8,9,16,128]{3,2,1,0:T(8,128)(2,1)S(1)}, bf16[8,9,16,128]{3,2,1,0:T(8,128)(2,1)S(1)}, u32[]{:S(2)}, u32[]{:S(2)}) %collective-permute-start.12) | collective-permute-done | bytes 294944 | tf_op jit(solution)/shard_map/ppermute | solution.py:426
  198.4 5.7 %lag_series.1 = (bf16[2,4,9,2,2048]{4,3,2,1,0:T(2,128)(2,1)}, bf16[2,9,2,2048]{3,2,1,0:T(2,128)(2,1)}) custom-call(s32[1]{0:T(128)} %bitcast.flag_ref.core_ref, bf16[8,2048,256]{2,1,0:T(8,128)(2,1)} %lag_table.1.table_ref, bf16[4,9,16,128]{3,2,1,0:T(8,128)(2,1)S(1)} %cross.9.one_ref, bf16[4,9,16,128]{3,2,1,0:T(8,128)(2,1)S(1)} %cross.5.refs_2_.two_ref, ...), custom_call_target="tpu_custom_call" | custom-call | flops 1509949440 | bytes 12000000 | tf_op jit(solution)/shard_map/lag_series/pallas_call | solution.py:353
  (49 shorter events, 15.7 us)
Async XLA Ops:
  9.5 94.7 %all-to-all-start = ((bf16[64,104,128]{2,1,0:T(8,128)(2,1)}), bf16[64,104,128]{2,1,0:T(8,128)(2,1)S(1)}, u32[]{:S(2)}, u32[]{:S(2)}) async-start(bf16[64,104,128]{2,1,0:T(8,128)(2,1)} %whiten.1), calls=%async_computation | async-start | bytes 3407872 | tf_op jit(solution)/shard_map/all_to_all | solution.py:480
  107.3 8.8 %collective-permute-start = (bf16[16,48,128]{2,1,0:T(8,128)(2,1)S(1)}, bf16[16,48,128]{2,1,0:T(8,128)(2,1)S(1)}, u32[]{:S(2)}, u32[]{:S(2)}) collective-permute-start(bf16[16,48,128]{2,1,0:T(8,128)(2,1)S(1)} %get-tuple-element.20), channel_id=1, source_target_pairs={{192,0},{448,256},{193,1},{449,257},{194,2},{450,258},{195,3},{451... | collective-permute-start | bytes 589832 | tf_op jit(solution)/shard_map/ppermute | solution.py:436
  108.6 10.8 %collective-permute-start.1 = (bf16[16,48,128]{2,1,0:T(8,128)(2,1)S(1)}, bf16[16,48,128]{2,1,0:T(8,128)(2,1)S(1)}, u32[]{:S(2)}, u32[]{:S(2)}) collective-permute-start(bf16[16,48,128]{2,1,0:T(8,128)(2,1)S(1)} %get-tuple-element.19), channel_id=1, source_target_pairs={{192,64},{448,320},{193,65},{449,321},{194,66},{450,322},{195,67},... | collective-permute-start | bytes 589832 | tf_op jit(solution)/shard_map/ppermute | solution.py:436
  109.3 10.2 %collective-permute-start.2 = (bf16[16,48,128]{2,1,0:T(8,128)(2,1)S(1)}, bf16[16,48,128]{2,1,0:T(8,128)(2,1)S(1)}, u32[]{:S(2)}, u32[]{:S(2)}) collective-permute-start(bf16[16,48,128]{2,1,0:T(8,128)(2,1)S(1)} %get-tuple-element.18), channel_id=1, source_target_pairs={{192,128},{448,384},{193,129},{449,385},{194,130},{450,386},{195,1... | collective-permute-start | bytes 589832 | tf_op jit(solution)/shard_map/ppermute | solution.py:436
  110.0 56.2 %collective-permute-start.3 = (bf16[64,48,128]{2,1,0:T(8,128)(2,1)}, bf16[64,48,128]{2,1,0:T(8,128)(2,1)S(1)}, u32[]{:S(2)}, u32[]{:S(2)}) collective-permute-start(bf16[64,48,128]{2,1,0:T(8,128)(2,1)} %sort_units.1.block_ref), channel_id=1, source_target_pairs={{0,1},{1,0},{2,3},{3,2},{4,5},{5,4},{6,7},{7,6},{8,9},{9,8},{10,11... | collective-permute-start | bytes 2359304 | tf_op jit(solution)/shard_map/ppermute | solution.py:430
  111.9 54.3 %collective-permute-start.7 = (bf16[64,48,128]{2,1,0:T(8,128)(2,1)}, bf16[64,48,128]{2,1,0:T(8,128)(2,1)S(1)}, u32[]{:S(2)}, u32[]{:S(2)}) collective-permute-start(bf16[64,48,128]{2,1,0:T(8,128)(2,1)} %sort_units.1.block_ref), channel_id=1, source_target_pairs={{0,64},{64,128},{128,192},{256,320},{320,384},{384,448},{1,65},{65... | collective-permute-start | bytes 2359304 | tf_op jit(solution)/shard_map/ppermute | solution.py:447
  116.1 36.9 %collective-permute-start.4 = (bf16[64,48,128]{2,1,0:T(8,128)(2,1)}, bf16[64,48,128]{2,1,0:T(8,128)(2,1)S(1)}, u32[]{:S(2)}, u32[]{:S(2)}) collective-permute-start(bf16[64,48,128]{2,1,0:T(8,128)(2,1)} %sort_units.1.block_ref), channel_id=1, source_target_pairs={{0,2},{1,3},{2,4},{3,5},{4,6},{5,7},{6,8},{7,9},{8,10},{9,11},{10,... | collective-permute-start | bytes 2359304 | tf_op jit(solution)/shard_map/ppermute | solution.py:426
  120.7 45.5 %collective-permute-start.8 = (bf16[16,48,128]{2,1,0:T(8,128)(2,1)S(1)}, bf16[16,48,128]{2,1,0:T(8,128)(2,1)S(1)}, u32[]{:S(2)}, u32[]{:S(2)}) collective-permute-start(bf16[16,48,128]{2,1,0:T(8,128)(2,1)S(1)} %get-tuple-element.11), channel_id=1, source_target_pairs={{0,256},{64,320},{128,384},{192,448},{256,0},{320,64},{384,128},{4... | collective-permute-start | bytes 589832 | tf_op jit(solution)/shard_map/ppermute | solution.py:450
  129.0 44.2 %collective-permute-start.6 = (bf16[64,48,128]{2,1,0:T(8,128)(2,1)S(1)}, bf16[64,48,128]{2,1,0:T(8,128)(2,1)S(1)}, u32[]{:S(2)}, u32[]{:S(2)}) collective-permute-start(bf16[64,48,128]{2,1,0:T(8,128)(2,1)S(1)} %get-tuple-element.10.refs_0_), channel_id=1, source_target_pairs={{0,62},{1,63},{2,0},{3,1},{4,2},{5,3},{6,4},{7,5},{8,6},{9,7},{10,... | collective-permute-start | bytes 2359304 | tf_op jit(solution)/shard_map/ppermute | solution.py:426
  153.0 28.9 %collective-permute-start.5 = (bf16[64,48,128]{2,1,0:T(8,128)(2,1)S(1)}, bf16[64,48,128]{2,1,0:T(8,128)(2,1)S(1)}, u32[]{:S(2)}, u32[]{:S(2)}) collective-permute-start(bf16[64,48,128]{2,1,0:T(8,128)(2,1)S(1)} %collective-permute-done.4.refs_1_), channel_id=1, source_target_pairs={{0,1},{1,0},{2,3},{3,2},{4,5},{5,4},{6,7},{7,6},{8,9},{9,8},{10,11... | collective-permute-start | bytes 2359304 | tf_op jit(solution)/shard_map/ppermute | solution.py:430
  166.2 1.0 copy-start
  166.2 1.3 copy-start.2
  167.5 9.4 %collective-permute-start.10 = (bf16[16,48,128]{2,1,0:T(8,128)(2,1)}, bf16[16,48,128]{2,1,0:T(8,128)(2,1)S(1)}, u32[]{:S(2)}, u32[]{:S(2)}) collective-permute-start(bf16[16,48,128]{2,1,0:T(8,128)(2,1)} %relay_piece.1), channel_id=1, source_target_pairs={{128,0},{384,256},{129,1},{385,257},{130,2},{386,258},{131,3},{387... | collective-permute-start | bytes 589832 | tf_op jit(solution)/shard_map/ppermute | solution.py:455
  168.8 10.3 %collective-permute-start.11 = (bf16[16,48,128]{2,1,0:T(8,128)(2,1)}, bf16[16,48,128]{2,1,0:T(8,128)(2,1)}, u32[]{:S(2)}, u32[]{:S(2)}) collective-permute-start(bf16[16,48,128]{2,1,0:T(8,128)(2,1)} %relay_piece.1), channel_id=1, source_target_pairs={{192,0},{448,256},{193,1},{449,257},{194,2},{450,258},{195,3},{451... | collective-permute-start | bytes 589832 | tf_op jit(solution)/shard_map/ppermute | solution.py:455
  170.1 9.0 %collective-permute-start.9 = (bf16[16,48,128]{2,1,0:T(8,128)(2,1)}, bf16[16,48,128]{2,1,0:T(8,128)(2,1)}, u32[]{:S(2)}, u32[]{:S(2)}) collective-permute-start(bf16[16,48,128]{2,1,0:T(8,128)(2,1)} %relay_piece.1), channel_id=1, source_target_pairs={{64,0},{320,256},{65,1},{321,257},{66,2},{322,258},{67,3},{323,259... | collective-permute-start | bytes 589832 | tf_op jit(solution)/shard_map/ppermute | solution.py:455
  171.4 7.7 %copy-start.3 = (bf16[64,48,128]{2,1,0:T(8,128)(2,1)S(1)}, bf16[64,48,128]{2,1,0:T(8,128)(2,1)}, u32[]{:S(2)}) copy-start(bf16[64,48,128]{2,1,0:T(8,128)(2,1)} %copy-done.2) | copy-start | bytes 2359300
  181.8 3.7 %copy-start.1 = (bf16[64,48,128]{2,1,0:T(8,128)(2,1)S(1)}, bf16[64,48,128]{2,1,0:T(8,128)(2,1)}, u32[]{:S(2)}) copy-start(bf16[64,48,128]{2,1,0:T(8,128)(2,1)} %copy-done) | copy-start | bytes 2359300
  183.7 14.8 %collective-permute-start.12 = (bf16[8,9,16,128]{3,2,1,0:T(8,128)(2,1)S(1)}, bf16[8,9,16,128]{3,2,1,0:T(8,128)(2,1)S(1)}, u32[]{:S(2)}, u32[]{:S(2)}) collective-permute-start(bf16[8,9,16,128]{3,2,1,0:T(8,128)(2,1)S(1)} %cross.8.refs_3_.kept_ref), channel_id=1, source_target_pairs={{0,2},{1,3},{2,4},{3,5},{4,6},{5,7},{6,8},{7,9},{8,10},{9,11},{10,... | collective-permute-start | bytes 884744 | tf_op jit(solution)/shard_map/ppermute | solution.py:426

commit v7 on v6

--- a/solution.py
+++ b/solution.py
@@ -134,7 +134,7 @@
     )(source, band, inverse, archive, marks)
 
 
-def sort_kernel(source_ref, got_ref, out_ref):
+def sort_kernel(source_ref, got_ref, out_ref, *piece_refs):
     rows = out_ref.shape[1]
 
     def move(unit, carry):
@@ -144,14 +144,17 @@
         return carry
 
     lax.fori_loop(0, UNITS, move, 0, unroll=8)
-
-
-def sort_units(source, got, rows):
+    for n, ref in enumerate(piece_refs):
+        ref[...] = out_ref[n * PIECE : (n + 1) * PIECE]
+
+
+def sort_units(source, got, rows, pieces):
+    shapes = [(UNITS, rows, LANES)] + [(PIECE, rows, LANES)] * pieces
     return pl.pallas_call(
         sort_kernel,
         in_specs=[SMEM, VMEM],
-        out_specs=VMEM,
-        out_shape=jax.ShapeDtypeStruct((UNITS, rows, LANES), jnp.bfloat16),
+        out_specs=[VMEM for _ in shapes],
+        out_shape=[jax.ShapeDtypeStruct(shape, jnp.bfloat16) for shape in shapes],
         compiler_params=pltpu.CompilerParams(vmem_limit_bytes=16 * 1024 * 1024),
         cost_estimate=pl.CostEstimate(flops=0, bytes_accessed=3_000_000, transcendentals=0),
         name="sort_units",
@@ -430,15 +433,12 @@
     return lax.ppermute(block, "blk", [(i, i ^ 1) for i in range(lax.axis_size("blk"))])
 
 
-def spread(block, planes):
+def spread(pieces):
+    planes = len(pieces) + 1
     starts = range(0, lax.axis_size("region"), planes)
     return [
-        lax.ppermute(
-            block[plane * PIECE : (plane + 1) * PIECE],
-            "region",
-            [(n + planes - 1, n + plane) for n in starts],
-        )
-        for plane in range(planes - 1)
+        lax.ppermute(piece, "region", [(n + planes - 1, n + plane) for n in starts])
+        for plane, piece in enumerate(pieces)
     ]
 
 
@@ -454,7 +454,7 @@
         far.append(
             lax.ppermute(piece, "region", [(n + plane, n) for n in range(0, regions, planes)])
         )
-    return near, far
+    return near, far, piece
 
 
 def body(archive, unit_of, row_counts):
@@ -495,22 +495,22 @@
     plane = lax.axis_index("region") % planes
     edge = (plane == 0).astype(jnp.int32)
     core = lax.axis_index("blk") & 1
-    early = sort_units(place, got[0], 3 * TILE)
-    piece, block = choose(plane, early, spread(early, planes))
+    early, *pieces = sort_units(place, got[0], 3 * TILE, planes - 1)
+    piece, block = choose(plane, early, spread(pieces))
     twin = swapped(early)
-    near, far = from_previous_region(early, piece, planes, twin)
+    near, far, passed = from_previous_region(early, piece, planes, twin)
     two = shifted(early, "blk", 2)
     ahead = shifted(block, "blk", -2)
     beside = swapped(two)
     own, twin, two, ahead, beside, near, far = (
         [block] for block in ([block], [twin], [two], [ahead], [beside], [near], far)
     )
-    by_two = cross(0, (((0, 1), (0, 1)),), core, (own, two), (), ())
-    by_four = cross(0, (((0, 1), (0, 1)),), core, (ahead, two), (), (by_two,))
-    by_region = cross(0, (((0, 1), (0, 2)),), edge, (own, near, far), (), (by_four,))
-    sent = cross(0, (((1, 2), (0, 2)),), core, (own, ahead, beside), (by_four,), (by_region,))
+    by_four = cross(0, (((0, 1), (0, 1)),), core, (ahead, two), (), (passed,))
+    sent = cross(0, (((1, 2), (0, 2)),), core, (own, ahead, beside), (by_four,))
     got_two = shifted(sent, "blk", 2)
-    by_one = cross(0, (((0, 2), (0, 1)),), core, (own, twin, beside), (), (sent,))
+    by_two = cross(0, (((0, 1), (0, 1)),), core, (own, two), (), (sent,))
+    by_one = cross(0, (((0, 2), (0, 1)),), core, (own, twin, beside), (), (by_two,))
+    by_region = cross(0, (((0, 1), (0, 2)),), edge, (own, near, far), (), (by_one,))
     cycle_series, region_series = lag_series(
         core, table, by_one, by_two, sent, got_two, by_region
     )

time: 205 us -> 201 us (0.980)
  the two profiles are of different devices: /device:TPU:64 before, /device:TPU:57 now
where the time goes in v7:
time: 201 us
  waiting for transfers between devices  88.8 us (44%)
  starting transfers between devices  63.8 us (32%)
  Pallas kernels  35.6 us (18%)
  other arithmetic  5.74 us (3%)
  local copies, waits for them, and re-layouts  4.96 us (2%)
    all_to_all x1, waiting for transfers between devices, body(): lax.all_to_all(part, 'blk', split_axis=0, concat_axis=0, tiled=True)  63.4 us
    ppermute x2, starting transfers between devices, swapped(): lax.ppermute(block, 'blk', [(i, i ^ 1) for i in range(lax.axis_size('blk'...  19 us
    all_to_all x1, starting transfers between devices, body(): lax.all_to_all(part, 'blk', split_axis=0, concat_axis=0, tiled=True)  15.8 us
    ppermute x1, waiting for transfers between devices, from_previous_region(): lax.ppermute(piece, 'region', [(i, (i + planes) % regions) for i in range...  13.4 us
    ppermute x3, starting transfers between devices, shifted(): lax.ppermute(block, axis, [(i, (i + by) % size) for i in range(size)])  11.5 us
    pallas_call x5, Pallas kernels, cross(): pl.pallas_call(functools.partial(cross_kernel, chunk, plan, tuple((len(bl...  11.1 us
    pallas_call x1, Pallas kernels, make_table(): pl.pallas_call(table_kernel, grid=(2, LAGS // COLUMNS), in_specs=[pl.Bloc...  9.35 us
    ppermute x1, starting transfers between devices, from_previous_region(): lax.ppermute(piece, 'region', [(i, (i + planes) % regions) for i in range...  7.93 us
  transfers between devices with their start and end apart: 14, of which 5 were waited for; matrix products, arithmetic and copies ran while one was open for 2% of the time, Pallas kernels for 11%

profile of v7, /device:TPU:57, one launch (start us, length us, event | category | flops | bytes accessed | tf_op | source)
XLA Modules:
  0.0 200.5 jit_solution(9701251924730168120)
XLA Ops:
  2.4 1.9 copy.11
  5.5 4.0 %whiten.1 = bf16[64,104,128]{2,1,0:T(8,128)(2,1)} custom-call(s32[128]{0:T(128)S(1)} %min.27.source_ref, bf16[256,128]{1,0:T(8,128)(2,1)S(1)} %add_convert_fusion.band_ref, f32[8,128]{1,0:T(8,128)S(1)} %convert_divide_fusion.inverse_ref, bf16[128,48,128]{2,1,0:T(8,128)(2,1)S(1)} %copy.12.archive_ref, bf16[64,8,128]{2,1,0:T(8,128)(2,1)S(1)} %broadcast_in_dim.91.mark_ref), custom_call_target="tpu_custom_call" | custom-call | flops 200000000 | bytes 4000000 | tf_op jit(solution)/shard_map/whiten/pallas_call | solution.py:123
  9.5 15.8 %all-to-all-start = ((bf16[64,104,128]{2,1,0:T(8,128)(2,1)}), bf16[64,104,128]{2,1,0:T(8,128)(2,1)S(1)}, u32[]{:S(2)}, u32[]{:S(2)}) async-start(bf16[64,104,128]{2,1,0:T(8,128)(2,1)} %whiten.1), calls=%async_computation | async-start | bytes 3407872 | tf_op jit(solution)/shard_map/all_to_all | solution.py:480
  25.7 4.1 %fusion.7 = (f32[1,128,2048]{2,1,0:T(8,128)S(1)}, f32[1,128,2048]{2,1,0:T(8,128)S(1)}) fusion(s32[2048]{0:T(1024)S(1)} %iota_add_fusion), kind=kLoop, calls=%fused_computation.11 | loop fusion | flops 3670016 | bytes 2105344 | tf_op jit(solution)/shard_map/cos | solution.py:408
  30.0 9.3 %lag_table.1.table_ref = bf16[8,2048,256]{2,1,0:T(8,128)(2,1)} custom-call(f32[2,128,2048]{2,1,0:T(8,128)S(1)} %pad_maximum_fusion.fine_ref, f32[2,8,2048]{2,1,0:T(8,128)S(1)} %pad_maximum_fusion.1.coarse_ref), custom_call_target="tpu_custom_call" | custom-call | flops 16000000 | bytes 12000000 | tf_op jit(solution)/shard_map/lag_table/pallas_call | solution.py:412
  39.4 63.4 %all-to-all-done.got_ref = bf16[64,104,128]{2,1,0:T(8,128)(2,1)S(1)} async-done(((bf16[64,104,128]{2,1,0:T(8,128)(2,1)}), bf16[64,104,128]{2,1,0:T(8,128)(2,1)S(1)}, u32[]{:S(2)}, u32[]{:S(2)}) %all-to-all-start) | async-done | bytes 1703968 | tf_op jit(solution)/shard_map/all_to_all | solution.py:480
  103.1 1.7 sort_units.1
  107.4 3.5 %collective-permute-start.3 = (bf16[64,48,128]{2,1,0:T(8,128)(2,1)}, bf16[64,48,128]{2,1,0:T(8,128)(2,1)}, u32[]{:S(2)}, u32[]{:S(2)}) collective-permute-start(bf16[64,48,128]{2,1,0:T(8,128)(2,1)} %get-tuple-element.14.block_ref), channel_id=1, source_target_pairs={{0,1},{1,0},{2,3},{3,2},{4,5},{5,4},{6,7},{7,6},{8,9},{9,8},{10,11... | collective-permute-start | bytes 2359304 | tf_op jit(solution)/shard_map/ppermute | solution.py:433
  111.0 3.2 %collective-permute-start.8 = (bf16[64,48,128]{2,1,0:T(8,128)(2,1)}, bf16[64,48,128]{2,1,0:T(8,128)(2,1)S(1)}, u32[]{:S(2)}, u32[]{:S(2)}) collective-permute-start(bf16[64,48,128]{2,1,0:T(8,128)(2,1)} %get-tuple-element.14.block_ref), channel_id=1, source_target_pairs={{0,64},{64,128},{128,192},{256,320},{320,384},{384,448},{1,65},{65... | collective-permute-start | bytes 2359304 | tf_op jit(solution)/shard_map/ppermute | solution.py:447
  114.2 3.7 %collective-permute-start.4 = (bf16[64,48,128]{2,1,0:T(8,128)(2,1)}, bf16[64,48,128]{2,1,0:T(8,128)(2,1)S(1)}, u32[]{:S(2)}, u32[]{:S(2)}) collective-permute-start(bf16[64,48,128]{2,1,0:T(8,128)(2,1)} %get-tuple-element.14.block_ref), channel_id=1, source_target_pairs={{0,2},{1,3},{2,4},{3,5},{4,6},{5,7},{6,8},{7,9},{8,10},{9,11},{10,... | collective-permute-start | bytes 2359304 | tf_op jit(solution)/shard_map/ppermute | solution.py:429
  119.5 1.9 choose_piece.1
  121.4 7.9 %collective-permute-start.7 = (bf16[16,48,128]{2,1,0:T(8,128)(2,1)}, bf16[16,48,128]{2,1,0:T(8,128)(2,1)S(1)}, u32[]{:S(2)}, u32[]{:S(2)}) collective-permute-start(bf16[16,48,128]{2,1,0:T(8,128)(2,1)} %get-tuple-element.19), channel_id=1, source_target_pairs={{0,256},{64,320},{128,384},{192,448},{256,0},{320,64},{384,128},{4... | collective-permute-start | bytes 589832 | tf_op jit(solution)/shard_map/ppermute | solution.py:450
  129.3 1.9 collective-permute-start.6
  131.3 4.6 %collective-permute-done.4.refs_1_ = bf16[64,48,128]{2,1,0:T(8,128)(2,1)S(1)} collective-permute-done((bf16[64,48,128]{2,1,0:T(8,128)(2,1)}, bf16[64,48,128]{2,1,0:T(8,128)(2,1)S(1)}, u32[]{:S(2)}, u32[]{:S(2)}) %collective-permute-start.4) | collective-permute-done | bytes 786464 | tf_op jit(solution)/shard_map/ppermute | solution.py:429
  135.9 15.4 %collective-permute-start.5 = (bf16[64,48,128]{2,1,0:T(8,128)(2,1)S(1)}, bf16[64,48,128]{2,1,0:T(8,128)(2,1)S(1)}, u32[]{:S(2)}, u32[]{:S(2)}) collective-permute-start(bf16[64,48,128]{2,1,0:T(8,128)(2,1)S(1)} %collective-permute-done.4.refs_1_), channel_id=1, source_target_pairs={{0,1},{1,0},{2,3},{3,2},{4,5},{5,4},{6,7},{7,6},{8,9},{9,8},{10,11... | collective-permute-start | bytes 2359304 | tf_op jit(solution)/shard_map/ppermute | solution.py:433
  151.3 13.4 %collective-permute-done.7.piece_ref.refs_2_ = bf16[16,48,128]{2,1,0:T(8,128)(2,1)S(1)} collective-permute-done((bf16[16,48,128]{2,1,0:T(8,128)(2,1)}, bf16[16,48,128]{2,1,0:T(8,128)(2,1)S(1)}, u32[]{:S(2)}, u32[]{:S(2)}) %collective-permute-start.7) | collective-permute-done | bytes 196640 | tf_op jit(solution)/shard_map/ppermute | solution.py:450
  165.4 1.8 cross.5.refs_3_
  167.2 1.8 cross.6.refs_2_.kept_ref
  169.0 5.9 %collective-permute-start.9 = (bf16[8,9,16,128]{3,2,1,0:T(8,128)(2,1)S(1)}, bf16[8,9,16,128]{3,2,1,0:T(8,128)(2,1)}, u32[]{:S(2)}, u32[]{:S(2)}) collective-permute-start(bf16[8,9,16,128]{3,2,1,0:T(8,128)(2,1)S(1)} %cross.6.refs_2_.kept_ref), channel_id=1, source_target_pairs={{0,2},{1,3},{2,4},{3,5},{4,6},{5,7},{6,8},{7,9},{8,10},{9,11},{10,... | collective-permute-start | bytes 884744 | tf_op jit(solution)/shard_map/ppermute | solution.py:429
  178.8 1.8 cross.7.refs_3_.two_ref
  180.6 2.9 %cross.8.refs_6_.one_ref = bf16[4,9,16,128]{3,2,1,0:T(8,128)(2,1)S(1)} custom-call(s32[1]{0:T(128)} %bitcast.flag_ref.core_ref, bf16[64,48,128]{2,1,0:T(8,128)(2,1)S(1)} %get-tuple-element.18.refs_0_, bf16[64,48,128]{2,1,0:T(8,128)(2,1)} %collective-permute-done.3.refs_1_, bf16[64,48,128]{2,1,0:T(8,128)(2,1)S(1)} %collective-permute-done.5.refs_2_, ...), custom_call_target="tpu_custom_call" | custom-call | flops 40000000 | bytes 1500000 | tf_op jit(solution)/shard_map/cross/pallas_call | solution.py:278
  184.9 6.0 %collective-permute-done.12.refs_5_ = bf16[16,48,128]{2,1,0:T(8,128)(2,1)} collective-permute-done((bf16[16,48,128]{2,1,0:T(8,128)(2,1)}, bf16[16,48,128]{2,1,0:T(8,128)(2,1)}, u32[]{:S(2)}, u32[]{:S(2)}) %collective-permute-start.12) | collective-permute-done | bytes 196640 | tf_op jit(solution)/shard_map/ppermute | solution.py:455
  190.9 2.9 %cross.9.across_ref = bf16[4,9,16,128]{3,2,1,0:T(8,128)(2,1)S(1)} custom-call(s32[1]{0:T(128)} %bitcast.7.flag_ref, bf16[64,48,128]{2,1,0:T(8,128)(2,1)S(1)} %get-tuple-element.18.refs_0_, bf16[64,48,128]{2,1,0:T(8,128)(2,1)S(1)} %collective-permute-done.8.refs_0_.refs_1_, bf16[16,48,128]{2,1,0:T(8,128)(2,1)S(1)} %copy-done.1, ...), custom_call_target="tpu_custom_call" | custom-call | flops 40000000 | bytes 1500000 | tf_op jit(solution)/shard_map/cross/pallas_call | solution.py:278
  193.8 6.7 %lag_series.1 = (bf16[2,4,9,2,2048]{4,3,2,1,0:T(2,128)(2,1)}, bf16[2,9,2,2048]{3,2,1,0:T(2,128)(2,1)}) custom-call(s32[1]{0:T(128)} %bitcast.flag_ref.core_ref, bf16[8,2048,256]{2,1,0:T(8,128)(2,1)} %lag_table.1.table_ref, bf16[4,9,16,128]{3,2,1,0:T(8,128)(2,1)S(1)} %cross.8.refs_6_.one_ref, bf16[4,9,16,128]{3,2,1,0:T(8,128)(2,1)S(1)} %cross.7.refs_3_.two_ref, ...), custom_call_target="tpu_custom_call" | custom-call | flops 1509949440 | bytes 12000000 | tf_op jit(solution)/shard_map/lag_series/pallas_call | solution.py:356
  (48 shorter events, 13.4 us)
Async XLA Ops:
  9.5 93.2 %all-to-all-start = ((bf16[64,104,128]{2,1,0:T(8,128)(2,1)}), bf16[64,104,128]{2,1,0:T(8,128)(2,1)S(1)}, u32[]{:S(2)}, u32[]{:S(2)}) async-start(bf16[64,104,128]{2,1,0:T(8,128)(2,1)} %whiten.1), calls=%async_computation | async-start | bytes 3407872 | tf_op jit(solution)/shard_map/all_to_all | solution.py:480
  104.8 9.4 %collective-permute-start = (bf16[16,48,128]{2,1,0:T(8,128)(2,1)}, bf16[16,48,128]{2,1,0:T(8,128)(2,1)S(1)}, u32[]{:S(2)}, u32[]{:S(2)}) collective-permute-start(bf16[16,48,128]{2,1,0:T(8,128)(2,1)} %get-tuple-element.15), channel_id=1, source_target_pairs={{192,0},{448,256},{193,1},{449,257},{194,2},{450,258},{195,3},{451... | collective-permute-start | bytes 589832 | tf_op jit(solution)/shard_map/ppermute | solution.py:440
  106.0 11.8 %collective-permute-start.1 = (bf16[16,48,128]{2,1,0:T(8,128)(2,1)S(1)}, bf16[16,48,128]{2,1,0:T(8,128)(2,1)S(1)}, u32[]{:S(2)}, u32[]{:S(2)}) collective-permute-start(bf16[16,48,128]{2,1,0:T(8,128)(2,1)S(1)} %get-tuple-element.16), channel_id=1, source_target_pairs={{192,64},{448,320},{193,65},{449,321},{194,66},{450,322},{195,67},... | collective-permute-start | bytes 589832 | tf_op jit(solution)/shard_map/ppermute | solution.py:440
  106.7 11.2 %collective-permute-start.2 = (bf16[16,48,128]{2,1,0:T(8,128)(2,1)S(1)}, bf16[16,48,128]{2,1,0:T(8,128)(2,1)S(1)}, u32[]{:S(2)}, u32[]{:S(2)}) collective-permute-start(bf16[16,48,128]{2,1,0:T(8,128)(2,1)S(1)} %get-tuple-element.17), channel_id=1, source_target_pairs={{192,128},{448,384},{193,129},{449,385},{194,130},{450,386},{195,1... | collective-permute-start | bytes 589832 | tf_op jit(solution)/shard_map/ppermute | solution.py:440
  107.4 57.3 %collective-permute-start.3 = (bf16[64,48,128]{2,1,0:T(8,128)(2,1)}, bf16[64,48,128]{2,1,0:T(8,128)(2,1)}, u32[]{:S(2)}, u32[]{:S(2)}) collective-permute-start(bf16[64,48,128]{2,1,0:T(8,128)(2,1)} %get-tuple-element.14.block_ref), channel_id=1, source_target_pairs={{0,1},{1,0},{2,3},{3,2},{4,5},{5,4},{6,7},{7,6},{8,9},{9,8},{10,11... | collective-permute-start | bytes 2359304 | tf_op jit(solution)/shard_map/ppermute | solution.py:433
  111.0 53.7 %collective-permute-start.8 = (bf16[64,48,128]{2,1,0:T(8,128)(2,1)}, bf16[64,48,128]{2,1,0:T(8,128)(2,1)S(1)}, u32[]{:S(2)}, u32[]{:S(2)}) collective-permute-start(bf16[64,48,128]{2,1,0:T(8,128)(2,1)} %get-tuple-element.14.block_ref), channel_id=1, source_target_pairs={{0,64},{64,128},{128,192},{256,320},{320,384},{384,448},{1,65},{65... | collective-permute-start | bytes 2359304 | tf_op jit(solution)/shard_map/ppermute | solution.py:447
  114.2 21.8 %collective-permute-start.4 = (bf16[64,48,128]{2,1,0:T(8,128)(2,1)}, bf16[64,48,128]{2,1,0:T(8,128)(2,1)S(1)}, u32[]{:S(2)}, u32[]{:S(2)}) collective-permute-start(bf16[64,48,128]{2,1,0:T(8,128)(2,1)} %get-tuple-element.14.block_ref), channel_id=1, source_target_pairs={{0,2},{1,3},{2,4},{3,5},{4,6},{5,7},{6,8},{7,9},{8,10},{9,11},{10,... | collective-permute-start | bytes 2359304 | tf_op jit(solution)/shard_map/ppermute | solution.py:429
  117.9 0.7 copy-start.2
  118.6 0.9 copy-start.3
  121.4 43.3 %collective-permute-start.7 = (bf16[16,48,128]{2,1,0:T(8,128)(2,1)}, bf16[16,48,128]{2,1,0:T(8,128)(2,1)S(1)}, u32[]{:S(2)}, u32[]{:S(2)}) collective-permute-start(bf16[16,48,128]{2,1,0:T(8,128)(2,1)} %get-tuple-element.19), channel_id=1, source_target_pairs={{0,256},{64,320},{128,384},{192,448},{256,0},{320,64},{384,128},{4... | collective-permute-start | bytes 589832 | tf_op jit(solution)/shard_map/ppermute | solution.py:450
  129.3 36.1 %collective-permute-start.6 = (bf16[64,48,128]{2,1,0:T(8,128)(2,1)S(1)}, bf16[64,48,128]{2,1,0:T(8,128)(2,1)S(1)}, u32[]{:S(2)}, u32[]{:S(2)}) collective-permute-start(bf16[64,48,128]{2,1,0:T(8,128)(2,1)S(1)} %get-tuple-element.18.refs_0_), channel_id=1, source_target_pairs={{0,62},{1,63},{2,0},{3,1},{4,2},{5,3},{6,4},{7,5},{8,6},{9,7},{10,... | collective-permute-start | bytes 2359304 | tf_op jit(solution)/shard_map/ppermute | solution.py:429
  135.9 31.3 %collective-permute-start.5 = (bf16[64,48,128]{2,1,0:T(8,128)(2,1)S(1)}, bf16[64,48,128]{2,1,0:T(8,128)(2,1)S(1)}, u32[]{:S(2)}, u32[]{:S(2)}) collective-permute-start(bf16[64,48,128]{2,1,0:T(8,128)(2,1)S(1)} %collective-permute-done.4.refs_1_), channel_id=1, source_target_pairs={{0,1},{1,0},{2,3},{3,2},{4,5},{5,4},{6,7},{7,6},{8,9},{9,8},{10,11... | collective-permute-start | bytes 2359304 | tf_op jit(solution)/shard_map/ppermute | solution.py:433
  164.7 0.7 copy-start
  169.0 24.8 %collective-permute-start.9 = (bf16[8,9,16,128]{3,2,1,0:T(8,128)(2,1)S(1)}, bf16[8,9,16,128]{3,2,1,0:T(8,128)(2,1)}, u32[]{:S(2)}, u32[]{:S(2)}) collective-permute-start(bf16[8,9,16,128]{3,2,1,0:T(8,128)(2,1)S(1)} %cross.6.refs_2_.kept_ref), channel_id=1, source_target_pairs={{0,2},{1,3},{2,4},{3,5},{4,6},{5,7},{6,8},{7,9},{8,10},{9,11},{10,... | collective-permute-start | bytes 884744 | tf_op jit(solution)/shard_map/ppermute | solution.py:429
  174.9 8.6 %collective-permute-start.10 = (bf16[16,48,128]{2,1,0:T(8,128)(2,1)}, bf16[16,48,128]{2,1,0:T(8,128)(2,1)}, u32[]{:S(2)}, u32[]{:S(2)}) collective-permute-start(bf16[16,48,128]{2,1,0:T(8,128)(2,1)} %relay_piece.1.refs_2_), channel_id=1, source_target_pairs={{64,0},{320,256},{65,1},{321,257},{66,2},{322,258},{67,3},{323,259... | collective-permute-start | bytes 589832 | tf_op jit(solution)/shard_map/ppermute | solution.py:455
  176.2 8.7 %collective-permute-start.11 = (bf16[16,48,128]{2,1,0:T(8,128)(2,1)}, bf16[16,48,128]{2,1,0:T(8,128)(2,1)}, u32[]{:S(2)}, u32[]{:S(2)}) collective-permute-start(bf16[16,48,128]{2,1,0:T(8,128)(2,1)} %relay_piece.1.refs_2_), channel_id=1, source_target_pairs={{128,0},{384,256},{129,1},{385,257},{130,2},{386,258},{131,3},{387... | collective-permute-start | bytes 589832 | tf_op jit(solution)/shard_map/ppermute | solution.py:455
  177.5 13.5 %collective-permute-start.12 = (bf16[16,48,128]{2,1,0:T(8,128)(2,1)}, bf16[16,48,128]{2,1,0:T(8,128)(2,1)}, u32[]{:S(2)}, u32[]{:S(2)}) collective-permute-start(bf16[16,48,128]{2,1,0:T(8,128)(2,1)} %relay_piece.1.refs_2_), channel_id=1, source_target_pairs={{192,0},{448,256},{193,1},{449,257},{194,2},{450,258},{195,3},{451... | collective-permute-start | bytes 589832 | tf_op jit(solution)/shard_map/ppermute | solution.py:455
  180.6 10.4 %copy-start.1 = (bf16[16,48,128]{2,1,0:T(8,128)(2,1)S(1)}, bf16[16,48,128]{2,1,0:T(8,128)(2,1)}, u32[]{:S(2)}) copy-start(bf16[16,48,128]{2,1,0:T(8,128)(2,1)} %copy-done) | copy-start | bytes 589828

commit v8 on v7

--- a/solution.py
+++ b/solution.py
@@ -128,7 +128,7 @@
             jax.ShapeDtypeStruct((marks.shape[0], size, LANES), jnp.bfloat16) for size in sizes
         ],
         scratch_shapes=[pltpu.VMEM((GROUP * FH + 2 * FH, LANES), jnp.float32)],
-        compiler_params=pltpu.CompilerParams(vmem_limit_bytes=16 * 1024 * 1024),
+        compiler_params=pltpu.CompilerParams(vmem_limit_bytes=8 * 1024 * 1024),
         cost_estimate=pl.CostEstimate(flops=200_000_000, bytes_accessed=4_000_000, transcendentals=0),
         name="whiten",
     )(source, band, inverse, archive, marks)
@@ -155,7 +155,7 @@
         in_specs=[SMEM, VMEM],
         out_specs=[VMEM for _ in shapes],
         out_shape=[jax.ShapeDtypeStruct(shape, jnp.bfloat16) for shape in shapes],
-        compiler_params=pltpu.CompilerParams(vmem_limit_bytes=16 * 1024 * 1024),
+        compiler_params=pltpu.CompilerParams(vmem_limit_bytes=6 * 1024 * 1024),
         cost_estimate=pl.CostEstimate(flops=0, bytes_accessed=3_000_000, transcendentals=0),
         name="sort_units",
     )(source, got)
@@ -185,7 +185,7 @@
             jax.ShapeDtypeStruct(pieces[0].shape, jnp.bfloat16),
             jax.ShapeDtypeStruct(block.shape, jnp.bfloat16),
         ],
-        compiler_params=pltpu.CompilerParams(vmem_limit_bytes=16 * 1024 * 1024),
+        compiler_params=pltpu.CompilerParams(vmem_limit_bytes=6 * 1024 * 1024),
         cost_estimate=pl.CostEstimate(flops=20_000_000_000, bytes_accessed=2_000_000, transcendentals=0),
         name="choose_piece",
     )(plane.reshape(1), block, *pieces)
@@ -201,7 +201,7 @@
         in_specs=[VMEM] + [pl.BlockSpec(memory_space=pl.ANY)] * len(after),
         out_specs=VMEM,
         out_shape=jax.ShapeDtypeStruct(piece.shape, jnp.bfloat16),
-        compiler_params=pltpu.CompilerParams(vmem_limit_bytes=8 * 1024 * 1024),
+        compiler_params=pltpu.CompilerParams(vmem_limit_bytes=4 * 1024 * 1024),
         cost_estimate=pl.CostEstimate(flops=20_000_000_000, bytes_accessed=400_000, transcendentals=0),
         name="relay_piece",
     )(piece, *after)
@@ -284,7 +284,7 @@
         + [pl.BlockSpec(memory_space=pl.ANY)] * len(after),
         out_specs=VMEM,
         out_shape=jax.ShapeDtypeStruct(shape, jnp.bfloat16),
-        compiler_params=pltpu.CompilerParams(vmem_limit_bytes=24 * 1024 * 1024),
+        compiler_params=pltpu.CompilerParams(vmem_limit_bytes=8 * 1024 * 1024),
         cost_estimate=pl.CostEstimate(
             flops=len(plan) * 40_000_000, bytes_accessed=len(plan) * 1_500_000, transcendentals=0
         ),
@@ -371,7 +371,7 @@
             pltpu.VMEM((LAGS // COLUMNS, 2 * F, COLUMNS), jnp.bfloat16),
             pltpu.SemaphoreType.DMA((LAGS // COLUMNS,)),
         ],
-        compiler_params=pltpu.CompilerParams(vmem_limit_bytes=32 * 1024 * 1024),
+        compiler_params=pltpu.CompilerParams(vmem_limit_bytes=18 * 1024 * 1024),
         cost_estimate=pl.CostEstimate(
             flops=2 * ALL_ROWS * 2 * F * LAGS, bytes_accessed=12_000_000, transcendentals=0
         ),
@@ -418,7 +418,7 @@
         ],
         out_specs=pl.BlockSpec((1, F, COLUMNS), lambda s, n: (n, s, 0)),
         out_shape=pltpu.HBM((LAGS // COLUMNS, 2 * F, COLUMNS), jnp.bfloat16),
-        compiler_params=pltpu.CompilerParams(vmem_limit_bytes=16 * 1024 * 1024),
+        compiler_params=pltpu.CompilerParams(vmem_limit_bytes=8 * 1024 * 1024),
         cost_estimate=pl.CostEstimate(flops=16_000_000, bytes_accessed=12_000_000, transcendentals=0),
         name="lag_table",
     )(fine, coarse)

time: 201 us -> 201 us (level)
  no operation moved by 1% of the time
where the time goes in v8:
time: 201 us
  waiting for transfers between devices  88.8 us (44%)
  starting transfers between devices  63.8 us (32%)
  Pallas kernels  35.6 us (18%)
  other arithmetic  5.74 us (3%)
  local copies, waits for them, and re-layouts  4.96 us (2%)
    all_to_all x1, waiting for transfers between devices, body(): lax.all_to_all(part, 'blk', split_axis=0, concat_axis=0, tiled=True)  63.4 us
    ppermute x2, starting transfers between devices, swapped(): lax.ppermute(block, 'blk', [(i, i ^ 1) for i in range(lax.axis_size('blk'...  19 us
    all_to_all x1, starting transfers between devices, body(): lax.all_to_all(part, 'blk', split_axis=0, concat_axis=0, tiled=True)  15.8 us
    ppermute x1, waiting for transfers between devices, from_previous_region(): lax.ppermute(piece, 'region', [(i, (i + planes) % regions) for i in range...  13.4 us
    ppermute x3, starting transfers between devices, shifted(): lax.ppermute(block, axis, [(i, (i + by) % size) for i in range(size)])  11.5 us
    pallas_call x5, Pallas kernels, cross(): pl.pallas_call(functools.partial(cross_kernel, chunk, plan, tuple((len(bl...  11.1 us
    pallas_call x1, Pallas kernels, make_table(): pl.pallas_call(table_kernel, grid=(2, LAGS // COLUMNS), in_specs=[pl.Bloc...  9.35 us
    ppermute x1, starting transfers between devices, from_previous_region(): lax.ppermute(piece, 'region', [(i, (i + planes) % regions) for i in range...  7.93 us
  transfers between devices with their start and end apart: 14, of which 5 were waited for; matrix products, arithmetic and copies ran while one was open for 2% of the time, Pallas kernels for 11%

profile of v8, /device:TPU:57, one launch (start us, length us, event | category | flops | bytes accessed | tf_op | source)
XLA Modules:
  0.0 200.5 jit_solution(1591925224394599311)
XLA Ops:
  2.4 1.9 copy.11
  5.5 4.0 %whiten.1 = bf16[64,104,128]{2,1,0:T(8,128)(2,1)} custom-call(s32[128]{0:T(128)S(1)} %min.27.source_ref, bf16[256,128]{1,0:T(8,128)(2,1)S(1)} %add_convert_fusion.band_ref, f32[8,128]{1,0:T(8,128)S(1)} %convert_divide_fusion.inverse_ref, bf16[128,48,128]{2,1,0:T(8,128)(2,1)S(1)} %copy.12.archive_ref, bf16[64,8,128]{2,1,0:T(8,128)(2,1)S(1)} %broadcast_in_dim.91.mark_ref), custom_call_target="tpu_custom_call" | custom-call | flops 200000000 | bytes 4000000 | tf_op jit(solution)/shard_map/whiten/pallas_call | solution.py:123
  9.5 15.8 %all-to-all-start = ((bf16[64,104,128]{2,1,0:T(8,128)(2,1)}), bf16[64,104,128]{2,1,0:T(8,128)(2,1)S(1)}, u32[]{:S(2)}, u32[]{:S(2)}) async-start(bf16[64,104,128]{2,1,0:T(8,128)(2,1)} %whiten.1), calls=%async_computation | async-start | bytes 3407872 | tf_op jit(solution)/shard_map/all_to_all | solution.py:480
  25.7 4.1 %fusion.7 = (f32[1,128,2048]{2,1,0:T(8,128)S(1)}, f32[1,128,2048]{2,1,0:T(8,128)S(1)}) fusion(s32[2048]{0:T(1024)S(1)} %iota_add_fusion), kind=kLoop, calls=%fused_computation.11 | loop fusion | flops 3670016 | bytes 2105344 | tf_op jit(solution)/shard_map/cos | solution.py:408
  30.0 9.3 %lag_table.1.table_ref = bf16[8,2048,256]{2,1,0:T(8,128)(2,1)} custom-call(f32[2,128,2048]{2,1,0:T(8,128)S(1)} %pad_maximum_fusion.fine_ref, f32[2,8,2048]{2,1,0:T(8,128)S(1)} %pad_maximum_fusion.1.coarse_ref), custom_call_target="tpu_custom_call" | custom-call | flops 16000000 | bytes 12000000 | tf_op jit(solution)/shard_map/lag_table/pallas_call | solution.py:412
  39.4 63.4 %all-to-all-done.got_ref = bf16[64,104,128]{2,1,0:T(8,128)(2,1)S(1)} async-done(((bf16[64,104,128]{2,1,0:T(8,128)(2,1)}), bf16[64,104,128]{2,1,0:T(8,128)(2,1)S(1)}, u32[]{:S(2)}, u32[]{:S(2)}) %all-to-all-start) | async-done | bytes 1703968 | tf_op jit(solution)/shard_map/all_to_all | solution.py:480
  103.1 1.7 sort_units.1
  107.4 3.5 %collective-permute-start.3 = (bf16[64,48,128]{2,1,0:T(8,128)(2,1)}, bf16[64,48,128]{2,1,0:T(8,128)(2,1)}, u32[]{:S(2)}, u32[]{:S(2)}) collective-permute-start(bf16[64,48,128]{2,1,0:T(8,128)(2,1)} %get-tuple-element.14.block_ref), channel_id=1, source_target_pairs={{0,1},{1,0},{2,3},{3,2},{4,5},{5,4},{6,7},{7,6},{8,9},{9,8},{10,11... | collective-permute-start | bytes 2359304 | tf_op jit(solution)/shard_map/ppermute | solution.py:433
  111.0 3.2 %collective-permute-start.8 = (bf16[64,48,128]{2,1,0:T(8,128)(2,1)}, bf16[64,48,128]{2,1,0:T(8,128)(2,1)S(1)}, u32[]{:S(2)}, u32[]{:S(2)}) collective-permute-start(bf16[64,48,128]{2,1,0:T(8,128)(2,1)} %get-tuple-element.14.block_ref), channel_id=1, source_target_pairs={{0,64},{64,128},{128,192},{256,320},{320,384},{384,448},{1,65},{65... | collective-permute-start | bytes 2359304 | tf_op jit(solution)/shard_map/ppermute | solution.py:447
  114.2 3.7 %collective-permute-start.4 = (bf16[64,48,128]{2,1,0:T(8,128)(2,1)}, bf16[64,48,128]{2,1,0:T(8,128)(2,1)S(1)}, u32[]{:S(2)}, u32[]{:S(2)}) collective-permute-start(bf16[64,48,128]{2,1,0:T(8,128)(2,1)} %get-tuple-element.14.block_ref), channel_id=1, source_target_pairs={{0,2},{1,3},{2,4},{3,5},{4,6},{5,7},{6,8},{7,9},{8,10},{9,11},{10,... | collective-permute-start | bytes 2359304 | tf_op jit(solution)/shard_map/ppermute | solution.py:429
  119.5 1.9 choose_piece.1
  121.4 7.9 %collective-permute-start.7 = (bf16[16,48,128]{2,1,0:T(8,128)(2,1)}, bf16[16,48,128]{2,1,0:T(8,128)(2,1)S(1)}, u32[]{:S(2)}, u32[]{:S(2)}) collective-permute-start(bf16[16,48,128]{2,1,0:T(8,128)(2,1)} %get-tuple-element.19), channel_id=1, source_target_pairs={{0,256},{64,320},{128,384},{192,448},{256,0},{320,64},{384,128},{4... | collective-permute-start | bytes 589832 | tf_op jit(solution)/shard_map/ppermute | solution.py:450
  129.3 1.9 collective-permute-start.6
  131.3 4.6 %collective-permute-done.4.refs_1_ = bf16[64,48,128]{2,1,0:T(8,128)(2,1)S(1)} collective-permute-done((bf16[64,48,128]{2,1,0:T(8,128)(2,1)}, bf16[64,48,128]{2,1,0:T(8,128)(2,1)S(1)}, u32[]{:S(2)}, u32[]{:S(2)}) %collective-permute-start.4) | collective-permute-done | bytes 786464 | tf_op jit(solution)/shard_map/ppermute | solution.py:429
  135.9 15.4 %collective-permute-start.5 = (bf16[64,48,128]{2,1,0:T(8,128)(2,1)S(1)}, bf16[64,48,128]{2,1,0:T(8,128)(2,1)S(1)}, u32[]{:S(2)}, u32[]{:S(2)}) collective-permute-start(bf16[64,48,128]{2,1,0:T(8,128)(2,1)S(1)} %collective-permute-done.4.refs_1_), channel_id=1, source_target_pairs={{0,1},{1,0},{2,3},{3,2},{4,5},{5,4},{6,7},{7,6},{8,9},{9,8},{10,11... | collective-permute-start | bytes 2359304 | tf_op jit(solution)/shard_map/ppermute | solution.py:433
  151.3 13.4 %collective-permute-done.7.piece_ref.refs_2_ = bf16[16,48,128]{2,1,0:T(8,128)(2,1)S(1)} collective-permute-done((bf16[16,48,128]{2,1,0:T(8,128)(2,1)}, bf16[16,48,128]{2,1,0:T(8,128)(2,1)S(1)}, u32[]{:S(2)}, u32[]{:S(2)}) %collective-permute-start.7) | collective-permute-done | bytes 196640 | tf_op jit(solution)/shard_map/ppermute | solution.py:450
  165.4 1.8 cross.5.refs_3_
  167.2 1.8 cross.6.refs_2_.kept_ref
  169.0 5.9 %collective-permute-start.9 = (bf16[8,9,16,128]{3,2,1,0:T(8,128)(2,1)S(1)}, bf16[8,9,16,128]{3,2,1,0:T(8,128)(2,1)}, u32[]{:S(2)}, u32[]{:S(2)}) collective-permute-start(bf16[8,9,16,128]{3,2,1,0:T(8,128)(2,1)S(1)} %cross.6.refs_2_.kept_ref), channel_id=1, source_target_pairs={{0,2},{1,3},{2,4},{3,5},{4,6},{5,7},{6,8},{7,9},{8,10},{9,11},{10,... | collective-permute-start | bytes 884744 | tf_op jit(solution)/shard_map/ppermute | solution.py:429
  178.8 1.8 cross.7.refs_3_.two_ref
  180.6 2.9 %cross.8.refs_6_.one_ref = bf16[4,9,16,128]{3,2,1,0:T(8,128)(2,1)S(1)} custom-call(s32[1]{0:T(128)} %bitcast.flag_ref.core_ref, bf16[64,48,128]{2,1,0:T(8,128)(2,1)S(1)} %get-tuple-element.18.refs_0_, bf16[64,48,128]{2,1,0:T(8,128)(2,1)} %collective-permute-done.3.refs_1_, bf16[64,48,128]{2,1,0:T(8,128)(2,1)S(1)} %collective-permute-done.5.refs_2_, ...), custom_call_target="tpu_custom_call" | custom-call | flops 40000000 | bytes 1500000 | tf_op jit(solution)/shard_map/cross/pallas_call | solution.py:278
  184.9 6.0 %collective-permute-done.12.refs_5_ = bf16[16,48,128]{2,1,0:T(8,128)(2,1)} collective-permute-done((bf16[16,48,128]{2,1,0:T(8,128)(2,1)}, bf16[16,48,128]{2,1,0:T(8,128)(2,1)}, u32[]{:S(2)}, u32[]{:S(2)}) %collective-permute-start.12) | collective-permute-done | bytes 196640 | tf_op jit(solution)/shard_map/ppermute | solution.py:455
  190.9 2.9 %cross.9.across_ref = bf16[4,9,16,128]{3,2,1,0:T(8,128)(2,1)S(1)} custom-call(s32[1]{0:T(128)} %bitcast.7.flag_ref, bf16[64,48,128]{2,1,0:T(8,128)(2,1)S(1)} %get-tuple-element.18.refs_0_, bf16[64,48,128]{2,1,0:T(8,128)(2,1)S(1)} %collective-permute-done.8.refs_0_.refs_1_, bf16[16,48,128]{2,1,0:T(8,128)(2,1)S(1)} %copy-done.1, ...), custom_call_target="tpu_custom_call" | custom-call | flops 40000000 | bytes 1500000 | tf_op jit(solution)/shard_map/cross/pallas_call | solution.py:278
  193.8 6.7 %lag_series.1 = (bf16[2,4,9,2,2048]{4,3,2,1,0:T(2,128)(2,1)}, bf16[2,9,2,2048]{3,2,1,0:T(2,128)(2,1)}) custom-call(s32[1]{0:T(128)} %bitcast.flag_ref.core_ref, bf16[8,2048,256]{2,1,0:T(8,128)(2,1)} %lag_table.1.table_ref, bf16[4,9,16,128]{3,2,1,0:T(8,128)(2,1)S(1)} %cross.8.refs_6_.one_ref, bf16[4,9,16,128]{3,2,1,0:T(8,128)(2,1)S(1)} %cross.7.refs_3_.two_ref, ...), custom_call_target="tpu_custom_call" | custom-call | flops 1509949440 | bytes 12000000 | tf_op jit(solution)/shard_map/lag_series/pallas_call | solution.py:356
  (48 shorter events, 13.4 us)
Async XLA Ops:
  9.5 93.2 %all-to-all-start = ((bf16[64,104,128]{2,1,0:T(8,128)(2,1)}), bf16[64,104,128]{2,1,0:T(8,128)(2,1)S(1)}, u32[]{:S(2)}, u32[]{:S(2)}) async-start(bf16[64,104,128]{2,1,0:T(8,128)(2,1)} %whiten.1), calls=%async_computation | async-start | bytes 3407872 | tf_op jit(solution)/shard_map/all_to_all | solution.py:480
  104.8 9.4 %collective-permute-start = (bf16[16,48,128]{2,1,0:T(8,128)(2,1)}, bf16[16,48,128]{2,1,0:T(8,128)(2,1)S(1)}, u32[]{:S(2)}, u32[]{:S(2)}) collective-permute-start(bf16[16,48,128]{2,1,0:T(8,128)(2,1)} %get-tuple-element.15), channel_id=1, source_target_pairs={{192,0},{448,256},{193,1},{449,257},{194,2},{450,258},{195,3},{451... | collective-permute-start | bytes 589832 | tf_op jit(solution)/shard_map/ppermute | solution.py:440
  106.0 11.8 %collective-permute-start.1 = (bf16[16,48,128]{2,1,0:T(8,128)(2,1)S(1)}, bf16[16,48,128]{2,1,0:T(8,128)(2,1)S(1)}, u32[]{:S(2)}, u32[]{:S(2)}) collective-permute-start(bf16[16,48,128]{2,1,0:T(8,128)(2,1)S(1)} %get-tuple-element.16), channel_id=1, source_target_pairs={{192,64},{448,320},{193,65},{449,321},{194,66},{450,322},{195,67},... | collective-permute-start | bytes 589832 | tf_op jit(solution)/shard_map/ppermute | solution.py:440
  106.7 11.2 %collective-permute-start.2 = (bf16[16,48,128]{2,1,0:T(8,128)(2,1)S(1)}, bf16[16,48,128]{2,1,0:T(8,128)(2,1)S(1)}, u32[]{:S(2)}, u32[]{:S(2)}) collective-permute-start(bf16[16,48,128]{2,1,0:T(8,128)(2,1)S(1)} %get-tuple-element.17), channel_id=1, source_target_pairs={{192,128},{448,384},{193,129},{449,385},{194,130},{450,386},{195,1... | collective-permute-start | bytes 589832 | tf_op jit(solution)/shard_map/ppermute | solution.py:440
  107.4 57.3 %collective-permute-start.3 = (bf16[64,48,128]{2,1,0:T(8,128)(2,1)}, bf16[64,48,128]{2,1,0:T(8,128)(2,1)}, u32[]{:S(2)}, u32[]{:S(2)}) collective-permute-start(bf16[64,48,128]{2,1,0:T(8,128)(2,1)} %get-tuple-element.14.block_ref), channel_id=1, source_target_pairs={{0,1},{1,0},{2,3},{3,2},{4,5},{5,4},{6,7},{7,6},{8,9},{9,8},{10,11... | collective-permute-start | bytes 2359304 | tf_op jit(solution)/shard_map/ppermute | solution.py:433
  111.0 53.7 %collective-permute-start.8 = (bf16[64,48,128]{2,1,0:T(8,128)(2,1)}, bf16[64,48,128]{2,1,0:T(8,128)(2,1)S(1)}, u32[]{:S(2)}, u32[]{:S(2)}) collective-permute-start(bf16[64,48,128]{2,1,0:T(8,128)(2,1)} %get-tuple-element.14.block_ref), channel_id=1, source_target_pairs={{0,64},{64,128},{128,192},{256,320},{320,384},{384,448},{1,65},{65... | collective-permute-start | bytes 2359304 | tf_op jit(solution)/shard_map/ppermute | solution.py:447
  114.2 21.8 %collective-permute-start.4 = (bf16[64,48,128]{2,1,0:T(8,128)(2,1)}, bf16[64,48,128]{2,1,0:T(8,128)(2,1)S(1)}, u32[]{:S(2)}, u32[]{:S(2)}) collective-permute-start(bf16[64,48,128]{2,1,0:T(8,128)(2,1)} %get-tuple-element.14.block_ref), channel_id=1, source_target_pairs={{0,2},{1,3},{2,4},{3,5},{4,6},{5,7},{6,8},{7,9},{8,10},{9,11},{10,... | collective-permute-start | bytes 2359304 | tf_op jit(solution)/shard_map/ppermute | solution.py:429
  117.9 0.7 copy-start.2
  118.6 0.9 copy-start.3
  121.4 43.3 %collective-permute-start.7 = (bf16[16,48,128]{2,1,0:T(8,128)(2,1)}, bf16[16,48,128]{2,1,0:T(8,128)(2,1)S(1)}, u32[]{:S(2)}, u32[]{:S(2)}) collective-permute-start(bf16[16,48,128]{2,1,0:T(8,128)(2,1)} %get-tuple-element.19), channel_id=1, source_target_pairs={{0,256},{64,320},{128,384},{192,448},{256,0},{320,64},{384,128},{4... | collective-permute-start | bytes 589832 | tf_op jit(solution)/shard_map/ppermute | solution.py:450
  129.3 36.1 %collective-permute-start.6 = (bf16[64,48,128]{2,1,0:T(8,128)(2,1)S(1)}, bf16[64,48,128]{2,1,0:T(8,128)(2,1)S(1)}, u32[]{:S(2)}, u32[]{:S(2)}) collective-permute-start(bf16[64,48,128]{2,1,0:T(8,128)(2,1)S(1)} %get-tuple-element.18.refs_0_), channel_id=1, source_target_pairs={{0,62},{1,63},{2,0},{3,1},{4,2},{5,3},{6,4},{7,5},{8,6},{9,7},{10,... | collective-permute-start | bytes 2359304 | tf_op jit(solution)/shard_map/ppermute | solution.py:429
  135.9 31.3 %collective-permute-start.5 = (bf16[64,48,128]{2,1,0:T(8,128)(2,1)S(1)}, bf16[64,48,128]{2,1,0:T(8,128)(2,1)S(1)}, u32[]{:S(2)}, u32[]{:S(2)}) collective-permute-start(bf16[64,48,128]{2,1,0:T(8,128)(2,1)S(1)} %collective-permute-done.4.refs_1_), channel_id=1, source_target_pairs={{0,1},{1,0},{2,3},{3,2},{4,5},{5,4},{6,7},{7,6},{8,9},{9,8},{10,11... | collective-permute-start | bytes 2359304 | tf_op jit(solution)/shard_map/ppermute | solution.py:433
  164.7 0.7 copy-start
  169.0 24.8 %collective-permute-start.9 = (bf16[8,9,16,128]{3,2,1,0:T(8,128)(2,1)S(1)}, bf16[8,9,16,128]{3,2,1,0:T(8,128)(2,1)}, u32[]{:S(2)}, u32[]{:S(2)}) collective-permute-start(bf16[8,9,16,128]{3,2,1,0:T(8,128)(2,1)S(1)} %cross.6.refs_2_.kept_ref), channel_id=1, source_target_pairs={{0,2},{1,3},{2,4},{3,5},{4,6},{5,7},{6,8},{7,9},{8,10},{9,11},{10,... | collective-permute-start | bytes 884744 | tf_op jit(solution)/shard_map/ppermute | solution.py:429
  174.9 8.6 %collective-permute-start.10 = (bf16[16,48,128]{2,1,0:T(8,128)(2,1)}, bf16[16,48,128]{2,1,0:T(8,128)(2,1)}, u32[]{:S(2)}, u32[]{:S(2)}) collective-permute-start(bf16[16,48,128]{2,1,0:T(8,128)(2,1)} %relay_piece.1.refs_2_), channel_id=1, source_target_pairs={{64,0},{320,256},{65,1},{321,257},{66,2},{322,258},{67,3},{323,259... | collective-permute-start | bytes 589832 | tf_op jit(solution)/shard_map/ppermute | solution.py:455
  176.2 8.7 %collective-permute-start.11 = (bf16[16,48,128]{2,1,0:T(8,128)(2,1)}, bf16[16,48,128]{2,1,0:T(8,128)(2,1)}, u32[]{:S(2)}, u32[]{:S(2)}) collective-permute-start(bf16[16,48,128]{2,1,0:T(8,128)(2,1)} %relay_piece.1.refs_2_), channel_id=1, source_target_pairs={{128,0},{384,256},{129,1},{385,257},{130,2},{386,258},{131,3},{387... | collective-permute-start | bytes 589832 | tf_op jit(solution)/shard_map/ppermute | solution.py:455
  177.5 13.5 %collective-permute-start.12 = (bf16[16,48,128]{2,1,0:T(8,128)(2,1)}, bf16[16,48,128]{2,1,0:T(8,128)(2,1)}, u32[]{:S(2)}, u32[]{:S(2)}) collective-permute-start(bf16[16,48,128]{2,1,0:T(8,128)(2,1)} %relay_piece.1.refs_2_), channel_id=1, source_target_pairs={{192,0},{448,256},{193,1},{449,257},{194,2},{450,258},{195,3},{451... | collective-permute-start | bytes 589832 | tf_op jit(solution)/shard_map/ppermute | solution.py:455
  180.6 10.4 %copy-start.1 = (bf16[16,48,128]{2,1,0:T(8,128)(2,1)S(1)}, bf16[16,48,128]{2,1,0:T(8,128)(2,1)}, u32[]{:S(2)}) copy-start(bf16[16,48,128]{2,1,0:T(8,128)(2,1)} %copy-done) | copy-start | bytes 589828

commit v9 on v8

--- a/solution.py
+++ b/solution.py
@@ -162,9 +162,8 @@
 
 
 def choose_kernel(plane_ref, block_ref, *refs):
-    pieces, (piece_ref, out_ref) = refs[:-2], refs[-2:]
+    pieces, piece_ref = refs[:-1], refs[-1]
     last = len(pieces)
-    out_ref[...] = block_ref[...]
     for plane, ref in enumerate(pieces):
 
         @pl.when(plane_ref[0] == plane)
@@ -180,11 +179,8 @@
     return pl.pallas_call(
         choose_kernel,
         in_specs=[SMEM] + [VMEM] * (1 + len(pieces)),
-        out_specs=[VMEM, VMEM],
-        out_shape=[
-            jax.ShapeDtypeStruct(pieces[0].shape, jnp.bfloat16),
-            jax.ShapeDtypeStruct(block.shape, jnp.bfloat16),
-        ],
+        out_specs=VMEM,
+        out_shape=jax.ShapeDtypeStruct(pieces[0].shape, jnp.bfloat16),
         compiler_params=pltpu.CompilerParams(vmem_limit_bytes=6 * 1024 * 1024),
         cost_estimate=pl.CostEstimate(flops=20_000_000_000, bytes_accessed=2_000_000, transcendentals=0),
         name="choose_piece",
@@ -495,11 +491,11 @@
     plane = lax.axis_index("region") % planes
     edge = (plane == 0).astype(jnp.int32)
     core = lax.axis_index("blk") & 1
-    early, *pieces = sort_units(place, got[0], 3 * TILE, planes - 1)
-    piece, block = choose(plane, early, spread(pieces))
-    twin = swapped(early)
-    near, far, passed = from_previous_region(early, piece, planes, twin)
-    two = shifted(early, "blk", 2)
+    block, *pieces = sort_units(place, got[0], 3 * TILE, planes - 1)
+    piece = choose(plane, block, spread(pieces))
+    twin = swapped(block)
+    near, far, passed = from_previous_region(block, piece, planes, twin)
+    two = shifted(block, "blk", 2)
     ahead = shifted(block, "blk", -2)
     beside = swapped(two)
     own, twin, two, ahead, beside, near, far = (

time: 201 us -> 197 us (0.980)
  waiting for transfers between devices: 88.8 us -> 81.4 us
  starting transfers between devices: 63.8 us -> 68.9 us
  Pallas kernels: 35.6 us -> 33 us
    ppermute x3, waiting for transfers between devices: 4.65 us -> 0.56 us  [shifted(): lax.ppermute(block, axis, [(i, (i + by) % size) for i in range(size)])]
    ppermute x2, starting transfers between devices: 19 us -> 22.9 us  [swapped(): lax.ppermute(block, 'blk', [(i, i ^ 1) for i in range(lax.axis_size('blk'...]
    ppermute x3, waiting for transfers between devices: 7.4 us -> 4.31 us  [from_previous_region(): lax.ppermute(piece, 'region', [(n + plane, n) for n in range(0, regions,...]
  transfers between devices with their start and end apart: 14 -> 14, of which waited for: 5 -> 4; matrix products, arithmetic and copies ran while one was open for 2% -> 2% of each run, Pallas kernels for 11% -> 10%
where the time goes in v9:
time: 197 us; the launch traced here: 195 us
  waiting for transfers between devices  81.4 us (41%)
  starting transfers between devices  68.9 us (35%)
  Pallas kernels  33 us (17%)
  other arithmetic  5.74 us (3%)
  local copies, waits for them, and re-layouts  4.61 us (2%)
    all_to_all x1, waiting for transfers between devices, body(): lax.all_to_all(part, 'blk', split_axis=0, concat_axis=0, tiled=True)  63.4 us
    ppermute x2, starting transfers between devices, swapped(): lax.ppermute(block, 'blk', [(i, i ^ 1) for i in range(lax.axis_size('blk'...  22.9 us
    all_to_all x1, starting transfers between devices, body(): lax.all_to_all(part, 'blk', split_axis=0, concat_axis=0, tiled=True)  15.8 us
    ppermute x1, waiting for transfers between devices, from_previous_region(): lax.ppermute(piece, 'region', [(i, (i + planes) % regions) for i in range...  13.1 us
    ppermute x3, starting transfers between devices, shifted(): lax.ppermute(block, axis, [(i, (i + by) % size) for i in range(size)])  12.6 us
    pallas_call x5, Pallas kernels, cross(): pl.pallas_call(functools.partial(cross_kernel, chunk, plan, tuple((len(bl...  11.1 us
    pallas_call x1, Pallas kernels, make_table(): pl.pallas_call(table_kernel, grid=(2, LAGS // COLUMNS), in_specs=[pl.Bloc...  9.33 us
    ppermute x1, starting transfers between devices, from_previous_region(): lax.ppermute(piece, 'region', [(i, (i + planes) % regions) for i in range...  7.93 us
  transfers between devices with their start and end apart: 14, of which 4 were waited for; matrix products, arithmetic and copies ran while one was open for 2% of the time, Pallas kernels for 10%

profile of v9, /device:TPU:57, one launch (start us, length us, event | category | flops | bytes accessed | tf_op | source)
XLA Modules:
  0.0 195.4 jit_solution(17383534902362307882)
XLA Ops:
  2.4 1.9 copy.11
  5.5 2.8 %whiten.1 = bf16[64,104,128]{2,1,0:T(8,128)(2,1)S(1)} custom-call(s32[128]{0:T(128)S(1)} %min.27.source_ref, bf16[256,128]{1,0:T(8,128)(2,1)S(1)} %add_convert_fusion.band_ref, f32[8,128]{1,0:T(8,128)S(1)} %convert_divide_fusion.inverse_ref, bf16[128,48,128]{2,1,0:T(8,128)(2,1)S(1)} %copy.12.archive_ref, bf16[64,8,128]{2,1,0:T(8,128)(2,1)S(1)} %broadcast_in_dim.91.mark_ref), custom_call_target="tpu_custom_call" | custom-call | flops 200000000 | bytes 4000000 | tf_op jit(solution)/shard_map/whiten/pallas_call | solution.py:123
  9.5 15.8 %all-to-all-start = ((bf16[64,104,128]{2,1,0:T(8,128)(2,1)}), bf16[64,104,128]{2,1,0:T(8,128)(2,1)S(1)}, u32[]{:S(2)}, u32[]{:S(2)}) async-start(bf16[64,104,128]{2,1,0:T(8,128)(2,1)} %copy-done), calls=%async_computation | async-start | bytes 3407872 | tf_op jit(solution)/shard_map/all_to_all | solution.py:476
  25.7 4.1 %fusion.7 = (f32[1,128,2048]{2,1,0:T(8,128)S(1)}, f32[1,128,2048]{2,1,0:T(8,128)S(1)}) fusion(s32[2048]{0:T(1024)S(1)} %iota_add_fusion), kind=kLoop, calls=%fused_computation.11 | loop fusion | flops 3670016 | bytes 2105344 | tf_op jit(solution)/shard_map/cos | solution.py:404
  30.0 9.3 %lag_table.1.table_ref = bf16[8,2048,256]{2,1,0:T(8,128)(2,1)} custom-call(f32[2,128,2048]{2,1,0:T(8,128)S(1)} %pad_maximum_fusion.fine_ref, f32[2,8,2048]{2,1,0:T(8,128)S(1)} %pad_maximum_fusion.1.coarse_ref), custom_call_target="tpu_custom_call" | custom-call | flops 16000000 | bytes 12000000 | tf_op jit(solution)/shard_map/lag_table/pallas_call | solution.py:408
  39.3 63.4 %all-to-all-done.got_ref = bf16[64,104,128]{2,1,0:T(8,128)(2,1)S(1)} async-done(((bf16[64,104,128]{2,1,0:T(8,128)(2,1)}), bf16[64,104,128]{2,1,0:T(8,128)(2,1)S(1)}, u32[]{:S(2)}, u32[]{:S(2)}) %all-to-all-start) | async-done | bytes 1703968 | tf_op jit(solution)/shard_map/all_to_all | solution.py:476
  103.1 1.6 sort_units.1
  107.3 3.2 %collective-permute-start.8 = (bf16[64,48,128]{2,1,0:T(8,128)(2,1)S(1)}, bf16[64,48,128]{2,1,0:T(8,128)(2,1)S(1)}, u32[]{:S(2)}, u32[]{:S(2)}) collective-permute-start(bf16[64,48,128]{2,1,0:T(8,128)(2,1)S(1)} %get-tuple-element.12.block_ref.refs_0_), channel_id=1, source_target_pairs={{0,64},{64,128},{128,192},{256,320},{320,384},{384,448},{1,65},{65... | collective-permute-start | bytes 2359304 | tf_op jit(solution)/shard_map/ppermute | solution.py:443
  110.5 3.7 %collective-permute-start.1 = (bf16[64,48,128]{2,1,0:T(8,128)(2,1)S(1)}, bf16[64,48,128]{2,1,0:T(8,128)(2,1)S(1)}, u32[]{:S(2)}, u32[]{:S(2)}) collective-permute-start(bf16[64,48,128]{2,1,0:T(8,128)(2,1)S(1)} %get-tuple-element.12.block_ref.refs_0_), channel_id=1, source_target_pairs={{0,2},{1,3},{2,4},{3,5},{4,6},{5,7},{6,8},{7,9},{8,10},{9,11},{10,... | collective-permute-start | bytes 2359304 | tf_op jit(solution)/shard_map/ppermute | solution.py:425
  114.2 4.1 %collective-permute-start = (bf16[64,48,128]{2,1,0:T(8,128)(2,1)S(1)}, bf16[64,48,128]{2,1,0:T(8,128)(2,1)}, u32[]{:S(2)}, u32[]{:S(2)}) collective-permute-start(bf16[64,48,128]{2,1,0:T(8,128)(2,1)S(1)} %get-tuple-element.12.block_ref.refs_0_), channel_id=1, source_target_pairs={{0,1},{1,0},{2,3},{3,2},{4,5},{5,4},{6,7},{7,6},{8,9},{9,8},{10,11... | collective-permute-start | bytes 2359304 | tf_op jit(solution)/shard_map/ppermute | solution.py:429
  119.1 7.9 %collective-permute-start.7 = (bf16[16,48,128]{2,1,0:T(8,128)(2,1)}, bf16[16,48,128]{2,1,0:T(8,128)(2,1)S(1)}, u32[]{:S(2)}, u32[]{:S(2)}) collective-permute-start(bf16[16,48,128]{2,1,0:T(8,128)(2,1)} %choose_piece.1), channel_id=1, source_target_pairs={{0,256},{64,320},{128,384},{192,448},{256,0},{320,64},{384,128},{4... | collective-permute-start | bytes 589832 | tf_op jit(solution)/shard_map/ppermute | solution.py:446
  127.0 1.9 collective-permute-start.3
  129.5 18.8 %collective-permute-start.2 = (bf16[64,48,128]{2,1,0:T(8,128)(2,1)S(1)}, bf16[64,48,128]{2,1,0:T(8,128)(2,1)S(1)}, u32[]{:S(2)}, u32[]{:S(2)}) collective-permute-start(bf16[64,48,128]{2,1,0:T(8,128)(2,1)S(1)} %collective-permute-done.1.refs_1_), channel_id=1, source_target_pairs={{0,1},{1,0},{2,3},{3,2},{4,5},{5,4},{6,7},{7,6},{8,9},{9,8},{10,11... | collective-permute-start | bytes 2359304 | tf_op jit(solution)/shard_map/ppermute | solution.py:429
  148.4 13.1 %collective-permute-done.7.piece_ref.refs_2_ = bf16[16,48,128]{2,1,0:T(8,128)(2,1)S(1)} collective-permute-done((bf16[16,48,128]{2,1,0:T(8,128)(2,1)}, bf16[16,48,128]{2,1,0:T(8,128)(2,1)S(1)}, u32[]{:S(2)}, u32[]{:S(2)}) %collective-permute-start.7) | collective-permute-done | bytes 196640 | tf_op jit(solution)/shard_map/ppermute | solution.py:446
  162.3 1.8 cross.5.refs_3_
  164.0 1.8 cross.6.refs_2_.kept_ref
  165.8 7.0 %collective-permute-start.9 = (bf16[8,9,16,128]{3,2,1,0:T(8,128)(2,1)S(1)}, bf16[8,9,16,128]{3,2,1,0:T(8,128)(2,1)}, u32[]{:S(2)}, u32[]{:S(2)}) collective-permute-start(bf16[8,9,16,128]{3,2,1,0:T(8,128)(2,1)S(1)} %cross.6.refs_2_.kept_ref), channel_id=1, source_target_pairs={{0,2},{1,3},{2,4},{3,5},{4,6},{5,7},{6,8},{7,9},{8,10},{9,11},{10,... | collective-permute-start | bytes 884744 | tf_op jit(solution)/shard_map/ppermute | solution.py:425
  172.8 1.3 collective-permute-start.12
  174.1 1.3 collective-permute-start.11
  176.7 1.8 cross.7.refs_3_.two_ref
  178.5 2.9 %cross.8.refs_6_.one_ref = bf16[4,9,16,128]{3,2,1,0:T(8,128)(2,1)S(1)} custom-call(s32[1]{0:T(128)} %bitcast.flag_ref.core_ref, bf16[64,48,128]{2,1,0:T(8,128)(2,1)S(1)} %get-tuple-element.12.block_ref.refs_0_, bf16[64,48,128]{2,1,0:T(8,128)(2,1)} %collective-permute-done.refs_1_, bf16[64,48,128]{2,1,0:T(8,128)(2,1)S(1)} %collective-permute-done.2.refs_2_, ...), custom_call_target="tpu_custom_call" | custom-call | flops 40000000 | bytes 1500000 | tf_op jit(solution)/shard_map/cross/pallas_call | solution.py:274
  181.4 4.3 %collective-permute-done.12.refs_5_ = bf16[16,48,128]{2,1,0:T(8,128)(2,1)} collective-permute-done((bf16[16,48,128]{2,1,0:T(8,128)(2,1)}, bf16[16,48,128]{2,1,0:T(8,128)(2,1)}, u32[]{:S(2)}, u32[]{:S(2)}) %collective-permute-start.12) | collective-permute-done | bytes 196640 | tf_op jit(solution)/shard_map/ppermute | solution.py:451
  185.8 2.9 %cross.9.across_ref = bf16[4,9,16,128]{3,2,1,0:T(8,128)(2,1)S(1)} custom-call(s32[1]{0:T(128)} %bitcast.7.flag_ref, bf16[64,48,128]{2,1,0:T(8,128)(2,1)S(1)} %get-tuple-element.12.block_ref.refs_0_, bf16[64,48,128]{2,1,0:T(8,128)(2,1)S(1)} %collective-permute-done.8.refs_0_.refs_1_, bf16[16,48,128]{2,1,0:T(8,128)(2,1)S(1)} %copy-done.2, ...), custom_call_target="tpu_custom_call" | custom-call | flops 40000000 | bytes 1500000 | tf_op jit(solution)/shard_map/cross/pallas_call | solution.py:274
  188.7 6.7 %lag_series.1 = (bf16[2,4,9,2,2048]{4,3,2,1,0:T(2,128)(2,1)}, bf16[2,9,2,2048]{3,2,1,0:T(2,128)(2,1)}) custom-call(s32[1]{0:T(128)} %bitcast.flag_ref.core_ref, bf16[8,2048,256]{2,1,0:T(8,128)(2,1)} %lag_table.1.table_ref, bf16[4,9,16,128]{3,2,1,0:T(8,128)(2,1)S(1)} %cross.8.refs_6_.one_ref, bf16[4,9,16,128]{3,2,1,0:T(8,128)(2,1)S(1)} %cross.7.refs_3_.two_ref, ...), custom_call_target="tpu_custom_call" | custom-call | flops 1509949440 | bytes 12000000 | tf_op jit(solution)/shard_map/lag_series/pallas_call | solution.py:352
  (46 shorter events, 10.3 us)
Async XLA Ops:
  8.3 1.3 copy-start
  9.5 93.2 %all-to-all-start = ((bf16[64,104,128]{2,1,0:T(8,128)(2,1)}), bf16[64,104,128]{2,1,0:T(8,128)(2,1)S(1)}, u32[]{:S(2)}, u32[]{:S(2)}) async-start(bf16[64,104,128]{2,1,0:T(8,128)(2,1)} %copy-done), calls=%async_computation | async-start | bytes 3407872 | tf_op jit(solution)/shard_map/all_to_all | solution.py:476
  104.7 9.6 %collective-permute-start.4 = (bf16[16,48,128]{2,1,0:T(8,128)(2,1)}, bf16[16,48,128]{2,1,0:T(8,128)(2,1)S(1)}, u32[]{:S(2)}, u32[]{:S(2)}) collective-permute-start(bf16[16,48,128]{2,1,0:T(8,128)(2,1)} %get-tuple-element.13), channel_id=1, source_target_pairs={{192,0},{448,256},{193,1},{449,257},{194,2},{450,258},{195,3},{451... | collective-permute-start | bytes 589832 | tf_op jit(solution)/shard_map/ppermute | solution.py:436
  106.0 12.4 %collective-permute-start.5 = (bf16[16,48,128]{2,1,0:T(8,128)(2,1)}, bf16[16,48,128]{2,1,0:T(8,128)(2,1)S(1)}, u32[]{:S(2)}, u32[]{:S(2)}) collective-permute-start(bf16[16,48,128]{2,1,0:T(8,128)(2,1)} %get-tuple-element.14), channel_id=1, source_target_pairs={{192,64},{448,320},{193,65},{449,321},{194,66},{450,322},{195,67},... | collective-permute-start | bytes 589832 | tf_op jit(solution)/shard_map/ppermute | solution.py:436
  106.6 11.7 %collective-permute-start.6 = (bf16[16,48,128]{2,1,0:T(8,128)(2,1)}, bf16[16,48,128]{2,1,0:T(8,128)(2,1)S(1)}, u32[]{:S(2)}, u32[]{:S(2)}) collective-permute-start(bf16[16,48,128]{2,1,0:T(8,128)(2,1)} %get-tuple-element.15), channel_id=1, source_target_pairs={{192,128},{448,384},{193,129},{449,385},{194,130},{450,386},{195,1... | collective-permute-start | bytes 589832 | tf_op jit(solution)/shard_map/ppermute | solution.py:436
  107.3 54.2 %collective-permute-start.8 = (bf16[64,48,128]{2,1,0:T(8,128)(2,1)S(1)}, bf16[64,48,128]{2,1,0:T(8,128)(2,1)S(1)}, u32[]{:S(2)}, u32[]{:S(2)}) collective-permute-start(bf16[64,48,128]{2,1,0:T(8,128)(2,1)S(1)} %get-tuple-element.12.block_ref.refs_0_), channel_id=1, source_target_pairs={{0,64},{64,128},{128,192},{256,320},{320,384},{384,448},{1,65},{65... | collective-permute-start | bytes 2359304 | tf_op jit(solution)/shard_map/ppermute | solution.py:443
  110.5 19.0 %collective-permute-start.1 = (bf16[64,48,128]{2,1,0:T(8,128)(2,1)S(1)}, bf16[64,48,128]{2,1,0:T(8,128)(2,1)S(1)}, u32[]{:S(2)}, u32[]{:S(2)}) collective-permute-start(bf16[64,48,128]{2,1,0:T(8,128)(2,1)S(1)} %get-tuple-element.12.block_ref.refs_0_), channel_id=1, source_target_pairs={{0,2},{1,3},{2,4},{3,5},{4,6},{5,7},{6,8},{7,9},{8,10},{9,11},{10,... | collective-permute-start | bytes 2359304 | tf_op jit(solution)/shard_map/ppermute | solution.py:425
  114.2 47.3 %collective-permute-start = (bf16[64,48,128]{2,1,0:T(8,128)(2,1)S(1)}, bf16[64,48,128]{2,1,0:T(8,128)(2,1)}, u32[]{:S(2)}, u32[]{:S(2)}) collective-permute-start(bf16[64,48,128]{2,1,0:T(8,128)(2,1)S(1)} %get-tuple-element.12.block_ref.refs_0_), channel_id=1, source_target_pairs={{0,1},{1,0},{2,3},{3,2},{4,5},{5,4},{6,7},{7,6},{8,9},{9,8},{10,11... | collective-permute-start | bytes 2359304 | tf_op jit(solution)/shard_map/ppermute | solution.py:429
  119.1 42.4 %collective-permute-start.7 = (bf16[16,48,128]{2,1,0:T(8,128)(2,1)}, bf16[16,48,128]{2,1,0:T(8,128)(2,1)S(1)}, u32[]{:S(2)}, u32[]{:S(2)}) collective-permute-start(bf16[16,48,128]{2,1,0:T(8,128)(2,1)} %choose_piece.1), channel_id=1, source_target_pairs={{0,256},{64,320},{128,384},{192,448},{256,0},{320,64},{384,128},{4... | collective-permute-start | bytes 589832 | tf_op jit(solution)/shard_map/ppermute | solution.py:446
  127.0 35.2 %collective-permute-start.3 = (bf16[64,48,128]{2,1,0:T(8,128)(2,1)S(1)}, bf16[64,48,128]{2,1,0:T(8,128)(2,1)S(1)}, u32[]{:S(2)}, u32[]{:S(2)}) collective-permute-start(bf16[64,48,128]{2,1,0:T(8,128)(2,1)S(1)} %get-tuple-element.12.block_ref.refs_0_), channel_id=1, source_target_pairs={{0,62},{1,63},{2,0},{3,1},{4,2},{5,3},{6,4},{7,5},{8,6},{9,7},{10,... | collective-permute-start | bytes 2359304 | tf_op jit(solution)/shard_map/ppermute | solution.py:425
  129.5 34.5 %collective-permute-start.2 = (bf16[64,48,128]{2,1,0:T(8,128)(2,1)S(1)}, bf16[64,48,128]{2,1,0:T(8,128)(2,1)S(1)}, u32[]{:S(2)}, u32[]{:S(2)}) collective-permute-start(bf16[64,48,128]{2,1,0:T(8,128)(2,1)S(1)} %collective-permute-done.1.refs_1_), channel_id=1, source_target_pairs={{0,1},{1,0},{2,3},{3,2},{4,5},{5,4},{6,7},{7,6},{8,9},{9,8},{10,11... | collective-permute-start | bytes 2359304 | tf_op jit(solution)/shard_map/ppermute | solution.py:429
  161.5 0.7 copy-start.1
  165.8 22.8 %collective-permute-start.9 = (bf16[8,9,16,128]{3,2,1,0:T(8,128)(2,1)S(1)}, bf16[8,9,16,128]{3,2,1,0:T(8,128)(2,1)}, u32[]{:S(2)}, u32[]{:S(2)}) collective-permute-start(bf16[8,9,16,128]{3,2,1,0:T(8,128)(2,1)S(1)} %cross.6.refs_2_.kept_ref), channel_id=1, source_target_pairs={{0,2},{1,3},{2,4},{3,5},{4,6},{5,7},{6,8},{7,9},{8,10},{9,11},{10,... | collective-permute-start | bytes 884744 | tf_op jit(solution)/shard_map/ppermute | solution.py:425
  172.8 12.9 %collective-permute-start.12 = (bf16[16,48,128]{2,1,0:T(8,128)(2,1)}, bf16[16,48,128]{2,1,0:T(8,128)(2,1)}, u32[]{:S(2)}, u32[]{:S(2)}) collective-permute-start(bf16[16,48,128]{2,1,0:T(8,128)(2,1)} %relay_piece.1.refs_2_), channel_id=1, source_target_pairs={{192,0},{448,256},{193,1},{449,257},{194,2},{450,258},{195,3},{451... | collective-permute-start | bytes 589832 | tf_op jit(solution)/shard_map/ppermute | solution.py:451
  174.1 11.7 %collective-permute-start.11 = (bf16[16,48,128]{2,1,0:T(8,128)(2,1)}, bf16[16,48,128]{2,1,0:T(8,128)(2,1)}, u32[]{:S(2)}, u32[]{:S(2)}) collective-permute-start(bf16[16,48,128]{2,1,0:T(8,128)(2,1)} %relay_piece.1.refs_2_), channel_id=1, source_target_pairs={{128,0},{384,256},{129,1},{385,257},{130,2},{386,258},{131,3},{387... | collective-permute-start | bytes 589832 | tf_op jit(solution)/shard_map/ppermute | solution.py:451
  175.4 10.4 %collective-permute-start.10 = (bf16[16,48,128]{2,1,0:T(8,128)(2,1)}, bf16[16,48,128]{2,1,0:T(8,128)(2,1)}, u32[]{:S(2)}, u32[]{:S(2)}) collective-permute-start(bf16[16,48,128]{2,1,0:T(8,128)(2,1)} %relay_piece.1.refs_2_), channel_id=1, source_target_pairs={{64,0},{320,256},{65,1},{321,257},{66,2},{322,258},{67,3},{323,259... | collective-permute-start | bytes 589832 | tf_op jit(solution)/shard_map/ppermute | solution.py:451
  178.5 7.3 %copy-start.2 = (bf16[16,48,128]{2,1,0:T(8,128)(2,1)S(1)}, bf16[16,48,128]{2,1,0:T(8,128)(2,1)}, u32[]{:S(2)}) copy-start(bf16[16,48,128]{2,1,0:T(8,128)(2,1)} %copy-done.1) | copy-start | bytes 589828

commit v10 on v9

--- a/solution.py
+++ b/solution.py
@@ -445,7 +445,7 @@
     )
     piece = lax.ppermute(piece, "region", [(i, (i + planes) % regions) for i in range(regions)])
     far = [piece]
-    piece = relay(piece, near, *after)
+    piece = relay(piece)
     for plane in range(1, planes):
         far.append(
             lax.ppermute(piece, "region", [(n + plane, n) for n in range(0, regions, planes)])

time: 197 us -> 193 us (0.980)
  the two profiles are of different devices: /device:TPU:57 before, /device:TPU:1 now
where the time goes in v10:
time: 193 us; the launch traced here: 192 us
  waiting for transfers between devices  91.3 us (47%)
  starting transfers between devices  56.7 us (29%)
  Pallas kernels  31.1 us (16%)
  other arithmetic  5.74 us (3%)
  local copies, waits for them, and re-layouts  5.57 us (3%)
    all_to_all x1, waiting for transfers between devices, body(): lax.all_to_all(part, 'blk', split_axis=0, concat_axis=0, tiled=True)  64.9 us
    all_to_all x1, starting transfers between devices, body(): lax.all_to_all(part, 'blk', split_axis=0, concat_axis=0, tiled=True)  17.2 us
    ppermute x3, starting transfers between devices, shifted(): lax.ppermute(block, axis, [(i, (i + by) % size) for i in range(size)])  13.3 us
    ppermute x3, waiting for transfers between devices, shifted(): lax.ppermute(block, axis, [(i, (i + by) % size) for i in range(size)])  12.8 us
    ppermute x3, waiting for transfers between devices, from_previous_region(): lax.ppermute(piece, 'region', [(n + plane, n) for n in range(0, regions,...  11 us
    pallas_call x5, Pallas kernels, cross(): pl.pallas_call(functools.partial(cross_kernel, chunk, plan, tuple((len(bl...  9.98 us
    pallas_call x1, Pallas kernels, make_table(): pl.pallas_call(table_kernel, grid=(2, LAGS // COLUMNS), in_specs=[pl.Bloc...  9.35 us
    ppermute x1, starting transfers between devices, from_previous_region(): lax.ppermute(piece, 'region', [(i, (i + planes) % regions) for i in range...  7.93 us
  transfers between devices with their start and end apart: 14, of which 5 were waited for; matrix products, arithmetic and copies ran while one was open for 2% of the time, Pallas kernels for 11%

profile of v10, /device:TPU:1, one launch (start us, length us, event | category | flops | bytes accessed | tf_op | source)
XLA Modules:
  0.0 192.2 jit_solution(9635700497005413641)
XLA Ops:
  2.4 1.9 copy.11
  5.5 2.8 %whiten.1 = bf16[64,104,128]{2,1,0:T(8,128)(2,1)S(1)} custom-call(s32[128]{0:T(128)S(1)} %min.27.source_ref, bf16[256,128]{1,0:T(8,128)(2,1)S(1)} %add_convert_fusion.band_ref, f32[8,128]{1,0:T(8,128)S(1)} %convert_divide_fusion.inverse_ref, bf16[128,48,128]{2,1,0:T(8,128)(2,1)S(1)} %copy.12.archive_ref, bf16[64,8,128]{2,1,0:T(8,128)(2,1)S(1)} %broadcast_in_dim.91.mark_ref), custom_call_target="tpu_custom_call" | custom-call | flops 200000000 | bytes 4000000 | tf_op jit(solution)/shard_map/whiten/pallas_call | solution.py:123
  9.5 17.2 %all-to-all-start = ((bf16[64,104,128]{2,1,0:T(8,128)(2,1)}), bf16[64,104,128]{2,1,0:T(8,128)(2,1)S(1)}, u32[]{:S(2)}, u32[]{:S(2)}) async-start(bf16[64,104,128]{2,1,0:T(8,128)(2,1)} %copy-done), calls=%async_computation | async-start | bytes 3407872 | tf_op jit(solution)/shard_map/all_to_all | solution.py:476
  27.1 4.1 %fusion.7 = (f32[1,128,2048]{2,1,0:T(8,128)S(1)}, f32[1,128,2048]{2,1,0:T(8,128)S(1)}) fusion(s32[2048]{0:T(1024)S(1)} %iota_add_fusion), kind=kLoop, calls=%fused_computation.11 | loop fusion | flops 3670016 | bytes 2105344 | tf_op jit(solution)/shard_map/cos | solution.py:404
  31.4 9.3 %lag_table.1.table_ref = bf16[8,2048,256]{2,1,0:T(8,128)(2,1)} custom-call(f32[2,128,2048]{2,1,0:T(8,128)S(1)} %pad_maximum_fusion.fine_ref, f32[2,8,2048]{2,1,0:T(8,128)S(1)} %pad_maximum_fusion.1.coarse_ref), custom_call_target="tpu_custom_call" | custom-call | flops 16000000 | bytes 12000000 | tf_op jit(solution)/shard_map/lag_table/pallas_call | solution.py:408
  40.8 64.9 %all-to-all-done.got_ref = bf16[64,104,128]{2,1,0:T(8,128)(2,1)S(1)} async-done(((bf16[64,104,128]{2,1,0:T(8,128)(2,1)}), bf16[64,104,128]{2,1,0:T(8,128)(2,1)S(1)}, u32[]{:S(2)}, u32[]{:S(2)}) %all-to-all-start) | async-done | bytes 1703968 | tf_op jit(solution)/shard_map/all_to_all | solution.py:476
  106.8 1.3 collective-permute-start.4
  109.5 3.1 %collective-permute-start.1 = (bf16[64,48,128]{2,1,0:T(8,128)(2,1)S(1)}, bf16[64,48,128]{2,1,0:T(8,128)(2,1)S(1)}, u32[]{:S(2)}, u32[]{:S(2)}) collective-permute-start(bf16[64,48,128]{2,1,0:T(8,128)(2,1)S(1)} %get-tuple-element.12.block_ref.refs_0_), channel_id=1, source_target_pairs={{0,2},{1,3},{2,4},{3,5},{4,6},{5,7},{6,8},{7,9},{8,10},{9,11},{10,... | collective-permute-start | bytes 2359304 | tf_op jit(solution)/shard_map/ppermute | solution.py:425
  112.6 2.7 %collective-permute-done.4.refs_0_ = bf16[16,48,128]{2,1,0:T(8,128)(2,1)S(1)} collective-permute-done((bf16[16,48,128]{2,1,0:T(8,128)(2,1)S(1)}, bf16[16,48,128]{2,1,0:T(8,128)(2,1)S(1)}, u32[]{:S(2)}, u32[]{:S(2)}) %collective-permute-start.4) | collective-permute-done | bytes 196640 | tf_op jit(solution)/shard_map/ppermute | solution.py:436
  116.0 7.9 %collective-permute-start.7 = (bf16[16,48,128]{2,1,0:T(8,128)(2,1)}, bf16[16,48,128]{2,1,0:T(8,128)(2,1)S(1)}, u32[]{:S(2)}, u32[]{:S(2)}) collective-permute-start(bf16[16,48,128]{2,1,0:T(8,128)(2,1)} %choose_piece.1), channel_id=1, source_target_pairs={{0,256},{64,320},{128,384},{192,448},{256,0},{320,64},{384,128},{4... | collective-permute-start | bytes 589832 | tf_op jit(solution)/shard_map/ppermute | solution.py:446
  123.9 8.2 %collective-permute-start.3 = (bf16[64,48,128]{2,1,0:T(8,128)(2,1)S(1)}, bf16[64,48,128]{2,1,0:T(8,128)(2,1)S(1)}, u32[]{:S(2)}, u32[]{:S(2)}) collective-permute-start(bf16[64,48,128]{2,1,0:T(8,128)(2,1)S(1)} %get-tuple-element.12.block_ref.refs_0_), channel_id=1, source_target_pairs={{0,62},{1,63},{2,0},{3,1},{4,2},{5,3},{6,4},{7,5},{8,6},{9,7},{10,... | collective-permute-start | bytes 2359304 | tf_op jit(solution)/shard_map/ppermute | solution.py:425
  132.2 3.8 %collective-permute-start = (bf16[64,48,128]{2,1,0:T(8,128)(2,1)S(1)}, bf16[64,48,128]{2,1,0:T(8,128)(2,1)S(1)}, u32[]{:S(2)}, u32[]{:S(2)}) collective-permute-start(bf16[64,48,128]{2,1,0:T(8,128)(2,1)S(1)} %get-tuple-element.12.block_ref.refs_0_), channel_id=1, source_target_pairs={{0,1},{1,0},{2,3},{3,2},{4,5},{5,4},{6,7},{7,6},{8,9},{9,8},{10,11... | collective-permute-start | bytes 2359304 | tf_op jit(solution)/shard_map/ppermute | solution.py:429
  135.9 5.1 %collective-permute-start.9 = (bf16[64,48,128]{2,1,0:T(8,128)(2,1)S(1)}, bf16[64,48,128]{2,1,0:T(8,128)(2,1)S(1)}, u32[]{:S(2)}, u32[]{:S(2)}) collective-permute-start(bf16[64,48,128]{2,1,0:T(8,128)(2,1)S(1)} %get-tuple-element.12.block_ref.refs_0_), channel_id=1, source_target_pairs={{0,64},{64,128},{128,192},{256,320},{320,384},{384,448},{1,65},{65... | collective-permute-start | bytes 2359304 | tf_op jit(solution)/shard_map/ppermute | solution.py:443
  141.0 3.0 %collective-permute-start.2 = (bf16[64,48,128]{2,1,0:T(8,128)(2,1)S(1)}, bf16[64,48,128]{2,1,0:T(8,128)(2,1)S(1)}, u32[]{:S(2)}, u32[]{:S(2)}) collective-permute-start(bf16[64,48,128]{2,1,0:T(8,128)(2,1)S(1)} %collective-permute-done.1.refs_1_), channel_id=1, source_target_pairs={{0,1},{1,0},{2,3},{3,2},{4,5},{5,4},{6,7},{7,6},{8,9},{9,8},{10,11... | collective-permute-start | bytes 2359304 | tf_op jit(solution)/shard_map/ppermute | solution.py:429
  144.8 12.7 %collective-permute-done.3.refs_0_.refs_1_ = bf16[64,48,128]{2,1,0:T(8,128)(2,1)S(1)} collective-permute-done((bf16[64,48,128]{2,1,0:T(8,128)(2,1)S(1)}, bf16[64,48,128]{2,1,0:T(8,128)(2,1)S(1)}, u32[]{:S(2)}, u32[]{:S(2)}) %collective-permute-start.3) | collective-permute-done | bytes 786464 | tf_op jit(solution)/shard_map/ppermute | solution.py:425
  157.5 1.8 cross.5.refs_3_
  159.3 1.8 cross.6.refs_2_.kept_ref
  161.1 1.9 %collective-permute-start.8 = (bf16[8,9,16,128]{3,2,1,0:T(8,128)(2,1)S(1)}, bf16[8,9,16,128]{3,2,1,0:T(8,128)(2,1)}, u32[]{:S(2)}, u32[]{:S(2)}) collective-permute-start(bf16[8,9,16,128]{3,2,1,0:T(8,128)(2,1)S(1)} %cross.6.refs_2_.kept_ref), channel_id=1, source_target_pairs={{0,2},{1,3},{2,4},{3,5},{4,6},{5,7},{6,8},{7,9},{8,10},{9,11},{10,... | collective-permute-start | bytes 884744 | tf_op jit(solution)/shard_map/ppermute | solution.py:425
  167.9 1.8 cross.7.refs_3_.two_ref
  169.7 1.8 cross.8.refs_6_.one_ref
  171.5 6.2 %collective-permute-done.11.refs_4_ = bf16[16,48,128]{2,1,0:T(8,128)(2,1)} collective-permute-done((bf16[16,48,128]{2,1,0:T(8,128)(2,1)}, bf16[16,48,128]{2,1,0:T(8,128)(2,1)}, u32[]{:S(2)}, u32[]{:S(2)}) %collective-permute-start.11) | collective-permute-done | bytes 196640 | tf_op jit(solution)/shard_map/ppermute | solution.py:451
  177.7 4.8 %collective-permute-done.12.refs_5_ = bf16[16,48,128]{2,1,0:T(8,128)(2,1)} collective-permute-done((bf16[16,48,128]{2,1,0:T(8,128)(2,1)}, bf16[16,48,128]{2,1,0:T(8,128)(2,1)}, u32[]{:S(2)}, u32[]{:S(2)}) %collective-permute-start.12) | collective-permute-done | bytes 196640 | tf_op jit(solution)/shard_map/ppermute | solution.py:451
  182.5 2.9 %cross.9.across_ref = bf16[4,9,16,128]{3,2,1,0:T(8,128)(2,1)S(1)} custom-call(s32[1]{0:T(128)} %bitcast.7.flag_ref, bf16[64,48,128]{2,1,0:T(8,128)(2,1)S(1)} %get-tuple-element.12.block_ref.refs_0_, bf16[64,48,128]{2,1,0:T(8,128)(2,1)S(1)} %collective-permute-done.9.refs_1_, bf16[16,48,128]{2,1,0:T(8,128)(2,1)S(1)} %copy-done.4, ...), custom_call_target="tpu_custom_call" | custom-call | flops 40000000 | bytes 1500000 | tf_op jit(solution)/shard_map/cross/pallas_call | solution.py:274
  185.4 6.7 %lag_series.1 = (bf16[2,4,9,2,2048]{4,3,2,1,0:T(2,128)(2,1)}, bf16[2,9,2,2048]{3,2,1,0:T(2,128)(2,1)}) custom-call(s32[1]{0:T(128)} %bitcast.flag_ref.core_ref, bf16[8,2048,256]{2,1,0:T(8,128)(2,1)} %lag_table.1.table_ref, bf16[4,9,16,128]{3,2,1,0:T(8,128)(2,1)S(1)} %cross.8.refs_6_.one_ref, bf16[4,9,16,128]{3,2,1,0:T(8,128)(2,1)S(1)} %cross.7.refs_3_.two_ref, ...), custom_call_target="tpu_custom_call" | custom-call | flops 1509949440 | bytes 12000000 | tf_op jit(solution)/shard_map/lag_series/pallas_call | solution.py:352
  (50 shorter events, 12.8 us)
Async XLA Ops:
  8.3 1.2 copy-start
  9.5 96.1 %all-to-all-start = ((bf16[64,104,128]{2,1,0:T(8,128)(2,1)}), bf16[64,104,128]{2,1,0:T(8,128)(2,1)S(1)}, u32[]{:S(2)}, u32[]{:S(2)}) async-start(bf16[64,104,128]{2,1,0:T(8,128)(2,1)} %copy-done), calls=%async_computation | async-start | bytes 3407872 | tf_op jit(solution)/shard_map/all_to_all | solution.py:476
  106.8 8.5 %collective-permute-start.4 = (bf16[16,48,128]{2,1,0:T(8,128)(2,1)S(1)}, bf16[16,48,128]{2,1,0:T(8,128)(2,1)S(1)}, u32[]{:S(2)}, u32[]{:S(2)}) collective-permute-start(bf16[16,48,128]{2,1,0:T(8,128)(2,1)S(1)} %get-tuple-element.13), channel_id=1, source_target_pairs={{192,0},{448,256},{193,1},{449,257},{194,2},{450,258},{195,3},{451... | collective-permute-start | bytes 589832 | tf_op jit(solution)/shard_map/ppermute | solution.py:436
  108.1 7.2 %collective-permute-start.5 = (bf16[16,48,128]{2,1,0:T(8,128)(2,1)S(1)}, bf16[16,48,128]{2,1,0:T(8,128)(2,1)S(1)}, u32[]{:S(2)}, u32[]{:S(2)}) collective-permute-start(bf16[16,48,128]{2,1,0:T(8,128)(2,1)S(1)} %get-tuple-element.14), channel_id=1, source_target_pairs={{192,64},{448,320},{193,65},{449,321},{194,66},{450,322},{195,67},... | collective-permute-start | bytes 589832 | tf_op jit(solution)/shard_map/ppermute | solution.py:436
  108.8 6.5 %collective-permute-start.6 = (bf16[16,48,128]{2,1,0:T(8,128)(2,1)S(1)}, bf16[16,48,128]{2,1,0:T(8,128)(2,1)S(1)}, u32[]{:S(2)}, u32[]{:S(2)}) collective-permute-start(bf16[16,48,128]{2,1,0:T(8,128)(2,1)S(1)} %get-tuple-element.15), channel_id=1, source_target_pairs={{192,128},{448,384},{193,129},{449,385},{194,130},{450,386},{195,1... | collective-permute-start | bytes 589832 | tf_op jit(solution)/shard_map/ppermute | solution.py:436
  109.5 31.5 %collective-permute-start.1 = (bf16[64,48,128]{2,1,0:T(8,128)(2,1)S(1)}, bf16[64,48,128]{2,1,0:T(8,128)(2,1)S(1)}, u32[]{:S(2)}, u32[]{:S(2)}) collective-permute-start(bf16[64,48,128]{2,1,0:T(8,128)(2,1)S(1)} %get-tuple-element.12.block_ref.refs_0_), channel_id=1, source_target_pairs={{0,2},{1,3},{2,4},{3,5},{4,6},{5,7},{6,8},{7,9},{8,10},{9,11},{10,... | collective-permute-start | bytes 2359304 | tf_op jit(solution)/shard_map/ppermute | solution.py:425
  116.0 28.1 %collective-permute-start.7 = (bf16[16,48,128]{2,1,0:T(8,128)(2,1)}, bf16[16,48,128]{2,1,0:T(8,128)(2,1)S(1)}, u32[]{:S(2)}, u32[]{:S(2)}) collective-permute-start(bf16[16,48,128]{2,1,0:T(8,128)(2,1)} %choose_piece.1), channel_id=1, source_target_pairs={{0,256},{64,320},{128,384},{192,448},{256,0},{320,64},{384,128},{4... | collective-permute-start | bytes 589832 | tf_op jit(solution)/shard_map/ppermute | solution.py:446
  123.9 33.6 %collective-permute-start.3 = (bf16[64,48,128]{2,1,0:T(8,128)(2,1)S(1)}, bf16[64,48,128]{2,1,0:T(8,128)(2,1)S(1)}, u32[]{:S(2)}, u32[]{:S(2)}) collective-permute-start(bf16[64,48,128]{2,1,0:T(8,128)(2,1)S(1)} %get-tuple-element.12.block_ref.refs_0_), channel_id=1, source_target_pairs={{0,62},{1,63},{2,0},{3,1},{4,2},{5,3},{6,4},{7,5},{8,6},{9,7},{10,... | collective-permute-start | bytes 2359304 | tf_op jit(solution)/shard_map/ppermute | solution.py:425
  132.2 33.5 %collective-permute-start = (bf16[64,48,128]{2,1,0:T(8,128)(2,1)S(1)}, bf16[64,48,128]{2,1,0:T(8,128)(2,1)S(1)}, u32[]{:S(2)}, u32[]{:S(2)}) collective-permute-start(bf16[64,48,128]{2,1,0:T(8,128)(2,1)S(1)} %get-tuple-element.12.block_ref.refs_0_), channel_id=1, source_target_pairs={{0,1},{1,0},{2,3},{3,2},{4,5},{5,4},{6,7},{7,6},{8,9},{9,8},{10,11... | collective-permute-start | bytes 2359304 | tf_op jit(solution)/shard_map/ppermute | solution.py:429
  135.9 46.6 %collective-permute-start.9 = (bf16[64,48,128]{2,1,0:T(8,128)(2,1)S(1)}, bf16[64,48,128]{2,1,0:T(8,128)(2,1)S(1)}, u32[]{:S(2)}, u32[]{:S(2)}) collective-permute-start(bf16[64,48,128]{2,1,0:T(8,128)(2,1)S(1)} %get-tuple-element.12.block_ref.refs_0_), channel_id=1, source_target_pairs={{0,64},{64,128},{128,192},{256,320},{320,384},{384,448},{1,65},{65... | collective-permute-start | bytes 2359304 | tf_op jit(solution)/shard_map/ppermute | solution.py:443
  141.0 18.3 %collective-permute-start.2 = (bf16[64,48,128]{2,1,0:T(8,128)(2,1)S(1)}, bf16[64,48,128]{2,1,0:T(8,128)(2,1)S(1)}, u32[]{:S(2)}, u32[]{:S(2)}) collective-permute-start(bf16[64,48,128]{2,1,0:T(8,128)(2,1)S(1)} %collective-permute-done.1.refs_1_), channel_id=1, source_target_pairs={{0,1},{1,0},{2,3},{3,2},{4,5},{5,4},{6,7},{7,6},{8,9},{9,8},{10,11... | collective-permute-start | bytes 2359304 | tf_op jit(solution)/shard_map/ppermute | solution.py:429
  144.0 0.7 copy-start.3
  161.1 24.3 %collective-permute-start.8 = (bf16[8,9,16,128]{3,2,1,0:T(8,128)(2,1)S(1)}, bf16[8,9,16,128]{3,2,1,0:T(8,128)(2,1)}, u32[]{:S(2)}, u32[]{:S(2)}) collective-permute-start(bf16[8,9,16,128]{3,2,1,0:T(8,128)(2,1)S(1)} %cross.6.refs_2_.kept_ref), channel_id=1, source_target_pairs={{0,2},{1,3},{2,4},{3,5},{4,6},{5,7},{6,8},{7,9},{8,10},{9,11},{10,... | collective-permute-start | bytes 884744 | tf_op jit(solution)/shard_map/ppermute | solution.py:425
  163.0 8.5 %collective-permute-start.10 = (bf16[16,48,128]{2,1,0:T(8,128)(2,1)}, bf16[16,48,128]{2,1,0:T(8,128)(2,1)}, u32[]{:S(2)}, u32[]{:S(2)}) collective-permute-start(bf16[16,48,128]{2,1,0:T(8,128)(2,1)} %relay_piece.1.refs_2_), channel_id=1, source_target_pairs={{64,0},{320,256},{65,1},{321,257},{66,2},{322,258},{67,3},{323,259... | collective-permute-start | bytes 589832 | tf_op jit(solution)/shard_map/ppermute | solution.py:451
  164.3 13.4 %collective-permute-start.11 = (bf16[16,48,128]{2,1,0:T(8,128)(2,1)}, bf16[16,48,128]{2,1,0:T(8,128)(2,1)}, u32[]{:S(2)}, u32[]{:S(2)}) collective-permute-start(bf16[16,48,128]{2,1,0:T(8,128)(2,1)} %relay_piece.1.refs_2_), channel_id=1, source_target_pairs={{128,0},{384,256},{129,1},{385,257},{130,2},{386,258},{131,3},{387... | collective-permute-start | bytes 589832 | tf_op jit(solution)/shard_map/ppermute | solution.py:451
  165.6 1.0 copy-start.1
  166.6 15.9 %collective-permute-start.12 = (bf16[16,48,128]{2,1,0:T(8,128)(2,1)}, bf16[16,48,128]{2,1,0:T(8,128)(2,1)}, u32[]{:S(2)}, u32[]{:S(2)}) collective-permute-start(bf16[16,48,128]{2,1,0:T(8,128)(2,1)} %relay_piece.1.refs_2_), channel_id=1, source_target_pairs={{192,0},{448,256},{193,1},{449,257},{194,2},{450,258},{195,3},{451... | collective-permute-start | bytes 589832 | tf_op jit(solution)/shard_map/ppermute | solution.py:451
  167.9 1.8 copy-start.2
  169.7 12.8 %copy-start.4 = (bf16[16,48,128]{2,1,0:T(8,128)(2,1)S(1)}, bf16[16,48,128]{2,1,0:T(8,128)(2,1)}, u32[]{:S(2)}) copy-start(bf16[16,48,128]{2,1,0:T(8,128)(2,1)} %copy-done.3) | copy-start | bytes 589828
